TPU v7x, 128 devices: a whole 4x4x4 slice. The times are simulated.
128 devices in a mesh: pair: 4 (over z), virt: 32 (over y, x, core).
Axes of the slice: x: 4, y: 4, z: 4, core: 2. Of those that a mesh axis runs over, the one named last changes fastest.
Arguments:
- amps: bfloat16 [2048, 24576], P('pair', 'virt'), may hold values from -6 to 6
- ints: bfloat16 [24576, 24576], P('pair', 'virt'), may hold values from -0.0390625 to 0.0390625
- amp_mask: int32 [16, 192], P('pair', 'virt'), may hold values 0 or 1
- int_mask: int32 [192, 192], P('pair', 'virt'), may hold values 0 or 1
- vir_energy: float32 [24576], P('virt'), may hold values from 0.5 to 3
- pair_energy: float32 [2048], P('pair'), may hold values from -2 to -0.5
Outputs:
- updated: float32 [2048, 24576], P('pair', 'virt')
All inputs are finite; a program needn't handle non-finite values. No bound on the sum of `amp_mask` or of `int_mask` on one device may be relied on, other than what follows from the above.
Results may differ from a plain program's by a relative error of at most 0.0003.
Values may be sent and summed in bfloat16 or wider, within the bound.
No kernel may reach another device: no remote copies, remote signals or barrier semaphores. Data moves between devices by JAX's collectives and lax.ppermute only.
A program may use at most 192 MiB of HBM per device.

v0:
```python
import jax
import jax.numpy as jnp
from jax import lax
from jax.sharding import PartitionSpec as P

TILE = 128


def widen(mask):
    return jnp.repeat(jnp.repeat(mask.astype(jnp.bfloat16), TILE, 0), TILE, 1)


def on_device(amps, ints, amp_mask, int_mask, vir_energy, pair_energy):
    screened = amps * widen(amp_mask)
    kept = ints * widen(int_mask)
    all_cols = lax.all_gather(screened, "virt", axis=1, tiled=True)
    contracted = jnp.dot(
        all_cols,
        lax.all_gather(kept, "pair", axis=0, tiled=True),
        preferred_element_type=jnp.float32,
    )
    denom = vir_energy[None, :] - pair_energy[:, None]
    return amps.astype(jnp.float32) + contracted / denom


def solution(mesh):
    return jax.shard_map(
        on_device,
        mesh=mesh,
        in_specs=(
            P("pair", "virt"),
            P("pair", "virt"),
            P("pair", "virt"),
            P("pair", "virt"),
            P("virt"),
            P("pair"),
        ),
        out_specs=P("pair", "virt"),
        check_vma=False,
    )
```

profile of v0, /device:TPU:1, one launch (start us, length us, event | category | flops | bytes accessed | tf_op | source)
XLA Modules:
  0.0 470.4 jit_solution(2130688028065973871)
XLA Ops:
  6.5 0.0 all-gather.3.cloned.1.call-start
  6.5 1.4 copy.9
  7.9 0.7 convert_element_type.10
  8.6 0.1 copy.8
  8.7 0.1 broadcast_bitcast_fusion.1
  8.8 0.9 bitcast_multiply_fusion.1
  9.8 0.0 all-gather.3.cloned.1.call-update
  9.8 0.0 copy-start.1
  9.8 0.0 all-gather.5.cloned.1.call-start
  9.9 12.7 %copy.10 = bf16[6144,768]{0,1:T(8,128)(2,1)} copy(bf16[6144,768]{1,0:T(8,128)(2,1)} %param.7) | data formatting | bytes 18874368 | tf_op args[1]
  22.5 0.0 copy-done.1
  22.6 0.1 broadcast_bitcast_fusion
  22.7 8.5 %bitcast_multiply_fusion = bf16[6144,768]{0,1:T(8,128)(2,1)} fusion(bf16[6144,768]{0,1:T(8,128)(2,1)} %copy.10, bf16[6144,6]{0,1:T(8,128)(2,1)S(1)} %bitcast.20), kind=kLoop, calls=%fused_computation | loop fusion | flops 4718592 | bytes 18948096 | tf_op jit(solution)/shard_map/mul | solution.py:15
  31.2 0.0 copy-start
  31.2 0.0 copy-start.2
  31.2 0.0 copy-start.3
  31.2 0.0 all-gather.5.cloned.1.call-update
  31.2 74.4 %all-gather.3.cloned.1.call-done = bf16[512,24576]{0,1:T(8,128)(2,1)} async-done(((bf16[512,768]{0,1:T(8,128)(2,1)}), bf16[512,24576]{0,1:T(8,128)(2,1)}) %all-gather.3.cloned.1.call-update) | async-done | bytes 25165840 | tf_op jit(solution)/shard_map/all_gather | solution.py:16
  105.6 330.2 %all-gather.5.cloned.1.call-done = bf16[24576,768]{0,1:T(8,128)(2,1)} async-done(((bf16[6144,768]{0,1:T(8,128)(2,1)}), bf16[24576,768]{0,1:T(8,128)(2,1)}) %all-gather.5.cloned.1.call-update) | async-done | bytes 37748752 | tf_op jit(solution)/shard_map/all_gather | solution.py:19
  435.7 0.0 copy-done
  435.7 0.0 copy-done.2
  435.8 0.0 copy-done.3
  435.8 27.8 %divide_add_fusion = f32[512,768]{1,0:T(8,128)} fusion(bf16[512,768]{1,0:T(8,128)(2,1)S(1)} %copy-done, bf16[512,24576]{0,1:T(8,128)(2,1)} %all-gather.3.cloned.1.call-done, bf16[24576,768]{0,1:T(8,128)(2,1)} %all-gather.5.cloned.1.call-done, f32[512]{0:T(512)S(1)} %copy-done.3, f32[768]{0:T(1024)S(1)} %copy-done.2), kind=kOutput, calls=%fused_computation.1 | convolution fusion | flops 19328925696 | bytes 65278976 | tf_op jit(solution)/shard_map/dot_general | solution.py:17
  (3 shorter events, 0.0 us)
Async XLA Ops:
  6.5 99.0 %all-gather.3.cloned.1.call-start = ((), (), s32[]{:S(2)}) async-start(), calls=%async_computation | async-start | bytes 25952256 | tf_op jit(solution)/shard_map/all_gather | solution.py:16
  9.8 12.8 %copy-start.1 = (s32[48,6]{0,1:T(8,128)S(1)}, s32[48,6]{0,1:T(8,128)}, u32[]{:S(2)}) copy-start(s32[48,6]{0,1:T(8,128)} %param.9) | copy-start | bytes 3460
  9.8 425.9 %all-gather.5.cloned.1.call-start = ((), (), s32[]{:S(2)}) async-start(), calls=%async_computation.1 | async-start | bytes 47185920 | tf_op jit(solution)/shard_map/all_gather | solution.py:19
  31.2 404.6 %copy-start = (bf16[512,768]{1,0:T(8,128)(2,1)S(1)}, bf16[512,768]{1,0:T(8,128)(2,1)}, u32[]{:S(2)}) copy-start(bf16[512,768]{1,0:T(8,128)(2,1)} %param.6) | copy-start | bytes 2359300
  31.2 404.6 %copy-start.2 = (f32[768]{0:T(1024)S(1)}, f32[768]{0:T(1024)}, u32[]{:S(2)}) copy-start(f32[768]{0:T(1024)} %param.10) | copy-start | bytes 9220
  31.2 404.6 %copy-start.3 = (f32[512]{0:T(512)S(1)}, f32[512]{0:T(512)}, u32[]{:S(2)}) copy-start(f32[512]{0:T(512)} %param.11) | copy-start | bytes 6148
Sparse Core Ops, SparseCore 0:
  9.9 95.6 all-gather.2
  107.2 328.4 all-gather.4
where the time goes:
time: 471 us; the launch traced here: 470 us
  waiting for transfers between devices  405 us (86%)
  matrix products  27.8 us (6%)
  local copies, waits for them, and re-layouts  14.4 us (3%)
  between operations  13.4 us (3%)
  other arithmetic  10.1 us (2%)
    all_gather x1, waiting for transfers between devices, on_device(): lax.all_gather(kept, 'pair', axis=0, tiled=True)  330 us
    all_gather x1, waiting for transfers between devices, on_device(): all_cols = lax.all_gather(screened, 'virt', axis=1, tiled=True)  74.4 us
    dot_general x1, matrix products, on_device(): jnp.dot(all_cols, lax.all_gather(kept, 'pair', axis=0, tiled=True), prefe...  27.8 us
    unnamed x14, local copies, waits for them, and re-layouts  14.3 us
  transfers between devices with their start and end apart: 2, of which 2 were waited for; matrix products, arithmetic and copies ran while one was open for 5% of the time, Pallas kernels for 0%

commit v1 on v0

v1 whole, which is shorter than its diff:
```python
import functools

import jax
import jax.numpy as jnp
import numpy as np
from jax import lax
from jax.experimental import pallas as pl
from jax.experimental.pallas import tpu as pltpu
from jax.sharding import PartitionSpec as P

TILE = 128
AXES = ("pair", "virt")
N = 4
SENT = jnp.float16
FLIP = {0: 0, 1: -1, -1: 1, 2: 2}


def lin(z, y, x, c):
    return ((z % N) * N + y % N) * 2 * N + (x % N) * 2 + c


def permute(arr, to):
    pairs = [
        (lin(z, y, x, c), lin(*to(z, y, x, c)))
        for z in range(N)
        for y in range(N)
        for x in range(N)
        for c in range(2)
    ]
    return lax.ppermute(arr, AXES, pairs)


def side(c):
    return -1 if c == 0 else 1


def swap(arr):
    return permute(arr, lambda z, y, x, c: (z, y, x, 1 - c))


def shift(arr, axis):
    if axis == "x":
        return permute(arr, lambda z, y, x, c: (z, y, x - side(c), c))
    return permute(arr, lambda z, y, x, c: (z, y - side(c), x, c))


def swapped(item):
    arr, labels = item
    return swap(arr), [(FLIP[f], FLIP[s], 1 - k) for f, s, k in labels]


def along(item, axis, place):
    arr, labels = item
    moved = []
    for lab in labels:
        lab = list(lab)
        lab[place] = {0: 1, 1: 2}[lab[place]]
        moved.append(tuple(lab))
    return shift(arr, axis), moved


def take(item, lo, hi):
    return item[0][lo:hi], item[1][lo:hi]


def gather(own, first, second, early, late):
    own = (own, [(0, 0, 0)])
    other = swapped(own)
    both = (jnp.concatenate([own[0], other[0]], 0), own[1] + other[1])
    near = along(both, first, 0)
    far_side = swapped(near)
    far = along(take(near, 0, 1), first, 0)
    far_other = swapped(far)
    blocks = {}
    for arr, labels in (own, other, near, far_side, far, far_other):
        for i, lab in enumerate(labels):
            blocks[lab] = arr[i : i + 1]
    items = []
    for offs in (early, late):
        labels = [(f, 0, k) for k in (0, 1) for f in offs]
        group = (jnp.concatenate([blocks[lab] for lab in labels], 0), labels)
        near2 = along(group, second, 1)
        far2 = along(take(near2, 0, len(offs)), second, 1)
        items += [group, near2, swapped(near2), far2, swapped(far2)]
    return items


def screen_amps(mask_ref, amps_ref, a_ref, b_ref):
    rows = a_ref.shape[1]
    for i in range(amps_ref.shape[0] // TILE):
        out, r = (a_ref, i * TILE) if i * TILE < rows else (b_ref, i * TILE - rows)
        for j in range(amps_ref.shape[1] // TILE):
            tile = amps_ref[i * TILE : (i + 1) * TILE, j * TILE : (j + 1) * TILE]
            out[0, r : r + TILE, j * TILE : (j + 1) * TILE] = jnp.where(mask_ref[i, j] != 0, tile, jnp.zeros_like(tile))


def screen_ints(mask_ref, ints_ref, out_ref):
    step = pl.program_id(0)
    n = ints_ref.shape[1] // TILE
    for i in range(n):
        for j in range(ints_ref.shape[2] // TILE):
            tile = ints_ref[0, i * TILE : (i + 1) * TILE, j * TILE : (j + 1) * TILE]
            out_ref[0, i * TILE : (i + 1) * TILE, j * TILE : (j + 1) * TILE] = jnp.where(
                mask_ref[step * n + i, j] != 0, tile, jnp.zeros_like(tile)
            )


def product_kernel(bounds, table_ref, where_ref, *refs):
    *a_refs, kept_ref, out_ref, acc_ref = refs
    s = pl.program_id(0)
    for (lo, hi), a_ref in zip(bounds, a_refs):

        @pl.when((s >= lo) & (s < hi))
        def _():
            part = jnp.dot(a_ref[0], kept_ref[0], preferred_element_type=jnp.float32)
            if lo == 0:

                @pl.when(s == 0)
                def _():
                    acc_ref[...] = part

                @pl.when(s != 0)
                def _():
                    acc_ref[...] += part
            else:
                acc_ref[...] += part

    @pl.when(s == bounds[-1][1] - 1)
    def _():
        out_ref[...] = acc_ref[...].astype(out_ref.dtype)


def product(chosen, kept, where):
    bounds, total = [], 0
    for _, positions, _ in chosen:
        bounds.append((total, total + len(positions)))
        total += len(positions)
    table = np.zeros((len(chosen) + 1, total), np.int32)
    for i, ((_, positions, ks), (lo, hi)) in enumerate(zip(chosen, bounds)):
        table[i, :lo], table[i, lo:hi], table[i, hi:] = positions[0], positions, positions[-1]
        table[-1, lo:hi] = ks
    rows, depth = chosen[0][0].shape[1:]
    width = kept.shape[2]
    a_specs = [pl.BlockSpec((1, rows, depth), lambda s, t, w, i=i: (t[i, s], 0, 0)) for i in range(len(chosen))]
    return pl.pallas_call(
        functools.partial(product_kernel, bounds),
        grid_spec=pltpu.PrefetchScalarGridSpec(
            num_scalar_prefetch=2,
            grid=(total,),
            in_specs=a_specs + [pl.BlockSpec((1, depth, width), lambda s, t, w: (w[t[len(chosen), s]], 0, 0))],
            out_specs=pl.BlockSpec((rows, width), lambda s, t, w: (0, 0)),
            scratch_shapes=[pltpu.VMEM((rows, width), jnp.float32)],
        ),
        out_shape=jax.ShapeDtypeStruct((rows, width), jnp.float32),
        compiler_params=pltpu.CompilerParams(vmem_limit_bytes=24 << 20),
        cost_estimate=pl.CostEstimate(
            flops=2 * rows * depth * width * total,
            bytes_accessed=2 * total * depth * (rows + width) + 4 * rows * width,
            transcendentals=0,
        ),
    )(jnp.asarray(table), where, *[c[0] for c in chosen], kept)


K_INDEX = {(off, k): i for i, (off, k) in enumerate((o, k) for o in (0, 1, -1, 2) for k in (0, 1))}


def pieces(items, row_place, kept, where):
    got = []
    for off in (0, 1, -1, 2):
        chosen = []
        for arr, labels in items:
            hits = [i for i, lab in enumerate(labels) if lab[row_place] == off]
            if hits:
                chosen.append((arr, hits, [K_INDEX[labels[i][1 - row_place], labels[i][2]] for i in hits]))
        part = product(chosen, kept, where).astype(SENT)
        got.append(permute(part, lambda z, y, x, c, off=off: (z + y + off * (side(c) if abs(off) == 1 else 1), y, x, c)))
    return got


def on_device(amps, ints, amp_mask, int_mask, vir_energy, pair_energy):
    rows, depth = amps.shape
    half = rows // 2
    part = jax.ShapeDtypeStruct((1, half, depth), amps.dtype)
    upper, lower = pl.pallas_call(
        screen_amps,
        in_specs=[pl.BlockSpec(memory_space=pltpu.SMEM), pl.BlockSpec(memory_space=pltpu.VMEM)],
        out_specs=[pl.BlockSpec(memory_space=pltpu.VMEM)] * 2,
        out_shape=[part, part],
    )(amp_mask, amps)
    to_plane = lambda z, y, x, c: (y, z - y, x, c)
    upper, lower = permute(upper, to_plane), permute(lower, to_plane)
    blocks = ints.shape[0] // depth
    kept = pl.pallas_call(
        screen_ints,
        grid_spec=pltpu.PrefetchScalarGridSpec(
            num_scalar_prefetch=1,
            grid=(blocks,),
            in_specs=[pl.BlockSpec((1, depth, ints.shape[1]), lambda s, m: (s, 0, 0))],
            out_specs=pl.BlockSpec((1, depth, ints.shape[1]), lambda s, m: (s, 0, 0)),
        ),
        out_shape=jax.ShapeDtypeStruct((blocks, depth, ints.shape[1]), ints.dtype),
    )(int_mask, ints.reshape(blocks, depth, ints.shape[1]))
    virt = lax.axis_index("virt")
    core, x = virt % 2, (virt // 2) % N
    d = 2 * core - 1
    where = jnp.stack([((x + off * (d if abs(off) == 1 else 1)) % N) * 2 + (core if k == 0 else 1 - core) for off, k in K_INDEX])
    got_upper = pieces(gather(upper, "x", "y", (0, 1, -1), (2,)), 1, kept, where)
    got_lower = pieces(gather(lower, "y", "x", (1, -1, 2), (0,)), 0, kept, where)
    total = lambda got: sum(g.astype(jnp.float32) for g in got)
    contracted = jnp.concatenate([total(got_upper), total(got_lower)], 0)
    denom = vir_energy[None, :] - pair_energy[:, None]
    return amps.astype(jnp.float32) + contracted / denom


def solution(mesh):
    return jax.shard_map(
        on_device,
        mesh=mesh,
        in_specs=(
            P("pair", "virt"),
            P("pair", "virt"),
            P("pair", "virt"),
            P("pair", "virt"),
            P("virt"),
            P("pair"),
        ),
        out_specs=P("pair", "virt"),
        check_vma=False,
    )
```

time: 471 us -> 240 us (0.51)
  waiting for transfers between devices: 405 us -> 79 us
  starting transfers between devices: 0.04 us -> 74.8 us
  Pallas kernels: 0 us -> 66.2 us
  matrix products: 27.8 us -> 0 us
  between operations: 13.4 us -> 0.7 us
  other arithmetic: 10.1 us -> 2.3 us
    all_gather x2 -> x0, waiting for transfers between devices: 405 us -> none  [the longest x1 330 us: on_device(): lax.all_gather(kept, 'pair', axis=0, tiled=True)]
    ppermute x0 -> x36, waiting for transfers between devices: none -> 79 us  [permute(): return lax.ppermute(arr, AXES, pairs)]
    ppermute x0 -> x36, starting transfers between devices: none -> 74.8 us  [permute(): return lax.ppermute(arr, AXES, pairs)]
    pallas_call x0 -> x10, Pallas kernels: none -> 66.2 us  [the longest x8 52.5 us: product(): pl.pallas_call(functools.partial(product_kernel, bounds), grid_spec=pltpu...]
    dot_general x1 -> x0, matrix products: 27.8 us -> none  [on_device(): jnp.dot(all_cols, lax.all_gather(kept, 'pair', axis=0, tiled=True), prefe...]
    mul x2 -> x0, other arithmetic: 9.39 us -> none  [the longest x1 8.45 us: on_device(): kept = ints * widen(int_mask)]
    unnamed x14 -> x59, local copies, waits for them, and re-layouts: 14.3 us -> 9.05 us
  transfers between devices with their start and end apart: 2 -> 36, of which waited for: 2 -> 8; matrix products, arithmetic and copies ran while one was open for 5% -> 2% of each run, Pallas kernels for 0% -> 27%
where the time goes in v1:
time: 240 us; the launch traced here: 236 us
  waiting for transfers between devices  79 us (33%)
  starting transfers between devices  74.8 us (31%)
  Pallas kernels  66.2 us (28%)
  local copies, waits for them, and re-layouts  12.9 us (5%)
    ppermute x36, waiting for transfers between devices, permute(): return lax.ppermute(arr, AXES, pairs)  79 us
    ppermute x36, starting transfers between devices, permute(): return lax.ppermute(arr, AXES, pairs)  74.8 us
    pallas_call x8, Pallas kernels, product(): pl.pallas_call(functools.partial(product_kernel, bounds), grid_spec=pltpu...  52.5 us
    pallas_call x1, Pallas kernels, on_device(): pl.pallas_call(screen_ints, grid_spec=pltpu.PrefetchScalarGridSpec(num_sc...  11.5 us
    unnamed x59, local copies, waits for them, and re-layouts  9.05 us
  transfers between devices with their start and end apart: 36, of which 8 were waited for; matrix products, arithmetic and copies ran while one was open for 2% of the time, Pallas kernels for 27%

profile of v1, /device:TPU:1, one launch (start us, length us, event | category | flops | bytes accessed | tf_op | source)
XLA Modules:
  0.0 235.9 jit_solution(5354962348168965280)
XLA Ops:
  0.0 2.2 shard_map.136
  7.0 22.5 %collective-permute-start.25 = (bf16[2,256,768]{2,1,0:T(8,128)(2,1)S(1)}, bf16[2,256,768]{2,1,0:T(8,128)(2,1)S(1)}, u32[]{:S(2)}, u32[]{:S(2)}) collective-permute-start(bf16[2,256,768]{2,1,0:T(8,128)(2,1)S(1)} %constant_dynamic-update-slice_fusion.5.refs_0_), channel_id=1, source_target_pairs={{0,8},{1,25},{2,10},{3,27},{4,12},{5,29},{6,14},{7,31},{8,16},{9,1... | collective-permute-start | bytes 2359304 | tf_op jit(solution)/shard_map/ppermute | solution.py:30
  31.3 2.5 %collective-permute-start.2 = (bf16[2,256,768]{2,1,0:T(8,128)(2,1)S(1)}, bf16[2,256,768]{2,1,0:T(8,128)(2,1)S(1)}, u32[]{:S(2)}, u32[]{:S(2)}) collective-permute-start(bf16[2,256,768]{2,1,0:T(8,128)(2,1)S(1)} %pad_maximum_fusion), channel_id=1, source_target_pairs={{0,2},{1,7},{2,4},{3,1},{4,6},{5,3},{6,0},{7,5},{8,10},{9,15},{10,... | collective-permute-start | bytes 2359304 | tf_op jit(solution)/shard_map/ppermute | solution.py:30
  33.8 10.1 %collective-permute-done.25 = bf16[2,256,768]{2,1,0:T(8,128)(2,1)S(1)} collective-permute-done((bf16[2,256,768]{2,1,0:T(8,128)(2,1)S(1)}, bf16[2,256,768]{2,1,0:T(8,128)(2,1)S(1)}, u32[]{:S(2)}, u32[]{:S(2)}) %collective-permute-start.25) | collective-permute-done | bytes 786464 | tf_op jit(solution)/shard_map/ppermute | solution.py:30
  44.0 3.0 %collective-permute-start.27 = (bf16[1,256,768]{2,1,0:T(8,128)(2,1)S(1)}, bf16[1,256,768]{2,1,0:T(8,128)(2,1)S(1)}, u32[]{:S(2)}, u32[]{:S(2)}) collective-permute-start(bf16[1,256,768]{2,1,0:T(8,128)(2,1)S(1)} %get-tuple-element.11), channel_id=1, source_target_pairs={{0,8},{1,25},{2,10},{3,27},{4,12},{5,29},{6,14},{7,31},{8,16},{9,1... | collective-permute-start | bytes 1179656 | tf_op jit(solution)/shard_map/ppermute | solution.py:30
  47.2 4.5 %collective-permute-done.27 = bf16[1,256,768]{2,1,0:T(8,128)(2,1)S(1)} collective-permute-done((bf16[1,256,768]{2,1,0:T(8,128)(2,1)S(1)}, bf16[1,256,768]{2,1,0:T(8,128)(2,1)S(1)}, u32[]{:S(2)}, u32[]{:S(2)}) %collective-permute-start.27) | collective-permute-done | bytes 393248 | tf_op jit(solution)/shard_map/ppermute | solution.py:30
  55.0 2.5 %collective-permute-start.29 = (bf16[6,256,768]{2,1,0:T(8,128)(2,1)S(1)}, bf16[6,256,768]{2,1,0:T(8,128)(2,1)S(1)}, u32[]{:S(2)}, u32[]{:S(2)}) collective-permute-start(bf16[6,256,768]{2,1,0:T(8,128)(2,1)S(1)} %constant_dynamic-update-slice_fusion.7.refs_0_), channel_id=1, source_target_pairs={{0,2},{1,7},{2,4},{3,1},{4,6},{5,3},{6,0},{7,5},{8,10},{9,15},{10,... | collective-permute-start | bytes 7077896 | tf_op jit(solution)/shard_map/ppermute | solution.py:30
  57.7 2.3 collective-permute-start.7
  60.8 35.2 %collective-permute-done.4 = bf16[1,256,768]{2,1,0:T(8,128)(2,1)S(1)} collective-permute-done((bf16[1,256,768]{2,1,0:T(8,128)(2,1)S(1)}, bf16[1,256,768]{2,1,0:T(8,128)(2,1)S(1)}, u32[]{:S(2)}, u32[]{:S(2)}) %collective-permute-start.4) | collective-permute-done | bytes 393248 | tf_op jit(solution)/shard_map/ppermute | solution.py:30
  96.0 2.2 collective-permute-start.5
  100.8 2.3 collective-permute-start.8
  103.1 2.4 slice.54
  105.4 12.6 %collective-permute-done.22.refs_3_ = bf16[1,256,768]{2,1,0:T(8,128)(2,1)} collective-permute-done((bf16[1,256,768]{2,1,0:T(8,128)(2,1)S(1)}, bf16[1,256,768]{2,1,0:T(8,128)(2,1)}, u32[]{:S(2)}, u32[]{:S(2)}) %collective-permute-start.22) | collective-permute-done | bytes 393248 | tf_op jit(solution)/shard_map/ppermute | solution.py:30
  118.0 2.6 %collective-permute-start.13 = (bf16[3,256,768]{2,1,0:T(8,128)(2,1)}, bf16[3,256,768]{2,1,0:T(8,128)(2,1)}, u32[]{:S(2)}, u32[]{:S(2)}) collective-permute-start(bf16[3,256,768]{2,1,0:T(8,128)(2,1)} %slice.54), channel_id=1, source_target_pairs={{0,8},{1,25},{2,10},{3,27},{4,12},{5,29},{6,14},{7,31},{8,16},{9,1... | collective-permute-start | bytes 3538952 | tf_op jit(solution)/shard_map/ppermute | solution.py:30
  124.1 11.5 %shard_map.137.refs_2_.refs_4_.refs_5_ = bf16[8,768,768]{2,1,0:T(8,128)(2,1)} custom-call(s32[48,6]{1,0:T(8,128)} %copy.15.mask_ref, bf16[8,768,768]{2,1,0:T(8,128)(2,1)} %bitcast.9), custom_call_target="tpu_custom_call" | custom-call | tf_op jit(solution)/shard_map/pallas_call | solution.py:193
  139.5 3.7 %copy-done = bf16[8,768,768]{2,1,0:T(8,128)(2,1)S(1)} copy-done((bf16[8,768,768]{2,1,0:T(8,128)(2,1)S(1)}, bf16[8,768,768]{2,1,0:T(8,128)(2,1)}, u32[]{:S(2)}) %copy-start) | copy-done | bytes 9437208
  146.6 6.4 %shard_map.142 = f32[256,768]{1,0:T(8,128)S(1)} custom-call(s32[6,8]{1,0:T(8,128)S(1)} %copy-done.15, s32[8]{0:T(128)S(1)} %stack.35.where_ref, bf16[2,256,768]{2,1,0:T(8,128)(2,1)S(1)} %copy-done.8, bf16[2,256,768]{2,1,0:T(8,128)(2,1)S(1)} %copy-done.6, bf16[2,256,768]{2,1,0:T(8,128)(2,1)S(1)} %copy-done.12, ...), custom_call_target="tpu_custom_call" | custom-call | flops 2415919104 | bytes 13369344 | tf_op jit(solution)/shard_map/pallas_call | solution.py:145
  153.0 5.1 %shard_map.138 = f32[256,768]{1,0:T(8,128)S(1)} custom-call(s32[3,8]{1,0:T(4,128)S(1)} %copy-done.13, s32[8]{0:T(128)S(1)} %stack.35.where_ref, bf16[6,256,768]{2,1,0:T(8,128)(2,1)S(1)} %copy-done.4, bf16[2,256,768]{2,1,0:T(8,128)(2,1)S(1)} %copy-done.10, bf16[8,768,768]{2,1,0:T(8,128)(2,1)S(1)} %copy-done), custom_call_target="tpu_custom_call" | custom-call | flops 2415919104 | bytes 13369344 | tf_op jit(solution)/shard_map/pallas_call | solution.py:145
  158.3 7.7 %shard_map.139 = f32[256,768]{1,0:T(8,128)S(1)} custom-call(s32[3,8]{1,0:T(4,128)S(1)} %copy-done.13, s32[8]{0:T(128)S(1)} %stack.35.where_ref, bf16[6,256,768]{2,1,0:T(8,128)(2,1)} %collective-permute-done.7.refs_0_, bf16[2,256,768]{2,1,0:T(8,128)(2,1)} %collective-permute-done.8.refs_1_, bf16[8,768,768]{2,1,0:T(8,128)(2,1)S(1)} %copy-done), custom_call_target="tpu_custom_call" | custom-call | flops 2415919104 | bytes 13369344 | tf_op jit(solution)/shard_map/pallas_call | solution.py:145
  167.4 6.7 %shard_map.145 = f32[256,768]{1,0:T(8,128)S(1)} custom-call(s32[6,8]{1,0:T(8,128)S(1)} %copy-done.18, s32[8]{0:T(128)S(1)} %stack.35.where_ref, bf16[6,256,768]{2,1,0:T(8,128)(2,1)S(1)} %copy-done.2, bf16[6,256,768]{2,1,0:T(8,128)(2,1)S(1)} %collective-permute-done.29.refs_1_, bf16[6,256,768]{2,1,0:T(8,128)(2,1)} %collective-permute-done.30.refs_2_, ...), custom_call_target="tpu_custom_call" | custom-call | flops 2415919104 | bytes 13369344 | tf_op jit(solution)/shard_map/pallas_call | solution.py:145
  174.1 6.7 %shard_map.144 = f32[256,768]{1,0:T(8,128)S(1)} custom-call(s32[6,8]{1,0:T(8,128)S(1)} %copy-done.17, s32[8]{0:T(128)S(1)} %stack.35.where_ref, bf16[6,256,768]{2,1,0:T(8,128)(2,1)S(1)} %copy-done.2, bf16[6,256,768]{2,1,0:T(8,128)(2,1)S(1)} %collective-permute-done.29.refs_1_, bf16[6,256,768]{2,1,0:T(8,128)(2,1)} %collective-permute-done.30.refs_2_, ...), custom_call_target="tpu_custom_call" | custom-call | flops 2415919104 | bytes 13369344 | tf_op jit(solution)/shard_map/pallas_call | solution.py:145
  180.8 6.7 %shard_map.143 = f32[256,768]{1,0:T(8,128)S(1)} custom-call(s32[6,8]{1,0:T(8,128)S(1)} %copy-done.16, s32[8]{0:T(128)S(1)} %stack.35.where_ref, bf16[6,256,768]{2,1,0:T(8,128)(2,1)S(1)} %copy-done.2, bf16[6,256,768]{2,1,0:T(8,128)(2,1)S(1)} %collective-permute-done.29.refs_1_, bf16[6,256,768]{2,1,0:T(8,128)(2,1)} %collective-permute-done.30.refs_2_, ...), custom_call_target="tpu_custom_call" | custom-call | flops 2415919104 | bytes 13369344 | tf_op jit(solution)/shard_map/pallas_call | solution.py:145
  187.6 2.4 %collective-permute-start.35 = (f16[256,768]{1,0:T(8,128)(2,1)S(1)}, f16[256,768]{1,0:T(8,128)(2,1)S(1)}, u32[]{:S(2)}, u32[]{:S(2)}) collective-permute-start(f16[256,768]{1,0:T(8,128)(2,1)S(1)} %convert_element_type.66), channel_id=1, source_target_pairs={{0,64},{1,65},{2,66},{3,67},{4,68},{5,69},{6,70},{7,71},{8,104},{9... | collective-permute-start | bytes 1179656 | tf_op jit(solution)/shard_map/ppermute | solution.py:30
  190.0 3.6 %collective-permute-start.34 = (f16[256,768]{1,0:T(8,128)(2,1)S(1)}, f16[256,768]{1,0:T(8,128)(2,1)S(1)}, u32[]{:S(2)}, u32[]{:S(2)}) collective-permute-start(f16[256,768]{1,0:T(8,128)(2,1)S(1)} %convert_element_type.64), channel_id=1, source_target_pairs={{0,32},{1,97},{2,34},{3,99},{4,36},{5,101},{6,38},{7,103},{8,72},{... | collective-permute-start | bytes 1179656 | tf_op jit(solution)/shard_map/ppermute | solution.py:30
  193.6 2.7 %collective-permute-start.33 = (f16[256,768]{1,0:T(8,128)(2,1)S(1)}, f16[256,768]{1,0:T(8,128)(2,1)S(1)}, u32[]{:S(2)}, u32[]{:S(2)}) collective-permute-start(f16[256,768]{1,0:T(8,128)(2,1)S(1)} %convert_element_type.62), channel_id=1, source_target_pairs={{0,96},{1,33},{2,98},{3,35},{4,100},{5,37},{6,102},{7,39},{8,8},{9... | collective-permute-start | bytes 1179656 | tf_op jit(solution)/shard_map/ppermute | solution.py:30
  196.4 6.4 %shard_map.141 = f32[256,768]{1,0:T(8,128)S(1)} custom-call(s32[5,8]{1,0:T(8,128)S(1)} %copy-done.14, s32[8]{0:T(128)S(1)} %stack.35.where_ref, bf16[3,256,768]{2,1,0:T(8,128)(2,1)} %collective-permute-done.13.refs_0_, bf16[3,256,768]{2,1,0:T(8,128)(2,1)S(1)} %collective-permute-done.14.refs_1_, bf16[1,256,768]{2,1,0:T(8,128)(2,1)S(1)} %collective-permute-done.15.refs_2_, ...), custom_call_target="tpu_custom_call" | custom-call | flops 2415919104 | bytes 13369344 | tf_op jit(solution)/shard_map/pallas_call | solution.py:145
  203.6 7.0 %shard_map.140 = f32[256,768]{1,0:T(8,128)S(1)} custom-call(s32[3,8]{1,0:T(4,128)S(1)} %copy-done.19, s32[8]{0:T(128)S(1)} %stack.35.where_ref, bf16[6,256,768]{2,1,0:T(8,128)(2,1)} %collective-permute-done.10.refs_0_, bf16[2,256,768]{2,1,0:T(8,128)(2,1)S(1)} %collective-permute-done.11.refs_1_, bf16[8,768,768]{2,1,0:T(8,128)(2,1)S(1)} %copy-done), custom_call_target="tpu_custom_call" | custom-call | flops 2415919104 | bytes 13369344 | tf_op jit(solution)/shard_map/pallas_call | solution.py:145
  210.7 3.5 %collective-permute-start.9 = (f16[256,768]{1,0:T(8,128)(2,1)S(1)}, f16[256,768]{1,0:T(8,128)(2,1)S(1)}, u32[]{:S(2)}, u32[]{:S(2)}) collective-permute-start(f16[256,768]{1,0:T(8,128)(2,1)S(1)} %convert_element_type.54), channel_id=1, source_target_pairs={{0,96},{1,33},{2,98},{3,35},{4,100},{5,37},{6,102},{7,39},{8,8},{9... | collective-permute-start | bytes 1179656 | tf_op jit(solution)/shard_map/ppermute | solution.py:30
  214.2 3.7 %collective-permute-start.17 = (f16[256,768]{1,0:T(8,128)(2,1)S(1)}, f16[256,768]{1,0:T(8,128)(2,1)S(1)}, u32[]{:S(2)}, u32[]{:S(2)}) collective-permute-start(f16[256,768]{1,0:T(8,128)(2,1)S(1)} %convert_element_type.58), channel_id=1, source_target_pairs={{0,64},{1,65},{2,66},{3,67},{4,68},{5,69},{6,70},{7,71},{8,104},{9... | collective-permute-start | bytes 1179656 | tf_op jit(solution)/shard_map/ppermute | solution.py:30
  217.9 2.5 %collective-permute-start.12 = (f16[256,768]{1,0:T(8,128)(2,1)S(1)}, f16[256,768]{1,0:T(8,128)(2,1)S(1)}, u32[]{:S(2)}, u32[]{:S(2)}) collective-permute-start(f16[256,768]{1,0:T(8,128)(2,1)S(1)} %convert_element_type.56), channel_id=1, source_target_pairs={{0,32},{1,97},{2,34},{3,99},{4,36},{5,101},{6,38},{7,103},{8,72},{... | collective-permute-start | bytes 1179656 | tf_op jit(solution)/shard_map/ppermute | solution.py:30
  220.6 9.2 %collective-permute-done.17 = f16[256,768]{1,0:T(8,128)(2,1)S(1)} collective-permute-done((f16[256,768]{1,0:T(8,128)(2,1)S(1)}, f16[256,768]{1,0:T(8,128)(2,1)S(1)}, u32[]{:S(2)}, u32[]{:S(2)}) %collective-permute-start.17) | collective-permute-done | bytes 393248 | tf_op jit(solution)/shard_map/ppermute | solution.py:30
  229.8 4.4 %collective-permute-done.12 = f16[256,768]{1,0:T(8,128)(2,1)S(1)} collective-permute-done((f16[256,768]{1,0:T(8,128)(2,1)S(1)}, f16[256,768]{1,0:T(8,128)(2,1)S(1)}, u32[]{:S(2)}, u32[]{:S(2)}) %collective-permute-start.12) | collective-permute-done | bytes 393248 | tf_op jit(solution)/shard_map/ppermute | solution.py:30
  (132 shorter events, 28.5 us)
Async XLA Ops:
  5.3 24.2 %collective-permute-start = (bf16[1,256,768]{2,1,0:T(8,128)(2,1)}, bf16[1,256,768]{2,1,0:T(8,128)(2,1)S(1)}, u32[]{:S(2)}, u32[]{:S(2)}) collective-permute-start(bf16[1,256,768]{2,1,0:T(8,128)(2,1)} %get-tuple-element.7), channel_id=1, source_target_pairs={{0,0},{1,1},{2,2},{3,3},{4,4},{5,5},{6,6},{7,7},{8,56},{9,57},{10,... | collective-permute-start | bytes 1179656 | tf_op jit(solution)/shard_map/ppermute | solution.py:30
  7.0 37.0 %collective-permute-start.25 = (bf16[2,256,768]{2,1,0:T(8,128)(2,1)S(1)}, bf16[2,256,768]{2,1,0:T(8,128)(2,1)S(1)}, u32[]{:S(2)}, u32[]{:S(2)}) collective-permute-start(bf16[2,256,768]{2,1,0:T(8,128)(2,1)S(1)} %constant_dynamic-update-slice_fusion.5.refs_0_), channel_id=1, source_target_pairs={{0,8},{1,25},{2,10},{3,27},{4,12},{5,29},{6,14},{7,31},{8,16},{9,1... | collective-permute-start | bytes 2359304 | tf_op jit(solution)/shard_map/ppermute | solution.py:30
  31.3 15.8 %collective-permute-start.2 = (bf16[2,256,768]{2,1,0:T(8,128)(2,1)S(1)}, bf16[2,256,768]{2,1,0:T(8,128)(2,1)S(1)}, u32[]{:S(2)}, u32[]{:S(2)}) collective-permute-start(bf16[2,256,768]{2,1,0:T(8,128)(2,1)S(1)} %pad_maximum_fusion), channel_id=1, source_target_pairs={{0,2},{1,7},{2,4},{3,1},{4,6},{5,3},{6,0},{7,5},{8,10},{9,15},{10,... | collective-permute-start | bytes 2359304 | tf_op jit(solution)/shard_map/ppermute | solution.py:30
  43.9 9.7 %collective-permute-start.26 = (bf16[2,256,768]{2,1,0:T(8,128)(2,1)S(1)}, bf16[2,256,768]{2,1,0:T(8,128)(2,1)S(1)}, u32[]{:S(2)}, u32[]{:S(2)}) collective-permute-start(bf16[2,256,768]{2,1,0:T(8,128)(2,1)S(1)} %collective-permute-done.25), channel_id=1, source_target_pairs={{0,1},{1,0},{2,3},{3,2},{4,5},{5,4},{6,7},{7,6},{8,9},{9,8},{10,11... | collective-permute-start | bytes 2359304 | tf_op jit(solution)/shard_map/ppermute | solution.py:30
  44.0 7.8 %collective-permute-start.27 = (bf16[1,256,768]{2,1,0:T(8,128)(2,1)S(1)}, bf16[1,256,768]{2,1,0:T(8,128)(2,1)S(1)}, u32[]{:S(2)}, u32[]{:S(2)}) collective-permute-start(bf16[1,256,768]{2,1,0:T(8,128)(2,1)S(1)} %get-tuple-element.11), channel_id=1, source_target_pairs={{0,8},{1,25},{2,10},{3,27},{4,12},{5,29},{6,14},{7,31},{8,16},{9,1... | collective-permute-start | bytes 1179656 | tf_op jit(solution)/shard_map/ppermute | solution.py:30
  47.1 10.4 %collective-permute-start.3 = (bf16[2,256,768]{2,1,0:T(8,128)(2,1)S(1)}, bf16[2,256,768]{2,1,0:T(8,128)(2,1)S(1)}, u32[]{:S(2)}, u32[]{:S(2)}) collective-permute-start(bf16[2,256,768]{2,1,0:T(8,128)(2,1)S(1)} %collective-permute-done.2), channel_id=1, source_target_pairs={{0,1},{1,0},{2,3},{3,2},{4,5},{5,4},{6,7},{7,6},{8,9},{9,8},{10,11... | collective-permute-start | bytes 2359304 | tf_op jit(solution)/shard_map/ppermute | solution.py:30
  55.0 43.1 %collective-permute-start.29 = (bf16[6,256,768]{2,1,0:T(8,128)(2,1)S(1)}, bf16[6,256,768]{2,1,0:T(8,128)(2,1)S(1)}, u32[]{:S(2)}, u32[]{:S(2)}) collective-permute-start(bf16[6,256,768]{2,1,0:T(8,128)(2,1)S(1)} %constant_dynamic-update-slice_fusion.7.refs_0_), channel_id=1, source_target_pairs={{0,2},{1,7},{2,4},{3,1},{4,6},{5,3},{6,0},{7,5},{8,10},{9,15},{10,... | collective-permute-start | bytes 7077896 | tf_op jit(solution)/shard_map/ppermute | solution.py:30
  57.7 43.1 %collective-permute-start.7 = (bf16[6,256,768]{2,1,0:T(8,128)(2,1)S(1)}, bf16[6,256,768]{2,1,0:T(8,128)(2,1)}, u32[]{:S(2)}, u32[]{:S(2)}) collective-permute-start(bf16[6,256,768]{2,1,0:T(8,128)(2,1)S(1)} %slice_dynamic-update-slice_fusion.3.refs_0_), channel_id=1, source_target_pairs={{0,8},{1,25},{2,10},{3,27},{4,12},{5,29},{6,14},{7,31},{8,16},{9,1... | collective-permute-start | bytes 7077896 | tf_op jit(solution)/shard_map/ppermute | solution.py:30
  60.0 39.8 %collective-permute-start.20 = (bf16[2,256,768]{2,1,0:T(8,128)(2,1)S(1)}, bf16[2,256,768]{2,1,0:T(8,128)(2,1)S(1)}, u32[]{:S(2)}, u32[]{:S(2)}) collective-permute-start(bf16[2,256,768]{2,1,0:T(8,128)(2,1)S(1)} %constant_dynamic-update-slice_fusion.5.refs_0_), channel_id=1, source_target_pairs={{0,2},{1,7},{2,4},{3,1},{4,6},{5,3},{6,0},{7,5},{8,10},{9,15},{10,... | collective-permute-start | bytes 2359304 | tf_op jit(solution)/shard_map/ppermute | solution.py:30
  60.5 35.5 %collective-permute-start.4 = (bf16[1,256,768]{2,1,0:T(8,128)(2,1)S(1)}, bf16[1,256,768]{2,1,0:T(8,128)(2,1)S(1)}, u32[]{:S(2)}, u32[]{:S(2)}) collective-permute-start(bf16[1,256,768]{2,1,0:T(8,128)(2,1)S(1)} %get-tuple-element.9), channel_id=1, source_target_pairs={{0,2},{1,7},{2,4},{3,1},{4,6},{5,3},{6,0},{7,5},{8,10},{9,15},{10,... | collective-permute-start | bytes 1179656 | tf_op jit(solution)/shard_map/ppermute | solution.py:30
  96.0 4.3 %collective-permute-start.5 = (bf16[1,256,768]{2,1,0:T(8,128)(2,1)S(1)}, bf16[1,256,768]{2,1,0:T(8,128)(2,1)S(1)}, u32[]{:S(2)}, u32[]{:S(2)}) collective-permute-start(bf16[1,256,768]{2,1,0:T(8,128)(2,1)S(1)} %collective-permute-done.4), channel_id=1, source_target_pairs={{0,1},{1,0},{2,3},{3,2},{4,5},{5,4},{6,7},{7,6},{8,9},{9,8},{10,11... | collective-permute-start | bytes 1179656 | tf_op jit(solution)/shard_map/ppermute | solution.py:30
  98.1 67.9 %collective-permute-start.30 = (bf16[6,256,768]{2,1,0:T(8,128)(2,1)S(1)}, bf16[6,256,768]{2,1,0:T(8,128)(2,1)}, u32[]{:S(2)}, u32[]{:S(2)}) collective-permute-start(bf16[6,256,768]{2,1,0:T(8,128)(2,1)S(1)} %collective-permute-done.29.refs_1_), channel_id=1, source_target_pairs={{0,1},{1,0},{2,3},{3,2},{4,5},{5,4},{6,7},{7,6},{8,9},{9,8},{10,11... | collective-permute-start | bytes 7077896 | tf_op jit(solution)/shard_map/ppermute | solution.py:30
  98.3 24.6 %collective-permute-start.31 = (bf16[3,256,768]{2,1,0:T(8,128)(2,1)S(1)}, bf16[3,256,768]{2,1,0:T(8,128)(2,1)S(1)}, u32[]{:S(2)}, u32[]{:S(2)}) collective-permute-start(bf16[3,256,768]{2,1,0:T(8,128)(2,1)S(1)} %slice.61), channel_id=1, source_target_pairs={{0,2},{1,7},{2,4},{3,1},{4,6},{5,3},{6,0},{7,5},{8,10},{9,15},{10,... | collective-permute-start | bytes 3538952 | tf_op jit(solution)/shard_map/ppermute | solution.py:30
  99.8 18.2 %collective-permute-start.22 = (bf16[1,256,768]{2,1,0:T(8,128)(2,1)S(1)}, bf16[1,256,768]{2,1,0:T(8,128)(2,1)}, u32[]{:S(2)}, u32[]{:S(2)}) collective-permute-start(bf16[1,256,768]{2,1,0:T(8,128)(2,1)S(1)} %slice.56), channel_id=1, source_target_pairs={{0,2},{1,7},{2,4},{3,1},{4,6},{5,3},{6,0},{7,5},{8,10},{9,15},{10,... | collective-permute-start | bytes 1179656 | tf_op jit(solution)/shard_map/ppermute | solution.py:30
  100.3 20.4 %collective-permute-start.21 = (bf16[2,256,768]{2,1,0:T(8,128)(2,1)S(1)}, bf16[2,256,768]{2,1,0:T(8,128)(2,1)S(1)}, u32[]{:S(2)}, u32[]{:S(2)}) collective-permute-start(bf16[2,256,768]{2,1,0:T(8,128)(2,1)S(1)} %collective-permute-done.20.refs_1_), channel_id=1, source_target_pairs={{0,1},{1,0},{2,3},{3,2},{4,5},{5,4},{6,7},{7,6},{8,9},{9,8},{10,11... | collective-permute-start | bytes 2359304 | tf_op jit(solution)/shard_map/ppermute | solution.py:30
  100.8 22.2 %collective-permute-start.8 = (bf16[2,256,768]{2,1,0:T(8,128)(2,1)S(1)}, bf16[2,256,768]{2,1,0:T(8,128)(2,1)}, u32[]{:S(2)}, u32[]{:S(2)}) collective-permute-start(bf16[2,256,768]{2,1,0:T(8,128)(2,1)S(1)} %constant_dynamic-update-slice_fusion.3.refs_1_), channel_id=1, source_target_pairs={{0,8},{1,25},{2,10},{3,27},{4,12},{5,29},{6,14},{7,31},{8,16},{9,1... | collective-permute-start | bytes 2359304 | tf_op jit(solution)/shard_map/ppermute | solution.py:30
  118.0 20.4 %collective-permute-start.13 = (bf16[3,256,768]{2,1,0:T(8,128)(2,1)}, bf16[3,256,768]{2,1,0:T(8,128)(2,1)}, u32[]{:S(2)}, u32[]{:S(2)}) collective-permute-start(bf16[3,256,768]{2,1,0:T(8,128)(2,1)} %slice.54), channel_id=1, source_target_pairs={{0,8},{1,25},{2,10},{3,27},{4,12},{5,29},{6,14},{7,31},{8,16},{9,1... | collective-permute-start | bytes 3538952 | tf_op jit(solution)/shard_map/ppermute | solution.py:30
  121.6 81.3 %collective-permute-start.10 = (bf16[6,256,768]{2,1,0:T(8,128)(2,1)}, bf16[6,256,768]{2,1,0:T(8,128)(2,1)}, u32[]{:S(2)}, u32[]{:S(2)}) collective-permute-start(bf16[6,256,768]{2,1,0:T(8,128)(2,1)} %collective-permute-done.7.refs_0_), channel_id=1, source_target_pairs={{0,1},{1,0},{2,3},{3,2},{4,5},{5,4},{6,7},{7,6},{8,9},{9,8},{10,11... | collective-permute-start | bytes 7077896 | tf_op jit(solution)/shard_map/ppermute | solution.py:30
  122.9 43.9 %collective-permute-start.32 = (bf16[3,256,768]{2,1,0:T(8,128)(2,1)S(1)}, bf16[3,256,768]{2,1,0:T(8,128)(2,1)}, u32[]{:S(2)}, u32[]{:S(2)}) collective-permute-start(bf16[3,256,768]{2,1,0:T(8,128)(2,1)S(1)} %collective-permute-done.31.refs_3_), channel_id=1, source_target_pairs={{0,1},{1,0},{2,3},{3,2},{4,5},{5,4},{6,7},{7,6},{8,9},{9,8},{10,11... | collective-permute-start | bytes 3538952 | tf_op jit(solution)/shard_map/ppermute | solution.py:30
  123.0 13.8 %collective-permute-start.23 = (bf16[1,256,768]{2,1,0:T(8,128)(2,1)}, bf16[1,256,768]{2,1,0:T(8,128)(2,1)}, u32[]{:S(2)}, u32[]{:S(2)}) collective-permute-start(bf16[1,256,768]{2,1,0:T(8,128)(2,1)} %collective-permute-done.22.refs_3_), channel_id=1, source_target_pairs={{0,1},{1,0},{2,3},{3,2},{4,5},{5,4},{6,7},{7,6},{8,9},{9,8},{10,11... | collective-permute-start | bytes 1179656 | tf_op jit(solution)/shard_map/ppermute | solution.py:30
  136.8 21.4 %collective-permute-start.15 = (bf16[1,256,768]{2,1,0:T(8,128)(2,1)S(1)}, bf16[1,256,768]{2,1,0:T(8,128)(2,1)S(1)}, u32[]{:S(2)}, u32[]{:S(2)}) collective-permute-start(bf16[1,256,768]{2,1,0:T(8,128)(2,1)S(1)} %slice.55), channel_id=1, source_target_pairs={{0,8},{1,25},{2,10},{3,27},{4,12},{5,29},{6,14},{7,31},{8,16},{9,1... | collective-permute-start | bytes 1179656 | tf_op jit(solution)/shard_map/ppermute | solution.py:30
  138.4 55.2 %collective-permute-start.14 = (bf16[3,256,768]{2,1,0:T(8,128)(2,1)}, bf16[3,256,768]{2,1,0:T(8,128)(2,1)S(1)}, u32[]{:S(2)}, u32[]{:S(2)}) collective-permute-start(bf16[3,256,768]{2,1,0:T(8,128)(2,1)} %collective-permute-done.13.refs_0_), channel_id=1, source_target_pairs={{0,1},{1,0},{2,3},{3,2},{4,5},{5,4},{6,7},{7,6},{8,9},{9,8},{10,11... | collective-permute-start | bytes 3538952 | tf_op jit(solution)/shard_map/ppermute | solution.py:30
  158.2 31.8 %collective-permute-start.11 = (bf16[2,256,768]{2,1,0:T(8,128)(2,1)}, bf16[2,256,768]{2,1,0:T(8,128)(2,1)S(1)}, u32[]{:S(2)}, u32[]{:S(2)}) collective-permute-start(bf16[2,256,768]{2,1,0:T(8,128)(2,1)} %collective-permute-done.8.refs_1_), channel_id=1, source_target_pairs={{0,1},{1,0},{2,3},{3,2},{4,5},{5,4},{6,7},{7,6},{8,9},{9,8},{10,11... | collective-permute-start | bytes 2359304 | tf_op jit(solution)/shard_map/ppermute | solution.py:30
  166.1 44.6 %collective-permute-start.24 = (f16[256,768]{1,0:T(8,128)(2,1)S(1)}, f16[256,768]{1,0:T(8,128)(2,1)S(1)}, u32[]{:S(2)}, u32[]{:S(2)}) collective-permute-start(f16[256,768]{1,0:T(8,128)(2,1)S(1)} %convert_element_type.60), channel_id=1, source_target_pairs={{0,0},{1,1},{2,2},{3,3},{4,4},{5,5},{6,6},{7,7},{8,40},{9,41},{10,... | collective-permute-start | bytes 1179656 | tf_op jit(solution)/shard_map/ppermute | solution.py:30
  166.8 20.8 %collective-permute-start.16 = (bf16[1,256,768]{2,1,0:T(8,128)(2,1)S(1)}, bf16[1,256,768]{2,1,0:T(8,128)(2,1)S(1)}, u32[]{:S(2)}, u32[]{:S(2)}) collective-permute-start(bf16[1,256,768]{2,1,0:T(8,128)(2,1)S(1)} %collective-permute-done.15.refs_2_), channel_id=1, source_target_pairs={{0,1},{1,0},{2,3},{3,2},{4,5},{5,4},{6,7},{7,6},{8,9},{9,8},{10,11... | collective-permute-start | bytes 1179656 | tf_op jit(solution)/shard_map/ppermute | solution.py:30
  187.6 26.6 %collective-permute-start.35 = (f16[256,768]{1,0:T(8,128)(2,1)S(1)}, f16[256,768]{1,0:T(8,128)(2,1)S(1)}, u32[]{:S(2)}, u32[]{:S(2)}) collective-permute-start(f16[256,768]{1,0:T(8,128)(2,1)S(1)} %convert_element_type.66), channel_id=1, source_target_pairs={{0,64},{1,65},{2,66},{3,67},{4,68},{5,69},{6,70},{7,71},{8,104},{9... | collective-permute-start | bytes 1179656 | tf_op jit(solution)/shard_map/ppermute | solution.py:30
  190.0 27.9 %collective-permute-start.34 = (f16[256,768]{1,0:T(8,128)(2,1)S(1)}, f16[256,768]{1,0:T(8,128)(2,1)S(1)}, u32[]{:S(2)}, u32[]{:S(2)}) collective-permute-start(f16[256,768]{1,0:T(8,128)(2,1)S(1)} %convert_element_type.64), channel_id=1, source_target_pairs={{0,32},{1,97},{2,34},{3,99},{4,36},{5,101},{6,38},{7,103},{8,72},{... | collective-permute-start | bytes 1179656 | tf_op jit(solution)/shard_map/ppermute | solution.py:30
  193.6 26.8 %collective-permute-start.33 = (f16[256,768]{1,0:T(8,128)(2,1)S(1)}, f16[256,768]{1,0:T(8,128)(2,1)S(1)}, u32[]{:S(2)}, u32[]{:S(2)}) collective-permute-start(f16[256,768]{1,0:T(8,128)(2,1)S(1)} %convert_element_type.62), channel_id=1, source_target_pairs={{0,96},{1,33},{2,98},{3,35},{4,100},{5,37},{6,102},{7,39},{8,8},{9... | collective-permute-start | bytes 1179656 | tf_op jit(solution)/shard_map/ppermute | solution.py:30
  202.9 17.7 %collective-permute-start.6 = (f16[256,768]{1,0:T(8,128)(2,1)S(1)}, f16[256,768]{1,0:T(8,128)(2,1)S(1)}, u32[]{:S(2)}, u32[]{:S(2)}) collective-permute-start(f16[256,768]{1,0:T(8,128)(2,1)S(1)} %convert_element_type.52), channel_id=1, source_target_pairs={{0,0},{1,1},{2,2},{3,3},{4,4},{5,5},{6,6},{7,7},{8,40},{9,41},{10,... | collective-permute-start | bytes 1179656 | tf_op jit(solution)/shard_map/ppermute | solution.py:30
  210.7 10.0 %collective-permute-start.9 = (f16[256,768]{1,0:T(8,128)(2,1)S(1)}, f16[256,768]{1,0:T(8,128)(2,1)S(1)}, u32[]{:S(2)}, u32[]{:S(2)}) collective-permute-start(f16[256,768]{1,0:T(8,128)(2,1)S(1)} %convert_element_type.54), channel_id=1, source_target_pairs={{0,96},{1,33},{2,98},{3,35},{4,100},{5,37},{6,102},{7,39},{8,8},{9... | collective-permute-start | bytes 1179656 | tf_op jit(solution)/shard_map/ppermute | solution.py:30
  214.2 15.6 %collective-permute-start.17 = (f16[256,768]{1,0:T(8,128)(2,1)S(1)}, f16[256,768]{1,0:T(8,128)(2,1)S(1)}, u32[]{:S(2)}, u32[]{:S(2)}) collective-permute-start(f16[256,768]{1,0:T(8,128)(2,1)S(1)} %convert_element_type.58), channel_id=1, source_target_pairs={{0,64},{1,65},{2,66},{3,67},{4,68},{5,69},{6,70},{7,71},{8,104},{9... | collective-permute-start | bytes 1179656 | tf_op jit(solution)/shard_map/ppermute | solution.py:30
  217.9 16.3 %collective-permute-start.12 = (f16[256,768]{1,0:T(8,128)(2,1)S(1)}, f16[256,768]{1,0:T(8,128)(2,1)S(1)}, u32[]{:S(2)}, u32[]{:S(2)}) collective-permute-start(f16[256,768]{1,0:T(8,128)(2,1)S(1)} %convert_element_type.56), channel_id=1, source_target_pairs={{0,32},{1,97},{2,34},{3,99},{4,36},{5,101},{6,38},{7,103},{8,72},{... | collective-permute-start | bytes 1179656 | tf_op jit(solution)/shard_map/ppermute | solution.py:30
  (28 other events, 402.2 us)

commit v2 on v0

v2 whole, which is shorter than its diff:
```python
import functools

import jax
import jax.numpy as jnp
import numpy as np
from jax import lax
from jax.experimental import pallas as pl
from jax.experimental.pallas import tpu as pltpu
from jax.sharding import PartitionSpec as P

TILE = 128
AXES = ("pair", "virt")
N = 4
SENT = jnp.float16
FLIP = {0: 0, 1: -1, -1: 1, 2: 2}


def lin(z, y, x, c):
    return ((z % N) * N + y % N) * 2 * N + (x % N) * 2 + c


def permute(arr, to):
    pairs = [
        (lin(z, y, x, c), lin(*to(z, y, x, c)))
        for z in range(N)
        for y in range(N)
        for x in range(N)
        for c in range(2)
    ]
    return lax.ppermute(arr, AXES, pairs)


def side(c):
    return -1 if c == 0 else 1


def swap(arr):
    return permute(arr, lambda z, y, x, c: (z, y, x, 1 - c))


def shift(arr, axis):
    if axis == "x":
        return permute(arr, lambda z, y, x, c: (z, y, x - side(c), c))
    return permute(arr, lambda z, y, x, c: (z, y - side(c), x, c))


def swapped(item):
    (arr,), offs, koffs, flip = item
    return (swap(arr),), tuple(FLIP[o] for o in offs), tuple(FLIP[o] for o in koffs), not flip


def tie(value, *others):
    return lax.optimization_barrier((value, *others))[0]


def first_round(own, other, axis):
    near = shift(jnp.concatenate([own, other], 0), axis)
    far = shift(near[:1], axis)
    near_swapped, far_swapped = swap(near), swap(far)
    return {
        (0, 0): own,
        (0, 1): other,
        (1, 0): near[:1],
        (1, 1): near[1:],
        (-1, 1): near_swapped[:1],
        (-1, 0): near_swapped[1:],
        (2, 0): far,
        (2, 1): far_swapped,
    }


def screen_amps(mask_ref, amps_ref, *out_refs):
    starts = np.cumsum([0] + [o.shape[1] for o in out_refs]).tolist()
    for out_ref, lo, hi in zip(out_refs, starts, starts[1:]):
        for top in range(lo, hi, TILE):
            top_tile = top // TILE
            end = min(hi, (top_tile + 1) * TILE)
            for j in range(amps_ref.shape[1] // TILE):
                tile = amps_ref[top:end, j * TILE : (j + 1) * TILE]
                out_ref[0, top - lo : end - lo, j * TILE : (j + 1) * TILE] = jnp.where(
                    mask_ref[top_tile, j] != 0, tile, jnp.zeros_like(tile)
                )


def screen_ints(mask_ref, ints_ref, out_ref):
    step = pl.program_id(0)
    n = ints_ref.shape[0] // TILE
    for i in range(n):
        for j in range(ints_ref.shape[1] // TILE):
            tile = ints_ref[i * TILE : (i + 1) * TILE, j * TILE : (j + 1) * TILE]
            out_ref[i * TILE : (i + 1) * TILE, j * TILE : (j + 1) * TILE] = jnp.where(
                mask_ref[step * n + i, j] != 0, tile, jnp.zeros_like(tile)
            )


OFFS = (0, 1, -1, 2)
CORE = 4


def product_kernel(phases, n_init, n_out, table_ref, where_ref, *refs):
    n = sum(count for _, _, lanes in phases for count, _, _ in lanes)
    a_refs, kept_ref, init_refs, out_refs = refs[:n], refs[n], refs[n + 1 : n + 1 + n_init], refs[-n_out:]
    s = pl.program_id(0)
    core = where_ref[CORE]
    rows = out_refs[0].shape[0]

    def add(places, lanes):
        sides = []
        for first, second in lanes:
            sides.append(jnp.concatenate([first, second], -1))
        a = sides[0] if len(sides) == 1 else jnp.concatenate(sides, 0)
        part = jnp.dot(a, kept_ref[...], preferred_element_type=jnp.float32)
        for i, o in enumerate(places):
            mine = part[i * rows : (i + 1) * rows]

            @pl.when(s == 0)
            def _():
                out_refs[o][...] = mine + init_refs[o][...] if n_init else mine

            @pl.when(s != 0)
            def _():
                out_refs[o][...] += mine

    at = 0
    for lo, hi, lanes in phases:
        places, blocks, split = [], [], None
        for count, order, flip in lanes:
            places += order
            if count == 2:
                split = a_refs[at], a_refs[at + 1]
            elif flip is None:
                blocks.append((a_refs[at], 0))
            else:
                blocks.append((a_refs[at], 1 - core if flip else core))
            at += count

        if split is None:

            @pl.when((s >= lo) & (s < hi))
            def _():
                add(places, [(ref[0, i], ref[0, 1 - i]) for ref, i in blocks])
        else:
            for here in (0, 1):

                @pl.when((s >= lo) & (s < hi) & (core == here))
                def _():
                    other = split[1][0]
                    if len(places) > 1:
                        turned = [places.index(OFFS.index(FLIP[OFFS[o]])) for o in places]
                        other = jnp.concatenate([other[i * rows : (i + 1) * rows] for i in turned], 0)
                    pair = split[0][0], other
                    add(places, [pair if here == 0 else pair[::-1]])


def product(groups, offs, kept, where, init=()):
    phases, total = [], 0
    for group in groups:
        steps = len(group[0][2])
        phases.append((total, total + steps, [(len(arrs), [offs.index(o) for o in order], flip) for arrs, order, _, flip in group]))
        total += steps
    arrs, table = [], []
    where_row = np.zeros(total, np.int32)
    for group, (lo, hi, _) in zip(groups, phases):
        wanted = group[0][2]
        for item in group:
            for i, arr in enumerate(item[0]):
                stored = item[2] if i == 0 else tuple(FLIP[o] for o in item[2])
                places = [stored.index(o) for o in wanted]
                row = np.zeros(total, np.int32)
                row[:lo], row[lo:hi], row[hi:] = places[0], places, places[-1]
                arrs.append(arr)
                table.append(row)
        where_row[lo:hi] = [OFFS.index(o) for o in wanted]
    table = np.stack(table + [where_row])
    rows, depth = arrs[0].shape[-2] // len(groups[0][0][1]), arrs[0].shape[-1]
    width, nf = kept.shape[1], len(offs)
    a_specs = [
        pl.BlockSpec((1,) + arr.shape[1:], lambda s, t, w, i=i, nd=arr.ndim: (t[i, s],) + (0,) * (nd - 1))
        for i, arr in enumerate(arrs)
    ]
    flat = pl.BlockSpec((rows, width), lambda s, t, w: (0, 0))
    return pl.pallas_call(
        functools.partial(product_kernel, phases, len(init), nf),
        grid_spec=pltpu.PrefetchScalarGridSpec(
            num_scalar_prefetch=2,
            grid=(total,),
            in_specs=a_specs
            + [pl.BlockSpec((2 * depth, width), lambda s, t, w: (w[t[len(arrs), s]], 0))]
            + [flat] * len(init),
            out_specs=[flat] * nf,
        ),
        out_shape=[jax.ShapeDtypeStruct((rows, width), jnp.float32)] * nf,
        compiler_params=pltpu.CompilerParams(vmem_limit_bytes=VMEM_BYTES),
        cost_estimate=pl.CostEstimate(
            flops=rows * nf * depth * width * total // 4,
            bytes_accessed=total * depth * (nf * rows + width) // 4,
            transcendentals=0,
        ),
    )(jnp.asarray(table), where, *arrs, kept, *init)


VMEM_BYTES = 16 << 20


M_ROWS = 256


def product_plane_kernel(ys, planes_ref, kept_ref, *refs):
    out_refs, (a_buf, b_buf, a_sem, b_sem) = refs[: len(ys)], refs[len(ys) :]
    rows, depth = a_buf.shape[-2:]

    def copies(step):
        kept = pltpu.make_async_copy(kept_ref.at[pl.ds(step * 2 * depth, 2 * depth)], b_buf.at[step], b_sem.at[step])
        return [kept] + [
            pltpu.make_async_copy(planes_ref.at[y, pl.ds(2 * step, 2)], a_buf.at[step, i], a_sem.at[step, i])
            for i, y in enumerate(ys)
        ]

    for step in range(N):
        for copy in copies(step):
            copy.start()
    for step in range(N):
        for copy in copies(step):
            copy.wait()
        for i, out_ref in enumerate(out_refs):
            for m in range(0, rows, M_ROWS):
                here = slice(m, min(m + M_ROWS, rows))
                a = jnp.concatenate([a_buf[step, i, 0, here], a_buf[step, i, 1, here]], -1)
                part = jnp.dot(a, b_buf[step], preferred_element_type=jnp.float32)
                out_ref[here] = part if step == 0 else out_ref[here] + part


def product_plane(planes, ys, kept):
    _, _, rows, depth = planes.shape
    width = kept.shape[1]
    return pl.pallas_call(
        functools.partial(product_plane_kernel, ys),
        in_specs=[pl.BlockSpec(memory_space=pltpu.HBM)] * 2,
        out_specs=[pl.BlockSpec(memory_space=pltpu.VMEM)] * len(ys),
        out_shape=[jax.ShapeDtypeStruct((rows, width), jnp.float32)] * len(ys),
        scratch_shapes=[
            pltpu.VMEM((N, len(ys), 2, rows, depth), planes.dtype),
            pltpu.VMEM((N, 2 * depth, width), kept.dtype),
            pltpu.SemaphoreType.DMA((N, len(ys))),
            pltpu.SemaphoreType.DMA((N,)),
        ],
        compiler_params=pltpu.CompilerParams(vmem_limit_bytes=30 << 20),
        cost_estimate=pl.CostEstimate(
            flops=4 * N * len(ys) * rows * depth * width,
            bytes_accessed=4 * N * depth * (len(ys) * rows + width) + 4 * len(ys) * rows * width,
            transcendentals=0,
        ),
    )(planes, kept)


def to_owner(part, off):
    step = lambda c: off * side(c) if abs(off) == 1 else off
    return permute(part.astype(SENT), lambda z, y, x, c: (z + y + step(c), y, x, c))


S_ROWS, A_ROWS, B_ROWS = 384, 64, 64


def on_device(amps, ints, amp_mask, int_mask, vir_energy, pair_energy):
    rows, depth = amps.shape
    split = (S_ROWS, A_ROWS, B_ROWS)
    screened = pl.pallas_call(
        screen_amps,
        in_specs=[pl.BlockSpec(memory_space=pltpu.SMEM), pl.BlockSpec(memory_space=pltpu.VMEM)],
        out_specs=[pl.BlockSpec(memory_space=pltpu.VMEM)] * len(split),
        out_shape=[jax.ShapeDtypeStruct((1, r, depth), amps.dtype) for r in split],
    )(amp_mask, amps)
    s_part, a_part, b_part = [permute(part, lambda z, y, x, c: (y, z - y, x, c)) for part in screened]
    width = ints.shape[1]
    kept = pl.pallas_call(
        screen_ints,
        grid_spec=pltpu.PrefetchScalarGridSpec(
            num_scalar_prefetch=1,
            grid=(ints.shape[0] // depth,),
            in_specs=[pl.BlockSpec((depth, width), lambda s, m: (s, 0))],
            out_specs=pl.BlockSpec((depth, width), lambda s, m: (s, 0)),
        ),
        out_shape=jax.ShapeDtypeStruct(ints.shape, ints.dtype),
        compiler_params=pltpu.CompilerParams(vmem_limit_bytes=VMEM_BYTES),
    )(int_mask, ints)
    virt = lax.axis_index("virt")
    core, x = virt % 2, (virt // 2) % N
    d = 2 * core - 1
    where = jnp.stack([(x + o * (d if abs(o) == 1 else 1)) % N for o in OFFS] + [core]).astype(jnp.int32)

    a_pair, b_pair = swap(a_part), swap(b_part)
    s_part, a_pair, b_pair = lax.optimization_barrier((s_part, a_pair, b_pair))
    planes = lax.all_gather(s_part[0], "virt", axis=0).reshape(N, 2 * N, S_ROWS, depth)
    round_a, round_b = first_round(a_part, a_pair, "x"), first_round(b_part, b_pair, "y")
    a_own = ((jnp.concatenate([round_a[o, k] for o in OFFS for k in (0, 1)], 0).reshape(N, 2, A_ROWS, depth),), (0,), OFFS, False)
    b_own = (
        (jnp.concatenate([round_b[o, k] for k in (0, 1) for o in OFFS], 0).reshape(1, 2, N * B_ROWS, depth),),
        OFFS,
        (0,),
        False,
    )
    a_near, b_near = ((shift(a_own[0][0], "y"),), (1,), OFFS, False), ((shift(b_own[0][0], "x"),), OFFS, (1,), False)
    a_next, b_next = a_near[0][0][:, 0], b_near[0][0][:, 0]
    a_next, b_next, kept = lax.optimization_barrier((a_next, b_next, kept))
    a_far, b_far = shift(a_next, "y"), shift(b_next, "x")
    a_side, b_side = swapped(a_near), swapped(b_near)

    b_early = product([[b_own], [b_near], [b_side]], OFFS, kept, where)
    a_early = product([[a_own, a_near, a_side]], OFFS[:3], kept, where)
    a_far, b_far = lax.optimization_barrier((a_far, b_far, b_early, a_early))[:2]
    a_other, b_other = swap(a_far), swap(b_far)
    b_done = product([[((b_far, b_other), OFFS, (2,), False)]], OFFS, kept, where, b_early)
    a_last = product([[((a_far, a_other), (2,), OFFS, False)]], (2,), kept, where)
    p_got = [
        to_owner(jnp.concatenate([a, b], 0), o) for a, b, o in zip([*a_early, *a_last], b_done, OFFS)
    ]
    planes, *p_got = lax.optimization_barrier((planes, *p_got))
    turn = lambda part, i: permute(part.astype(SENT), lambda z, y, x, c: (z + i, y, x, c))
    mid = S_ROWS // 2
    (across,) = product_plane(planes, (2,), kept)
    low, high = turn(across[:mid], 1), turn(across[mid:], 3)
    up, down = product_plane(planes, (1, 3), kept)
    up = jnp.concatenate([up[:mid] + low.astype(jnp.float32), up[mid:]], 0).astype(SENT)
    down = jnp.concatenate([down[:mid], down[mid:] + high.astype(jnp.float32)], 0).astype(SENT)
    planes, up, down = lax.optimization_barrier((planes, up, down))
    up, down = turn(up, 1), turn(down, 3)
    (here,) = product_plane(planes, (0,), kept)
    s_got = [here, up, down]

    total = lambda got: sum(g.astype(jnp.float32) for g in got)
    contracted = jnp.concatenate([total(s_got), total(p_got)], 0)
    denom = vir_energy[None, :] - pair_energy[:, None]
    return amps.astype(jnp.float32) + contracted / denom


def solution(mesh):
    return jax.shard_map(
        on_device,
        mesh=mesh,
        in_specs=(
            P("pair", "virt"),
            P("pair", "virt"),
            P("pair", "virt"),
            P("pair", "virt"),
            P("virt"),
            P("pair"),
        ),
        out_specs=P("pair", "virt"),
        check_vma=False,
    )
```

time: 471 us -> 171 us (0.36)
  waiting for transfers between devices: 405 us -> 29.7 us
  starting transfers between devices: 0.04 us -> 62.7 us
  Pallas kernels: 0 us -> 39.3 us
  matrix products: 27.8 us -> 0 us
  other arithmetic: 10.1 us -> 2.65 us
  local copies, waits for them, and re-layouts: 14.4 us -> 21.4 us
    all_gather x2 -> x1, waiting for transfers between devices: 405 us -> 5.45 us  [on_device(): lax.all_gather(s_part[0], 'virt', axis=0).reshape(N, 2 * N, S_ROWS, depth)]
    ppermute x0 -> x29, starting transfers between devices: none -> 62.7 us  [permute(): return lax.ppermute(arr, AXES, pairs)]
    pallas_call x0 -> x9, Pallas kernels: none -> 39.3 us  [the longest x3 21.7 us: product_plane(): pl.pallas_call(functools.partial(product_plane_kernel, ys), in_specs=[pl....]
    dot_general x1 -> x0, matrix products: 27.8 us -> none  [on_device(): jnp.dot(all_cols, lax.all_gather(kept, 'pair', axis=0, tiled=True), prefe...]
    ppermute x0 -> x29, waiting for transfers between devices: none -> 24.2 us  [permute(): return lax.ppermute(arr, AXES, pairs)]
    mul x2 -> x0, other arithmetic: 9.39 us -> none  [the longest x1 8.45 us: on_device(): kept = ints * widen(int_mask)]
    unnamed x14 -> x39, local copies, waits for them, and re-layouts: 14.3 us -> 16.2 us
  transfers between devices with their start and end apart: 2 -> 30, of which waited for: 2 -> 13; matrix products, arithmetic and copies ran while one was open for 5% -> 3% of each run, Pallas kernels for 0% -> 18%
where the time goes in v2:
time: 171 us; the launch traced here: 170 us
  starting transfers between devices  62.7 us (37%)
  Pallas kernels  39.3 us (23%)
  waiting for transfers between devices  29.7 us (17%)
  local copies, waits for them, and re-layouts  21.4 us (13%)
  between operations  14 us (8%)
  other arithmetic  2.65 us (2%)
    ppermute x29, starting transfers between devices, permute(): return lax.ppermute(arr, AXES, pairs)  62.7 us
    ppermute x29, waiting for transfers between devices, permute(): return lax.ppermute(arr, AXES, pairs)  24.2 us
    pallas_call x3, Pallas kernels, product_plane(): pl.pallas_call(functools.partial(product_plane_kernel, ys), in_specs=[pl....  21.7 us
    unnamed x39, local copies, waits for them, and re-layouts  16.2 us
    pallas_call x4, Pallas kernels, product(): pl.pallas_call(functools.partial(product_kernel, phases, len(init), nf),...  12.2 us
    all_gather x1, waiting for transfers between devices, on_device(): lax.all_gather(s_part[0], 'virt', axis=0).reshape(N, 2 * N, S_ROWS, depth)  5.45 us
  transfers between devices with their start and end apart: 30, of which 13 were waited for; matrix products, arithmetic and copies ran while one was open for 3% of the time, Pallas kernels for 18%

profile of v2, /device:TPU:1, one launch (start us, length us, event | category | flops | bytes accessed | tf_op | source)
XLA Modules:
  0.0 169.8 jit_solution(17192890439539326107)
XLA Ops:
  6.5 2.2 %shard_map.100 = (bf16[1,384,768]{2,1,0:T(8,128)(2,1)}, bf16[1,64,768]{2,1,0:T(8,128)(2,1)}, bf16[1,64,768]{2,1,0:T(8,128)(2,1)}) custom-call(s32[4,6]{1,0:T(4,128)} %mask_ref.2, bf16[512,768]{1,0:T(8,128)(2,1)} %amps_ref.1), custom_call_target="tpu_custom_call" | custom-call | tf_op jit(solution)/shard_map/pallas_call | solution.py:267
  8.7 1.7 %collective-permute-start = (bf16[1,384,768]{2,1,0:T(8,128)(2,1)}, bf16[1,384,768]{2,1,0:T(8,128)(2,1)S(1)}, u32[]{:S(2)}, u32[]{:S(2)}) collective-permute-start(bf16[1,384,768]{2,1,0:T(8,128)(2,1)} %get-tuple-element.37), channel_id=1, source_target_pairs={{0,0},{1,1},{2,2},{3,3},{4,4},{5,5},{6,6},{7,7},{8,56},{9,57},{10,... | collective-permute-start | bytes 1769480 | tf_op jit(solution)/shard_map/ppermute | solution.py:30
  10.4 1.5 collective-permute-start.1
  12.0 1.5 collective-permute-start.3
  17.1 22.4 %collective-permute-start.11 = (bf16[2,64,768]{2,1,0:T(8,128)(2,1)S(1)}, bf16[2,64,768]{2,1,0:T(8,128)(2,1)S(1)}, u32[]{:S(2)}, u32[]{:S(2)}) collective-permute-start(bf16[2,64,768]{2,1,0:T(8,128)(2,1)S(1)} %pad_maximum_fusion.3), channel_id=1, source_target_pairs={{0,8},{1,25},{2,10},{3,27},{4,12},{5,29},{6,14},{7,31},{8,16},{9,1... | collective-permute-start | bytes 589832 | tf_op jit(solution)/shard_map/ppermute | solution.py:30
  39.6 2.5 %collective-permute-start.5 = (bf16[2,64,768]{2,1,0:T(8,128)(2,1)S(1)}, bf16[2,64,768]{2,1,0:T(8,128)(2,1)S(1)}, u32[]{:S(2)}, u32[]{:S(2)}) collective-permute-start(bf16[2,64,768]{2,1,0:T(8,128)(2,1)S(1)} %pad_maximum_fusion.2), channel_id=1, source_target_pairs={{0,2},{1,7},{2,4},{3,1},{4,6},{5,3},{6,0},{7,5},{8,10},{9,15},{10,... | collective-permute-start | bytes 589832 | tf_op jit(solution)/shard_map/ppermute | solution.py:30
  42.2 2.6 %collective-permute-done.5 = bf16[2,64,768]{2,1,0:T(8,128)(2,1)S(1)} collective-permute-done((bf16[2,64,768]{2,1,0:T(8,128)(2,1)S(1)}, bf16[2,64,768]{2,1,0:T(8,128)(2,1)S(1)}, u32[]{:S(2)}, u32[]{:S(2)}) %collective-permute-start.5) | collective-permute-done | bytes 196640 | tf_op jit(solution)/shard_map/ppermute | solution.py:30
  44.8 2.2 %collective-permute-start.13 = (bf16[1,64,768]{2,1,0:T(8,128)(2,1)S(1)}, bf16[1,64,768]{2,1,0:T(8,128)(2,1)S(1)}, u32[]{:S(2)}, u32[]{:S(2)}) collective-permute-start(bf16[1,64,768]{2,1,0:T(8,128)(2,1)S(1)} %get-tuple-element.75), channel_id=1, source_target_pairs={{0,8},{1,25},{2,10},{3,27},{4,12},{5,29},{6,14},{7,31},{8,16},{9,1... | collective-permute-start | bytes 294920 | tf_op jit(solution)/shard_map/ppermute | solution.py:30
  47.0 2.1 %collective-permute-start.7 = (bf16[1,64,768]{2,1,0:T(8,128)(2,1)S(1)}, bf16[1,64,768]{2,1,0:T(8,128)(2,1)S(1)}, u32[]{:S(2)}, u32[]{:S(2)}) collective-permute-start(bf16[1,64,768]{2,1,0:T(8,128)(2,1)S(1)} %slice.70), channel_id=1, source_target_pairs={{0,2},{1,7},{2,4},{3,1},{4,6},{5,3},{6,0},{7,5},{8,10},{9,15},{10,... | collective-permute-start | bytes 294920 | tf_op jit(solution)/shard_map/ppermute | solution.py:30
  52.6 3.2 %collective-permute-start.8 = (bf16[1,64,768]{2,1,0:T(8,128)(2,1)S(1)}, bf16[1,64,768]{2,1,0:T(8,128)(2,1)S(1)}, u32[]{:S(2)}, u32[]{:S(2)}) collective-permute-start(bf16[1,64,768]{2,1,0:T(8,128)(2,1)S(1)} %collective-permute-done.7), channel_id=1, source_target_pairs={{0,1},{1,0},{2,3},{3,2},{4,5},{5,4},{6,7},{7,6},{8,9},{9,8},{10,11... | collective-permute-start | bytes 294920 | tf_op jit(solution)/shard_map/ppermute | solution.py:30
  58.4 3.8 %copy-done.3 = bf16[6144,768]{1,0:T(8,128)(2,1)S(1)} copy-done((bf16[6144,768]{1,0:T(8,128)(2,1)S(1)}, bf16[6144,768]{1,0:T(8,128)(2,1)}, u32[]{:S(2)}) %copy-start.3) | copy-done | bytes 9437208
  62.2 3.2 %shard_map.101.refs_3_.refs_2_.kept_ref = bf16[6144,768]{1,0:T(8,128)(2,1)S(1)} custom-call(s32[48,6]{1,0:T(8,128)S(1)} %copy.20.mask_ref, bf16[6144,768]{1,0:T(8,128)(2,1)S(1)} %copy-done.3), custom_call_target="tpu_custom_call" | custom-call | tf_op jit(solution)/shard_map/pallas_call | solution.py:275
  65.4 3.6 %copy-done = bf16[6144,768]{1,0:T(8,128)(2,1)} copy-done((bf16[6144,768]{1,0:T(8,128)(2,1)}, bf16[6144,768]{1,0:T(8,128)(2,1)S(1)}, u32[]{:S(2)}) %copy-start) | copy-done | bytes 9437208
  69.0 2.4 %collective-permute-done.9 = bf16[4,2,64,768]{3,2,0,1:T(8,128)(2,1)} collective-permute-done((bf16[4,2,64,768]{3,2,0,1:T(8,128)(2,1)S(1)}, bf16[4,2,64,768]{3,2,0,1:T(8,128)(2,1)}, u32[]{:S(2)}, u32[]{:S(2)}) %collective-permute-start.9) | collective-permute-done | bytes 786464 | tf_op jit(solution)/shard_map/ppermute | solution.py:30
  73.7 1.8 %slice_bitcast_fusion.1 = bf16[4,64,768]{2,1,0:T(8,128)(2,1)} fusion(bf16[4,2,64,768]{3,2,0,1:T(8,128)(2,1)} %collective-permute-done.9), kind=kLoop, calls=%fused_computation.10 | loop fusion | bytes 786432 | tf_op jit(solution)/shard_map/squeeze | solution.py:303
  80.4 4.1 %copy-done.1 = bf16[6144,768]{1,0:T(8,128)(2,1)S(1)} copy-done((bf16[6144,768]{1,0:T(8,128)(2,1)S(1)}, bf16[6144,768]{1,0:T(8,128)(2,1)}, u32[]{:S(2)}) %copy-start.1) | copy-done | bytes 9437208
  84.5 3.4 %shard_map.102 = (f32[64,768]{1,0:T(8,128)S(1)}, f32[64,768]{1,0:T(8,128)S(1)}, f32[64,768]{1,0:T(8,128)S(1)}) custom-call(s32[4,4]{1,0:T(4,128)S(1)} %copy-done.7, s32[5]{0:T(128)S(1)} %stack.23.where_ref, bf16[4,2,64,768]{3,2,1,0:T(8,128)(2,1)S(1)} %bitcast.13, bf16[4,2,64,768]{3,2,1,0:T(8,128)(2,1)S(1)} %copy.21.refs_1_, ...), custom_call_target="tpu_custom_call" | custom-call | flops 113246208 | bytes 737280 | tf_op jit(solution)/shard_map/pallas_call | solution.py:182
  88.0 3.3 %shard_map.103 = (f32[64,768]{1,0:T(8,128)S(1)}, f32[64,768]{1,0:T(8,128)S(1)}, f32[64,768]{1,0:T(8,128)S(1)}, f32[64,768]{1,0:T(8,128)S(1)}) custom-call(s32[4,3]{1,0:T(4,128)S(1)} %copy-done.6, s32[5]{0:T(128)S(1)} %stack.23.where_ref, bf16[1,2,256,768]{3,2,1,0:T(8,128)(2,1)S(1)} %bitcast.15, bf16[1,2,256,768]{3,2,1,0:T(8,128)(2,1)S(1)} %collective-permute-done.15.refs_1_, ...), custom_call_target="tpu_custom_call" | custom-call | flops 113246208 | bytes 589824 | tf_op jit(solution)/shard_map/pallas_call | solution.py:182
  93.8 2.0 %collective-permute-done.23.refs_1_ = bf16[4,64,768]{2,1,0:T(8,128)(2,1)S(1)} collective-permute-done((bf16[4,64,768]{2,1,0:T(8,128)(2,1)}, bf16[4,64,768]{2,1,0:T(8,128)(2,1)S(1)}, u32[]{:S(2)}, u32[]{:S(2)}) %collective-permute-start.23) | collective-permute-done | bytes 393248 | tf_op jit(solution)/shard_map/ppermute | solution.py:30
  95.8 4.1 %shard_map.105 = f32[64,768]{1,0:T(8,128)S(1)} custom-call(s32[3,4]{1,0:T(4,128)S(1)} %copy-done.5, s32[5]{0:T(128)S(1)} %stack.23.where_ref, bf16[4,64,768]{2,1,0:T(8,128)(2,1)} %collective-permute-done.16.refs_0_, bf16[4,64,768]{2,1,0:T(8,128)(2,1)S(1)} %collective-permute-done.23.refs_1_, bf16[6144,768]{1,0:T(8,128)(2,1)S(1)} %copy-done.1), custom_call_target="tpu_custom_call" | custom-call | flops 37748736 | bytes 638976 | tf_op jit(solution)/shard_map/pallas_call | solution.py:182
  101.4 4.5 %collective-permute-start.24 = (f16[128,768]{1,0:T(8,128)(2,1)S(1)}, f16[128,768]{1,0:T(8,128)(2,1)S(1)}, u32[]{:S(2)}, u32[]{:S(2)}) collective-permute-start(f16[128,768]{1,0:T(8,128)(2,1)S(1)} %pad_maximum_fusion.7), channel_id=1, source_target_pairs={{0,64},{1,65},{2,66},{3,67},{4,68},{5,69},{6,70},{7,71},{8,104},{9... | collective-permute-start | bytes 589832 | tf_op jit(solution)/shard_map/ppermute | solution.py:30
  106.0 2.9 %collective-permute-start.22 = (f16[128,768]{1,0:T(8,128)(2,1)S(1)}, f16[128,768]{1,0:T(8,128)(2,1)S(1)}, u32[]{:S(2)}, u32[]{:S(2)}) collective-permute-start(f16[128,768]{1,0:T(8,128)(2,1)S(1)} %pad_maximum_fusion.6), channel_id=1, source_target_pairs={{0,32},{1,97},{2,34},{3,99},{4,36},{5,101},{6,38},{7,103},{8,72},{... | collective-permute-start | bytes 589832 | tf_op jit(solution)/shard_map/ppermute | solution.py:30
  108.9 2.5 %collective-permute-start.21 = (f16[128,768]{1,0:T(8,128)(2,1)S(1)}, f16[128,768]{1,0:T(8,128)(2,1)S(1)}, u32[]{:S(2)}, u32[]{:S(2)}) collective-permute-start(f16[128,768]{1,0:T(8,128)(2,1)S(1)} %pad_maximum_fusion.5), channel_id=1, source_target_pairs={{0,96},{1,33},{2,98},{3,35},{4,100},{5,37},{6,102},{7,39},{8,8},{9... | collective-permute-start | bytes 589832 | tf_op jit(solution)/shard_map/ppermute | solution.py:30
  112.2 2.7 %collective-permute-done.22 = f16[128,768]{1,0:T(8,128)(2,1)S(1)} collective-permute-done((f16[128,768]{1,0:T(8,128)(2,1)S(1)}, f16[128,768]{1,0:T(8,128)(2,1)S(1)}, u32[]{:S(2)}, u32[]{:S(2)}) %collective-permute-start.22) | collective-permute-done | bytes 196640 | tf_op jit(solution)/shard_map/ppermute | solution.py:30
  114.9 2.4 %collective-permute-done.21 = f16[128,768]{1,0:T(8,128)(2,1)S(1)} collective-permute-done((f16[128,768]{1,0:T(8,128)(2,1)S(1)}, f16[128,768]{1,0:T(8,128)(2,1)S(1)}, u32[]{:S(2)}, u32[]{:S(2)}) %collective-permute-start.21) | collective-permute-done | bytes 196640 | tf_op jit(solution)/shard_map/ppermute | solution.py:30
  117.3 5.4 %all-gather.2.cloned.1.call-done = bf16[32,384,768]{2,1,0:T(8,128)(2,1)} async-done(((bf16[1,384,768]{2,1,0:T(8,128)(2,1)}), bf16[32,384,768]{2,1,0:T(8,128)(2,1)}) %all-gather.2.cloned.1.call-update) | async-done | bytes 18874384 | tf_op jit(solution)/shard_map/all_gather | solution.py:293
  122.7 3.7 %copy-done.2 = bf16[6144,768]{1,0:T(8,128)(2,1)S(1)} copy-done((bf16[6144,768]{1,0:T(8,128)(2,1)S(1)}, bf16[6144,768]{1,0:T(8,128)(2,1)}, u32[]{:S(2)}) %copy-start.2) | copy-done | bytes 9437208
  126.4 6.0 %shard_map.107 = f32[384,768]{1,0:T(8,128)S(1)} custom-call(bf16[4,8,384,768]{3,2,1,0:T(8,128)(2,1)} %bitcast.16, bf16[6144,768]{1,0:T(8,128)(2,1)S(1)} %copy-done.2), custom_call_target="tpu_custom_call" | custom-call | flops 3623878656 | bytes 15335424 | tf_op jit(solution)/shard_map/pallas_call | solution.py:236
  135.4 9.6 %shard_map.106 = (f32[384,768]{1,0:T(8,128)S(1)}, f32[384,768]{1,0:T(8,128)S(1)}) custom-call(bf16[4,8,384,768]{3,2,1,0:T(8,128)(2,1)} %bitcast.17, bf16[6144,768]{1,0:T(8,128)(2,1)S(1)} %copy-done.2), custom_call_target="tpu_custom_call" | custom-call | flops 7247757312 | bytes 21233664 | tf_op jit(solution)/shard_map/pallas_call | solution.py:236
  145.9 2.7 %collective-permute-start.28 = (f16[384,768]{1,0:T(8,128)(2,1)S(1)}, f16[384,768]{1,0:T(8,128)(2,1)S(1)}, u32[]{:S(2)}, u32[]{:S(2)}) collective-permute-start(f16[384,768]{1,0:T(8,128)(2,1)S(1)} %pad_maximum_fusion.1), channel_id=1, source_target_pairs={{0,96},{1,97},{2,98},{3,99},{4,100},{5,101},{6,102},{7,103},{8,104... | collective-permute-start | bytes 1769480 | tf_op jit(solution)/shard_map/ppermute | solution.py:30
  148.7 6.0 %shard_map.108 = f32[384,768]{1,0:T(8,128)S(1)} custom-call(bf16[4,8,384,768]{3,2,1,0:T(8,128)(2,1)} %bitcast.18, bf16[6144,768]{1,0:T(8,128)(2,1)S(1)} %copy-done.2), custom_call_target="tpu_custom_call" | custom-call | flops 3623878656 | bytes 15335424 | tf_op jit(solution)/shard_map/pallas_call | solution.py:236
  154.8 6.5 %collective-permute-done.27 = f16[384,768]{1,0:T(8,128)(2,1)S(1)} collective-permute-done((f16[384,768]{1,0:T(8,128)(2,1)S(1)}, f16[384,768]{1,0:T(8,128)(2,1)S(1)}, u32[]{:S(2)}, u32[]{:S(2)}) %collective-permute-start.27) | collective-permute-done | bytes 589856 | tf_op jit(solution)/shard_map/ppermute | solution.py:30
  (109 shorter events, 27.2 us)
Async XLA Ops:
  6.5 116.2 %all-gather.2.cloned.1.call-start = ((), (), s32[]{:S(2)}) async-start(), calls=%async_computation | async-start | bytes 19464192 | tf_op jit(solution)/shard_map/all_gather | solution.py:293
  8.7 7.5 %collective-permute-start = (bf16[1,384,768]{2,1,0:T(8,128)(2,1)}, bf16[1,384,768]{2,1,0:T(8,128)(2,1)S(1)}, u32[]{:S(2)}, u32[]{:S(2)}) collective-permute-start(bf16[1,384,768]{2,1,0:T(8,128)(2,1)} %get-tuple-element.37), channel_id=1, source_target_pairs={{0,0},{1,1},{2,2},{3,3},{4,4},{5,5},{6,6},{7,7},{8,56},{9,57},{10,... | collective-permute-start | bytes 1769480 | tf_op jit(solution)/shard_map/ppermute | solution.py:30
  10.4 3.1 %collective-permute-start.1 = (bf16[1,64,768]{2,1,0:T(8,128)(2,1)}, bf16[1,64,768]{2,1,0:T(8,128)(2,1)S(1)}, u32[]{:S(2)}, u32[]{:S(2)}) collective-permute-start(bf16[1,64,768]{2,1,0:T(8,128)(2,1)} %get-tuple-element.38), channel_id=1, source_target_pairs={{0,0},{1,1},{2,2},{3,3},{4,4},{5,5},{6,6},{7,7},{8,56},{9,57},{10,... | collective-permute-start | bytes 294920 | tf_op jit(solution)/shard_map/ppermute | solution.py:30
  12.0 3.0 %collective-permute-start.3 = (bf16[1,64,768]{2,1,0:T(8,128)(2,1)}, bf16[1,64,768]{2,1,0:T(8,128)(2,1)S(1)}, u32[]{:S(2)}, u32[]{:S(2)}) collective-permute-start(bf16[1,64,768]{2,1,0:T(8,128)(2,1)} %get-tuple-element.39), channel_id=1, source_target_pairs={{0,0},{1,1},{2,2},{3,3},{4,4},{5,5},{6,6},{7,7},{8,56},{9,57},{10,... | collective-permute-start | bytes 294920 | tf_op jit(solution)/shard_map/ppermute | solution.py:30
  13.5 2.4 %collective-permute-start.2 = (bf16[1,64,768]{2,1,0:T(8,128)(2,1)S(1)}, bf16[1,64,768]{2,1,0:T(8,128)(2,1)S(1)}, u32[]{:S(2)}, u32[]{:S(2)}) collective-permute-start(bf16[1,64,768]{2,1,0:T(8,128)(2,1)S(1)} %collective-permute-done.1), channel_id=1, source_target_pairs={{0,1},{1,0},{2,3},{3,2},{4,5},{5,4},{6,7},{7,6},{8,9},{9,8},{10,11... | collective-permute-start | bytes 294920 | tf_op jit(solution)/shard_map/ppermute | solution.py:30
  15.0 1.3 collective-permute-start.4
  17.1 27.6 %collective-permute-start.11 = (bf16[2,64,768]{2,1,0:T(8,128)(2,1)S(1)}, bf16[2,64,768]{2,1,0:T(8,128)(2,1)S(1)}, u32[]{:S(2)}, u32[]{:S(2)}) collective-permute-start(bf16[2,64,768]{2,1,0:T(8,128)(2,1)S(1)} %pad_maximum_fusion.3), channel_id=1, source_target_pairs={{0,8},{1,25},{2,10},{3,27},{4,12},{5,29},{6,14},{7,31},{8,16},{9,1... | collective-permute-start | bytes 589832 | tf_op jit(solution)/shard_map/ppermute | solution.py:30
  39.6 5.2 %collective-permute-start.5 = (bf16[2,64,768]{2,1,0:T(8,128)(2,1)S(1)}, bf16[2,64,768]{2,1,0:T(8,128)(2,1)S(1)}, u32[]{:S(2)}, u32[]{:S(2)}) collective-permute-start(bf16[2,64,768]{2,1,0:T(8,128)(2,1)S(1)} %pad_maximum_fusion.2), channel_id=1, source_target_pairs={{0,2},{1,7},{2,4},{3,1},{4,6},{5,3},{6,0},{7,5},{8,10},{9,15},{10,... | collective-permute-start | bytes 589832 | tf_op jit(solution)/shard_map/ppermute | solution.py:30
  44.8 11.0 %collective-permute-start.6 = (bf16[2,64,768]{2,1,0:T(8,128)(2,1)S(1)}, bf16[2,64,768]{2,1,0:T(8,128)(2,1)S(1)}, u32[]{:S(2)}, u32[]{:S(2)}) collective-permute-start(bf16[2,64,768]{2,1,0:T(8,128)(2,1)S(1)} %collective-permute-done.5), channel_id=1, source_target_pairs={{0,1},{1,0},{2,3},{3,2},{4,5},{5,4},{6,7},{7,6},{8,9},{9,8},{10,11... | collective-permute-start | bytes 589832 | tf_op jit(solution)/shard_map/ppermute | solution.py:30
  44.8 5.2 %collective-permute-start.13 = (bf16[1,64,768]{2,1,0:T(8,128)(2,1)S(1)}, bf16[1,64,768]{2,1,0:T(8,128)(2,1)S(1)}, u32[]{:S(2)}, u32[]{:S(2)}) collective-permute-start(bf16[1,64,768]{2,1,0:T(8,128)(2,1)S(1)} %get-tuple-element.75), channel_id=1, source_target_pairs={{0,8},{1,25},{2,10},{3,27},{4,12},{5,29},{6,14},{7,31},{8,16},{9,1... | collective-permute-start | bytes 294920 | tf_op jit(solution)/shard_map/ppermute | solution.py:30
  47.0 5.5 %collective-permute-start.7 = (bf16[1,64,768]{2,1,0:T(8,128)(2,1)S(1)}, bf16[1,64,768]{2,1,0:T(8,128)(2,1)S(1)}, u32[]{:S(2)}, u32[]{:S(2)}) collective-permute-start(bf16[1,64,768]{2,1,0:T(8,128)(2,1)S(1)} %slice.70), channel_id=1, source_target_pairs={{0,2},{1,7},{2,4},{3,1},{4,6},{5,3},{6,0},{7,5},{8,10},{9,15},{10,... | collective-permute-start | bytes 294920 | tf_op jit(solution)/shard_map/ppermute | solution.py:30
  49.1 7.8 %collective-permute-start.12 = (bf16[2,64,768]{2,1,0:T(8,128)(2,1)S(1)}, bf16[2,64,768]{2,1,0:T(8,128)(2,1)S(1)}, u32[]{:S(2)}, u32[]{:S(2)}) collective-permute-start(bf16[2,64,768]{2,1,0:T(8,128)(2,1)S(1)} %collective-permute-done.11), channel_id=1, source_target_pairs={{0,1},{1,0},{2,3},{3,2},{4,5},{5,4},{6,7},{7,6},{8,9},{9,8},{10,11... | collective-permute-start | bytes 589832 | tf_op jit(solution)/shard_map/ppermute | solution.py:30
  50.0 7.0 %collective-permute-start.14 = (bf16[1,64,768]{2,1,0:T(8,128)(2,1)S(1)}, bf16[1,64,768]{2,1,0:T(8,128)(2,1)S(1)}, u32[]{:S(2)}, u32[]{:S(2)}) collective-permute-start(bf16[1,64,768]{2,1,0:T(8,128)(2,1)S(1)} %collective-permute-done.13), channel_id=1, source_target_pairs={{0,1},{1,0},{2,3},{3,2},{4,5},{5,4},{6,7},{7,6},{8,9},{9,8},{10,11... | collective-permute-start | bytes 294920 | tf_op jit(solution)/shard_map/ppermute | solution.py:30
  52.6 4.2 %collective-permute-start.8 = (bf16[1,64,768]{2,1,0:T(8,128)(2,1)S(1)}, bf16[1,64,768]{2,1,0:T(8,128)(2,1)S(1)}, u32[]{:S(2)}, u32[]{:S(2)}) collective-permute-start(bf16[1,64,768]{2,1,0:T(8,128)(2,1)S(1)} %collective-permute-done.7), channel_id=1, source_target_pairs={{0,1},{1,0},{2,3},{3,2},{4,5},{5,4},{6,7},{7,6},{8,9},{9,8},{10,11... | collective-permute-start | bytes 294920 | tf_op jit(solution)/shard_map/ppermute | solution.py:30
  56.8 14.6 %collective-permute-start.9 = (bf16[4,2,64,768]{3,2,0,1:T(8,128)(2,1)S(1)}, bf16[4,2,64,768]{3,2,0,1:T(8,128)(2,1)}, u32[]{:S(2)}, u32[]{:S(2)}) collective-permute-start(bf16[4,2,64,768]{3,2,0,1:T(8,128)(2,1)S(1)} %copy.19), channel_id=1, source_target_pairs={{0,8},{1,25},{2,10},{3,27},{4,12},{5,29},{6,14},{7,31},{8,16},{9,1... | collective-permute-start | bytes 2359304 | tf_op jit(solution)/shard_map/ppermute | solution.py:30
  57.0 15.9 %collective-permute-start.15 = (bf16[1,2,256,768]{3,2,1,0:T(8,128)(2,1)S(1)}, bf16[1,2,256,768]{3,2,1,0:T(8,128)(2,1)S(1)}, u32[]{:S(2)}, u32[]{:S(2)}) collective-permute-start(bf16[1,2,256,768]{3,2,1,0:T(8,128)(2,1)S(1)} %bitcast.14), channel_id=1, source_target_pairs={{0,2},{1,7},{2,4},{3,1},{4,6},{5,3},{6,0},{7,5},{8,10},{9,15},{10,... | collective-permute-start | bytes 2359304 | tf_op jit(solution)/shard_map/ppermute | solution.py:30
  71.4 7.8 %collective-permute-start.10 = (bf16[4,2,64,768]{3,2,0,1:T(8,128)(2,1)}, bf16[4,2,64,768]{3,2,0,1:T(8,128)(2,1)}, u32[]{:S(2)}, u32[]{:S(2)}) collective-permute-start(bf16[4,2,64,768]{3,2,0,1:T(8,128)(2,1)} %collective-permute-done.9), channel_id=1, source_target_pairs={{0,1},{1,0},{2,3},{3,2},{4,5},{5,4},{6,7},{7,6},{8,9},{9,8},{10,11... | collective-permute-start | bytes 2359304 | tf_op jit(solution)/shard_map/ppermute | solution.py:30
  72.9 15.1 %collective-permute-start.18 = (bf16[1,2,256,768]{3,2,1,0:T(8,128)(2,1)S(1)}, bf16[1,2,256,768]{3,2,1,0:T(8,128)(2,1)S(1)}, u32[]{:S(2)}, u32[]{:S(2)}) collective-permute-start(bf16[1,2,256,768]{3,2,1,0:T(8,128)(2,1)S(1)} %collective-permute-done.15.refs_1_), channel_id=1, source_target_pairs={{0,1},{1,0},{2,3},{3,2},{4,5},{5,4},{6,7},{7,6},{8,9},{9,8},{10,11... | collective-permute-start | bytes 2359304 | tf_op jit(solution)/shard_map/ppermute | solution.py:30
  75.5 15.8 %collective-permute-start.16 = (bf16[4,64,768]{2,1,0:T(8,128)(2,1)}, bf16[4,64,768]{2,1,0:T(8,128)(2,1)}, u32[]{:S(2)}, u32[]{:S(2)}) collective-permute-start(bf16[4,64,768]{2,1,0:T(8,128)(2,1)} %slice_bitcast_fusion.1), channel_id=1, source_target_pairs={{0,8},{1,25},{2,10},{3,27},{4,12},{5,29},{6,14},{7,31},{8,16},{9,1... | collective-permute-start | bytes 1179656 | tf_op jit(solution)/shard_map/ppermute | solution.py:30
  76.9 15.6 %collective-permute-start.17 = (bf16[1,256,768]{2,1,0:T(8,128)(2,1)}, bf16[1,256,768]{2,1,0:T(8,128)(2,1)S(1)}, u32[]{:S(2)}, u32[]{:S(2)}) collective-permute-start(bf16[1,256,768]{2,1,0:T(8,128)(2,1)} %slice_bitcast_fusion), channel_id=1, source_target_pairs={{0,2},{1,7},{2,4},{3,1},{4,6},{5,3},{6,0},{7,5},{8,10},{9,15},{10,... | collective-permute-start | bytes 1179656 | tf_op jit(solution)/shard_map/ppermute | solution.py:30
  88.0 7.8 %copy-start.5 = (s32[3,4]{1,0:T(4,128)S(1)}, s32[3,4]{1,0:T(4,128)}, u32[]{:S(2)}) copy-start(s32[3,4]{1,0:T(4,128)} %constant.68.clone.table_ref) | copy-start | bytes 148
  92.6 3.2 %collective-permute-start.23 = (bf16[4,64,768]{2,1,0:T(8,128)(2,1)}, bf16[4,64,768]{2,1,0:T(8,128)(2,1)S(1)}, u32[]{:S(2)}, u32[]{:S(2)}) collective-permute-start(bf16[4,64,768]{2,1,0:T(8,128)(2,1)} %collective-permute-done.16.refs_0_), channel_id=1, source_target_pairs={{0,1},{1,0},{2,3},{3,2},{4,5},{5,4},{6,7},{7,6},{8,9},{9,8},{10,11... | collective-permute-start | bytes 1179656 | tf_op jit(solution)/shard_map/ppermute | solution.py:30
  93.7 6.2 %collective-permute-start.19 = (bf16[1,256,768]{2,1,0:T(8,128)(2,1)S(1)}, bf16[1,256,768]{2,1,0:T(8,128)(2,1)S(1)}, u32[]{:S(2)}, u32[]{:S(2)}) collective-permute-start(bf16[1,256,768]{2,1,0:T(8,128)(2,1)S(1)} %collective-permute-done.17.refs_0_), channel_id=1, source_target_pairs={{0,1},{1,0},{2,3},{3,2},{4,5},{5,4},{6,7},{7,6},{8,9},{9,8},{10,11... | collective-permute-start | bytes 1179656 | tf_op jit(solution)/shard_map/ppermute | solution.py:30
  101.4 10.8 %collective-permute-start.24 = (f16[128,768]{1,0:T(8,128)(2,1)S(1)}, f16[128,768]{1,0:T(8,128)(2,1)S(1)}, u32[]{:S(2)}, u32[]{:S(2)}) collective-permute-start(f16[128,768]{1,0:T(8,128)(2,1)S(1)} %pad_maximum_fusion.7), channel_id=1, source_target_pairs={{0,64},{1,65},{2,66},{3,67},{4,68},{5,69},{6,70},{7,71},{8,104},{9... | collective-permute-start | bytes 589832 | tf_op jit(solution)/shard_map/ppermute | solution.py:30
  106.0 8.9 %collective-permute-start.22 = (f16[128,768]{1,0:T(8,128)(2,1)S(1)}, f16[128,768]{1,0:T(8,128)(2,1)S(1)}, u32[]{:S(2)}, u32[]{:S(2)}) collective-permute-start(f16[128,768]{1,0:T(8,128)(2,1)S(1)} %pad_maximum_fusion.6), channel_id=1, source_target_pairs={{0,32},{1,97},{2,34},{3,99},{4,36},{5,101},{6,38},{7,103},{8,72},{... | collective-permute-start | bytes 589832 | tf_op jit(solution)/shard_map/ppermute | solution.py:30
  108.9 8.3 %collective-permute-start.21 = (f16[128,768]{1,0:T(8,128)(2,1)S(1)}, f16[128,768]{1,0:T(8,128)(2,1)S(1)}, u32[]{:S(2)}, u32[]{:S(2)}) collective-permute-start(f16[128,768]{1,0:T(8,128)(2,1)S(1)} %pad_maximum_fusion.5), channel_id=1, source_target_pairs={{0,96},{1,33},{2,98},{3,35},{4,100},{5,37},{6,102},{7,39},{8,8},{9... | collective-permute-start | bytes 589832 | tf_op jit(solution)/shard_map/ppermute | solution.py:30
  111.5 5.8 %collective-permute-start.20 = (f16[128,768]{1,0:T(8,128)(2,1)S(1)}, f16[128,768]{1,0:T(8,128)(2,1)S(1)}, u32[]{:S(2)}, u32[]{:S(2)}) collective-permute-start(f16[128,768]{1,0:T(8,128)(2,1)S(1)} %pad_maximum_fusion.4), channel_id=1, source_target_pairs={{0,0},{1,1},{2,2},{3,3},{4,4},{5,5},{6,6},{7,7},{8,40},{9,41},{10,... | collective-permute-start | bytes 589832 | tf_op jit(solution)/shard_map/ppermute | solution.py:30
  132.6 12.5 %collective-permute-start.25 = (f16[192,768]{1,0:T(8,128)(2,1)S(1)}, f16[192,768]{1,0:T(8,128)(2,1)S(1)}, u32[]{:S(2)}, u32[]{:S(2)}) collective-permute-start(f16[192,768]{1,0:T(8,128)(2,1)S(1)} %get-tuple-element.74), channel_id=1, source_target_pairs={{0,32},{1,33},{2,34},{3,35},{4,36},{5,37},{6,38},{7,39},{8,40},{9,... | collective-permute-start | bytes 884744 | tf_op jit(solution)/shard_map/ppermute | solution.py:30
  134.0 11.1 %collective-permute-start.26 = (f16[192,768]{1,0:T(8,128)(2,1)S(1)}, f16[192,768]{1,0:T(8,128)(2,1)S(1)}, u32[]{:S(2)}, u32[]{:S(2)}) collective-permute-start(f16[192,768]{1,0:T(8,128)(2,1)S(1)} %get-tuple-element.73), channel_id=1, source_target_pairs={{0,96},{1,97},{2,98},{3,99},{4,100},{5,101},{6,102},{7,103},{8,104... | collective-permute-start | bytes 884744 | tf_op jit(solution)/shard_map/ppermute | solution.py:30
  145.6 15.6 %collective-permute-start.27 = (f16[384,768]{1,0:T(8,128)(2,1)S(1)}, f16[384,768]{1,0:T(8,128)(2,1)S(1)}, u32[]{:S(2)}, u32[]{:S(2)}) collective-permute-start(f16[384,768]{1,0:T(8,128)(2,1)S(1)} %pad_maximum_fusion), channel_id=1, source_target_pairs={{0,32},{1,33},{2,34},{3,35},{4,36},{5,37},{6,38},{7,39},{8,40},{9,... | collective-permute-start | bytes 1769480 | tf_op jit(solution)/shard_map/ppermute | solution.py:30
  145.9 15.3 %collective-permute-start.28 = (f16[384,768]{1,0:T(8,128)(2,1)S(1)}, f16[384,768]{1,0:T(8,128)(2,1)S(1)}, u32[]{:S(2)}, u32[]{:S(2)}) collective-permute-start(f16[384,768]{1,0:T(8,128)(2,1)S(1)} %pad_maximum_fusion.1), channel_id=1, source_target_pairs={{0,96},{1,97},{2,98},{3,99},{4,100},{5,101},{6,102},{7,103},{8,104... | collective-permute-start | bytes 1769480 | tf_op jit(solution)/shard_map/ppermute | solution.py:30
  154.7 6.7 %copy-start.8 = (bf16[512,768]{1,0:T(8,128)(2,1)S(1)}, bf16[512,768]{1,0:T(8,128)(2,1)}, u32[]{:S(2)}) copy-start(bf16[512,768]{1,0:T(8,128)(2,1)} %amps_ref.1) | copy-start | bytes 2359300
  (11 other events, 43.9 us)
Sparse Core Ops, SparseCore 0:
  17.2 105.4 all-gather.1

commit v3 on v2

--- a/solution.py
+++ b/solution.py
@@ -72,9 +72,9 @@
 def screen_amps(mask_ref, amps_ref, *out_refs):
     starts = np.cumsum([0] + [o.shape[1] for o in out_refs]).tolist()
     for out_ref, lo, hi in zip(out_refs, starts, starts[1:]):
-        for top in range(lo, hi, TILE):
+        cuts = [lo, *range((lo // TILE + 1) * TILE, hi, TILE), hi]
+        for top, end in zip(cuts, cuts[1:]):
             top_tile = top // TILE
-            end = min(hi, (top_tile + 1) * TILE)
             for j in range(amps_ref.shape[1] // TILE):
                 tile = amps_ref[top:end, j * TILE : (j + 1) * TILE]
                 out_ref[0, top - lo : end - lo, j * TILE : (j + 1) * TILE] = jnp.where(
@@ -202,7 +202,7 @@
 VMEM_BYTES = 16 << 20
 
 
-M_ROWS = 256
+M_ROWS = 192
 
 
 def product_plane_kernel(ys, planes_ref, kept_ref, *refs):
@@ -258,7 +258,7 @@
     return permute(part.astype(SENT), lambda z, y, x, c: (z + y + step(c), y, x, c))
 
 
-S_ROWS, A_ROWS, B_ROWS = 384, 64, 64
+S_ROWS, A_ROWS, B_ROWS = 368, 64, 80
 
 
 def on_device(amps, ints, amp_mask, int_mask, vir_energy, pair_energy):
@@ -288,8 +288,9 @@
     d = 2 * core - 1
     where = jnp.stack([(x + o * (d if abs(o) == 1 else 1)) % N for o in OFFS] + [core]).astype(jnp.int32)
 
+    a_part, b_part, kept = lax.optimization_barrier((a_part, b_part, kept))
     a_pair, b_pair = swap(a_part), swap(b_part)
-    s_part, a_pair, b_pair = lax.optimization_barrier((s_part, a_pair, b_pair))
+    s_part = lax.optimization_barrier((s_part, kept))[0]
     planes = lax.all_gather(s_part[0], "virt", axis=0).reshape(N, 2 * N, S_ROWS, depth)
     round_a, round_b = first_round(a_part, a_pair, "x"), first_round(b_part, b_pair, "y")
     a_own = ((jnp.concatenate([round_a[o, k] for o in OFFS for k in (0, 1)], 0).reshape(N, 2, A_ROWS, depth),), (0,), OFFS, False)
@@ -301,7 +302,6 @@
     )
     a_near, b_near = ((shift(a_own[0][0], "y"),), (1,), OFFS, False), ((shift(b_own[0][0], "x"),), OFFS, (1,), False)
     a_next, b_next = a_near[0][0][:, 0], b_near[0][0][:, 0]
-    a_next, b_next, kept = lax.optimization_barrier((a_next, b_next, kept))
     a_far, b_far = shift(a_next, "y"), shift(b_next, "x")
     a_side, b_side = swapped(a_near), swapped(b_near)
 
@@ -311,17 +311,15 @@
     a_other, b_other = swap(a_far), swap(b_far)
     b_done = product([[((b_far, b_other), OFFS, (2,), False)]], OFFS, kept, where, b_early)
     a_last = product([[((a_far, a_other), (2,), OFFS, False)]], (2,), kept, where)
-    p_got = [
-        to_owner(jnp.concatenate([a, b], 0), o) for a, b, o in zip([*a_early, *a_last], b_done, OFFS)
-    ]
-    planes, *p_got = lax.optimization_barrier((planes, *p_got))
+    p_parts = [jnp.concatenate([a, b], 0).astype(SENT) for a, b in zip([*a_early, *a_last], b_done)]
+    p_got = [to_owner(part, o) for part, o in zip(p_parts, OFFS)]
+    planes = lax.optimization_barrier((planes, p_parts))[0]
     turn = lambda part, i: permute(part.astype(SENT), lambda z, y, x, c: (z + i, y, x, c))
-    mid = S_ROWS // 2
     (across,) = product_plane(planes, (2,), kept)
-    low, high = turn(across[:mid], 1), turn(across[mid:], 3)
+    across = permute(across.astype(SENT), lambda z, y, x, c: (z - side(c), y, x, c)).astype(jnp.float32)
     up, down = product_plane(planes, (1, 3), kept)
-    up = jnp.concatenate([up[:mid] + low.astype(jnp.float32), up[mid:]], 0).astype(SENT)
-    down = jnp.concatenate([down[:mid], down[mid:] + high.astype(jnp.float32)], 0).astype(SENT)
+    up = (up + jnp.where(core == 0, across, 0.0)).astype(SENT)
+    down = (down + jnp.where(core == 1, across, 0.0)).astype(SENT)
     planes, up, down = lax.optimization_barrier((planes, up, down))
     up, down = turn(up, 1), turn(down, 3)
     (here,) = product_plane(planes, (0,), kept)

time: 171 us -> 166 us (0.971); the launches traced: 170 us -> 163 us
  starting transfers between devices: 62.7 us -> 49 us
  local copies, waits for them, and re-layouts: 21.4 us -> 28.3 us
  waiting for transfers between devices: 29.7 us -> 26.4 us
  other arithmetic: 2.65 us -> 5.4 us
    ppermute x29 -> x28, starting transfers between devices: 62.7 us -> 49 us  [permute(): return lax.ppermute(arr, AXES, pairs)]
    unnamed x39 -> x55, local copies, waits for them, and re-layouts: 16.2 us -> 23 us
    all_gather x1, waiting for transfers between devices: 5.45 us -> 0.02 us  [on_device(): lax.all_gather(s_part[0], 'virt', axis=0).reshape(N, 2 * N, S_ROWS, depth)]
    ppermute x29 -> x28, waiting for transfers between devices: 24.2 us -> 26.4 us  [permute(): return lax.ppermute(arr, AXES, pairs)]
    pallas_call x4, Pallas kernels: 12.2 us -> 14.1 us  [product(): pl.pallas_call(functools.partial(product_kernel, phases, len(init), nf),...]
  transfers between devices with their start and end apart: 30 -> 29, of which waited for: 13 -> 8; matrix products, arithmetic and copies ran while one was open for 3% -> 6% of each run, Pallas kernels for 18% -> 23%
where the time goes in v3:
time: 166 us; the launch traced here: 163 us
  starting transfers between devices  49 us (30%)
  Pallas kernels  39.7 us (24%)
  local copies, waits for them, and re-layouts  28.3 us (17%)
  waiting for transfers between devices  26.4 us (16%)
  between operations  14 us (8%)
  other arithmetic  5.4 us (3%)
    ppermute x28, starting transfers between devices, permute(): return lax.ppermute(arr, AXES, pairs)  49 us
    ppermute x28, waiting for transfers between devices, permute(): return lax.ppermute(arr, AXES, pairs)  26.4 us
    unnamed x55, local copies, waits for them, and re-layouts  23 us
    pallas_call x3, Pallas kernels, product_plane(): pl.pallas_call(functools.partial(product_plane_kernel, ys), in_specs=[pl....  20.1 us
    pallas_call x4, Pallas kernels, product(): pl.pallas_call(functools.partial(product_kernel, phases, len(init), nf),...  14.1 us
  transfers between devices with their start and end apart: 29, of which 8 were waited for; matrix products, arithmetic and copies ran while one was open for 6% of the time, Pallas kernels for 23%

profile of v3, /device:TPU:1, one launch (start us, length us, event | category | flops | bytes accessed | tf_op | source)
XLA Modules:
  0.0 162.8 jit_solution(7353664454296280455)
XLA Ops:
  6.5 2.2 %shard_map.100 = (bf16[1,368,768]{2,1,0:T(8,128)(2,1)}, bf16[1,64,768]{2,1,0:T(8,128)(2,1)}, bf16[1,80,768]{2,1,0:T(8,128)(2,1)}) custom-call(s32[4,6]{1,0:T(4,128)} %mask_ref.2, bf16[512,768]{1,0:T(8,128)(2,1)} %amps_ref.1), custom_call_target="tpu_custom_call" | custom-call | tf_op jit(solution)/shard_map/pallas_call | solution.py:267
  8.7 1.7 %collective-permute-start = (bf16[1,368,768]{2,1,0:T(8,128)(2,1)}, bf16[1,368,768]{2,1,0:T(8,128)(2,1)S(1)}, u32[]{:S(2)}, u32[]{:S(2)}) collective-permute-start(bf16[1,368,768]{2,1,0:T(8,128)(2,1)} %get-tuple-element.31), channel_id=1, source_target_pairs={{0,0},{1,1},{2,2},{3,3},{4,4},{5,5},{6,6},{7,7},{8,56},{9,57},{10,... | collective-permute-start | bytes 1695752 | tf_op jit(solution)/shard_map/ppermute | solution.py:30
  10.4 1.5 collective-permute-start.2
  12.0 1.5 collective-permute-start.1
  14.3 3.7 %copy-done.4 = bf16[6144,768]{1,0:T(8,128)(2,1)S(1)} copy-done((bf16[6144,768]{1,0:T(8,128)(2,1)S(1)}, bf16[6144,768]{1,0:T(8,128)(2,1)}, u32[]{:S(2)}) %copy-start.4) | copy-done | bytes 9437208
  18.0 3.2 %shard_map.101.refs_3_.refs_2_.kept_ref = bf16[6144,768]{1,0:T(8,128)(2,1)S(1)} custom-call(s32[48,6]{1,0:T(8,128)S(1)} %copy.19.mask_ref, bf16[6144,768]{1,0:T(8,128)(2,1)S(1)} %copy-done.4), custom_call_target="tpu_custom_call" | custom-call | tf_op jit(solution)/shard_map/pallas_call | solution.py:275
  21.2 3.7 %copy-done = bf16[6144,768]{1,0:T(8,128)(2,1)} copy-done((bf16[6144,768]{1,0:T(8,128)(2,1)}, bf16[6144,768]{1,0:T(8,128)(2,1)S(1)}, u32[]{:S(2)}) %copy-start) | copy-done | bytes 9437208
  25.8 1.5 collective-permute-start.3
  28.2 2.6 %collective-permute-start.4 = (bf16[2,64,768]{2,1,0:T(8,128)(2,1)S(1)}, bf16[2,64,768]{2,1,0:T(8,128)(2,1)S(1)}, u32[]{:S(2)}, u32[]{:S(2)}) collective-permute-start(bf16[2,64,768]{2,1,0:T(8,128)(2,1)S(1)} %pad_maximum_fusion.5), channel_id=1, source_target_pairs={{0,2},{1,7},{2,4},{3,1},{4,6},{5,3},{6,0},{7,5},{8,10},{9,15},{10,... | collective-permute-start | bytes 589832 | tf_op jit(solution)/shard_map/ppermute | solution.py:30
  30.9 12.7 %collective-permute-start.12 = (bf16[2,80,768]{2,1,0:T(8,128)(2,1)S(1)}, bf16[2,80,768]{2,1,0:T(8,128)(2,1)S(1)}, u32[]{:S(2)}, u32[]{:S(2)}) collective-permute-start(bf16[2,80,768]{2,1,0:T(8,128)(2,1)S(1)} %pad_maximum_fusion), channel_id=1, source_target_pairs={{0,8},{1,25},{2,10},{3,27},{4,12},{5,29},{6,14},{7,31},{8,16},{9,1... | collective-permute-start | bytes 737288 | tf_op jit(solution)/shard_map/ppermute | solution.py:30
  44.3 2.5 %collective-permute-done.12 = bf16[2,80,768]{2,1,0:T(8,128)(2,1)S(1)} collective-permute-done((bf16[2,80,768]{2,1,0:T(8,128)(2,1)S(1)}, bf16[2,80,768]{2,1,0:T(8,128)(2,1)S(1)}, u32[]{:S(2)}, u32[]{:S(2)}) %collective-permute-start.12) | collective-permute-done | bytes 245792 | tf_op jit(solution)/shard_map/ppermute | solution.py:30
  47.4 2.6 %collective-permute-start.14 = (bf16[1,80,768]{2,1,0:T(8,128)(2,1)S(1)}, bf16[1,80,768]{2,1,0:T(8,128)(2,1)S(1)}, u32[]{:S(2)}, u32[]{:S(2)}) collective-permute-start(bf16[1,80,768]{2,1,0:T(8,128)(2,1)S(1)} %get-tuple-element.59), channel_id=1, source_target_pairs={{0,8},{1,25},{2,10},{3,27},{4,12},{5,29},{6,14},{7,31},{8,16},{9,1... | collective-permute-start | bytes 368648 | tf_op jit(solution)/shard_map/ppermute | solution.py:30
  50.0 4.2 %collective-permute-done.14 = bf16[1,80,768]{2,1,0:T(8,128)(2,1)S(1)} collective-permute-done((bf16[1,80,768]{2,1,0:T(8,128)(2,1)S(1)}, bf16[1,80,768]{2,1,0:T(8,128)(2,1)S(1)}, u32[]{:S(2)}, u32[]{:S(2)}) %collective-permute-start.14) | collective-permute-done | bytes 122912 | tf_op jit(solution)/shard_map/ppermute | solution.py:30
  54.2 1.6 collective-permute-start.15
  58.3 2.1 %collective-permute-start.8 = (bf16[4,2,64,768]{3,2,0,1:T(8,128)(2,1)S(1)}, bf16[4,2,64,768]{3,2,0,1:T(8,128)(2,1)}, u32[]{:S(2)}, u32[]{:S(2)}) collective-permute-start(bf16[4,2,64,768]{3,2,0,1:T(8,128)(2,1)S(1)} %copy.20), channel_id=1, source_target_pairs={{0,8},{1,25},{2,10},{3,27},{4,12},{5,29},{6,14},{7,31},{8,16},{9,1... | collective-permute-start | bytes 2359304 | tf_op jit(solution)/shard_map/ppermute | solution.py:30
  60.4 11.8 %collective-permute-done.16.refs_1_ = bf16[1,2,320,768]{3,2,1,0:T(8,128)(2,1)S(1)} collective-permute-done((bf16[1,2,320,768]{3,2,1,0:T(8,128)(2,1)S(1)}, bf16[1,2,320,768]{3,2,1,0:T(8,128)(2,1)S(1)}, u32[]{:S(2)}, u32[]{:S(2)}) %collective-permute-start.16) | collective-permute-done | bytes 983072 | tf_op jit(solution)/shard_map/ppermute | solution.py:30
  75.5 1.8 %slice_bitcast_fusion.1 = bf16[4,64,768]{2,1,0:T(8,128)(2,1)} fusion(bf16[4,2,64,768]{3,2,0,1:T(8,128)(2,1)} %collective-permute-done.8), kind=kLoop, calls=%fused_computation.11 | loop fusion | bytes 786432 | tf_op jit(solution)/shard_map/squeeze | solution.py:304
  81.1 4.0 %copy-done.1 = bf16[6144,768]{1,0:T(8,128)(2,1)S(1)} copy-done((bf16[6144,768]{1,0:T(8,128)(2,1)S(1)}, bf16[6144,768]{1,0:T(8,128)(2,1)}, u32[]{:S(2)}) %copy-start.1) | copy-done | bytes 9437208
  85.2 3.4 %shard_map.102 = (f32[64,768]{1,0:T(8,128)S(1)}, f32[64,768]{1,0:T(8,128)S(1)}, f32[64,768]{1,0:T(8,128)S(1)}) custom-call(s32[4,4]{1,0:T(4,128)S(1)} %copy-done.15, s32[5]{0:T(128)S(1)} %stack.23.where_ref, bf16[4,2,64,768]{3,2,1,0:T(8,128)(2,1)S(1)} %bitcast.13, bf16[4,2,64,768]{3,2,1,0:T(8,128)(2,1)S(1)} %copy.21.refs_1_, ...), custom_call_target="tpu_custom_call" | custom-call | flops 113246208 | bytes 737280 | tf_op jit(solution)/shard_map/pallas_call | solution.py:182
  88.7 5.0 %shard_map.103 = (f32[80,768]{1,0:T(8,128)S(1)}, f32[80,768]{1,0:T(8,128)S(1)}, f32[80,768]{1,0:T(8,128)S(1)}, f32[80,768]{1,0:T(8,128)S(1)}) custom-call(s32[4,3]{1,0:T(4,128)S(1)} %copy-done.16, s32[5]{0:T(128)S(1)} %stack.23.where_ref, bf16[1,2,320,768]{3,2,1,0:T(8,128)(2,1)S(1)} %bitcast.15, ...), custom_call_target="tpu_custom_call" | custom-call | flops 141557760 | bytes 626688 | tf_op jit(solution)/shard_map/pallas_call | solution.py:182
  98.8 4.1 %copy-done.2 = bf16[6144,768]{1,0:T(8,128)(2,1)S(1)} copy-done((bf16[6144,768]{1,0:T(8,128)(2,1)S(1)}, bf16[6144,768]{1,0:T(8,128)(2,1)}, u32[]{:S(2)}) %copy-start.2) | copy-done | bytes 9437208
  102.8 4.1 %shard_map.105 = f32[64,768]{1,0:T(8,128)S(1)} custom-call(s32[3,4]{1,0:T(4,128)S(1)} %copy-done.14, s32[5]{0:T(128)S(1)} %stack.23.where_ref, bf16[4,64,768]{2,1,0:T(8,128)(2,1)} %collective-permute-done.10.refs_0_, bf16[4,64,768]{2,1,0:T(8,128)(2,1)S(1)} %collective-permute-done.20.refs_1_, bf16[6144,768]{1,0:T(8,128)(2,1)S(1)} %copy-done.2), custom_call_target="tpu_custom_call" | custom-call | flops 37748736 | bytes 638976 | tf_op jit(solution)/shard_map/pallas_call | solution.py:182
  107.0 1.7 %shard_map.104 = (f32[80,768]{1,0:T(8,128)S(1)}, f32[80,768]{1,0:T(8,128)S(1)}, f32[80,768]{1,0:T(8,128)S(1)}, f32[80,768]{1,0:T(8,128)S(1)}) custom-call(s32[3,1]{1,0:T(4,128)S(1)} %copy-done.13, s32[5]{0:T(128)S(1)} %stack.23.where_ref, bf16[1,320,768]{2,1,0:T(8,128)(2,1)S(1)} %collective-permute-done.17.refs_0_, ...), custom_call_target="tpu_custom_call" | custom-call | flops 47185920 | bytes 208896 | tf_op jit(solution)/shard_map/pallas_call | solution.py:182
  108.7 4.2 %collective-permute-start.27 = (f16[144,768]{1,0:T(8,128)(2,1)S(1)}, f16[144,768]{1,0:T(8,128)(2,1)S(1)}, u32[]{:S(2)}, u32[]{:S(2)}) collective-permute-start(f16[144,768]{1,0:T(8,128)(2,1)S(1)} %pad_maximum_fusion.4), channel_id=1, source_target_pairs={{0,64},{1,65},{2,66},{3,67},{4,68},{5,69},{6,70},{7,71},{8,104},{9... | collective-permute-start | bytes 663560 | tf_op jit(solution)/shard_map/ppermute | solution.py:30
  113.0 2.9 %collective-permute-start.26 = (f16[144,768]{1,0:T(8,128)(2,1)S(1)}, f16[144,768]{1,0:T(8,128)(2,1)S(1)}, u32[]{:S(2)}, u32[]{:S(2)}) collective-permute-start(f16[144,768]{1,0:T(8,128)(2,1)S(1)} %pad_maximum_fusion.3), channel_id=1, source_target_pairs={{0,32},{1,97},{2,34},{3,99},{4,36},{5,101},{6,38},{7,103},{8,72},{... | collective-permute-start | bytes 663560 | tf_op jit(solution)/shard_map/ppermute | solution.py:30
  116.0 2.4 %collective-permute-start.25 = (f16[144,768]{1,0:T(8,128)(2,1)S(1)}, f16[144,768]{1,0:T(8,128)(2,1)}, u32[]{:S(2)}, u32[]{:S(2)}) collective-permute-start(f16[144,768]{1,0:T(8,128)(2,1)S(1)} %pad_maximum_fusion.2), channel_id=1, source_target_pairs={{0,96},{1,33},{2,98},{3,35},{4,100},{5,37},{6,102},{7,39},{8,8},{9... | collective-permute-start | bytes 663560 | tf_op jit(solution)/shard_map/ppermute | solution.py:30
  119.2 3.7 %copy-done.3 = bf16[6144,768]{1,0:T(8,128)(2,1)S(1)} copy-done((bf16[6144,768]{1,0:T(8,128)(2,1)S(1)}, bf16[6144,768]{1,0:T(8,128)(2,1)}, u32[]{:S(2)}) %copy-start.3) | copy-done | bytes 9437208
  122.9 5.4 %shard_map.107 = f32[368,768]{1,0:T(8,128)S(1)} custom-call(bf16[4,8,368,768]{3,2,1,0:T(8,128)(2,1)} %bitcast.16, bf16[6144,768]{1,0:T(8,128)(2,1)S(1)} %copy-done.3), custom_call_target="tpu_custom_call" | custom-call | flops 3472883712 | bytes 15089664 | tf_op jit(solution)/shard_map/pallas_call | solution.py:236
  128.4 2.6 %collective-permute-start.21 = (f16[368,768]{1,0:T(8,128)(2,1)S(1)}, f16[368,768]{1,0:T(8,128)(2,1)S(1)}, u32[]{:S(2)}, u32[]{:S(2)}) collective-permute-start(f16[368,768]{1,0:T(8,128)(2,1)S(1)} %convert_element_type.38), channel_id=1, source_target_pairs={{0,32},{1,97},{2,34},{3,99},{4,36},{5,101},{6,38},{7,103},{8,40},{... | collective-permute-start | bytes 1695752 | tf_op jit(solution)/shard_map/ppermute | solution.py:30
  131.0 9.3 %shard_map.106 = (f32[368,768]{1,0:T(8,128)S(1)}, f32[368,768]{1,0:T(8,128)S(1)}) custom-call(bf16[4,8,368,768]{3,2,1,0:T(8,128)(2,1)} %bitcast.17, bf16[6144,768]{1,0:T(8,128)(2,1)S(1)} %copy-done.3), custom_call_target="tpu_custom_call" | custom-call | flops 6945767424 | bytes 20742144 | tf_op jit(solution)/shard_map/pallas_call | solution.py:236
  143.3 5.4 %shard_map.108 = f32[368,768]{1,0:T(8,128)S(1)} custom-call(bf16[4,8,368,768]{3,2,1,0:T(8,128)(2,1)} %bitcast.18, bf16[6144,768]{1,0:T(8,128)(2,1)S(1)} %copy-done.3), custom_call_target="tpu_custom_call" | custom-call | flops 3472883712 | bytes 15089664 | tf_op jit(solution)/shard_map/pallas_call | solution.py:236
  148.7 5.1 %collective-permute-done.23 = f16[368,768]{1,0:T(8,128)(2,1)S(1)} collective-permute-done((f16[368,768]{1,0:T(8,128)(2,1)S(1)}, f16[368,768]{1,0:T(8,128)(2,1)S(1)}, u32[]{:S(2)}, u32[]{:S(2)}) %collective-permute-start.23) | collective-permute-done | bytes 565280 | tf_op jit(solution)/shard_map/ppermute | solution.py:30
  (120 shorter events, 24.7 us)
Async XLA Ops:
  6.5 112.7 %all-gather.2.cloned.1.call-start = ((), (), s32[]{:S(2)}) async-start(), calls=%async_computation | async-start | bytes 18653184 | tf_op jit(solution)/shard_map/all_gather | solution.py:294
  8.7 16.2 %collective-permute-start = (bf16[1,368,768]{2,1,0:T(8,128)(2,1)}, bf16[1,368,768]{2,1,0:T(8,128)(2,1)S(1)}, u32[]{:S(2)}, u32[]{:S(2)}) collective-permute-start(bf16[1,368,768]{2,1,0:T(8,128)(2,1)} %get-tuple-element.31), channel_id=1, source_target_pairs={{0,0},{1,1},{2,2},{3,3},{4,4},{5,5},{6,6},{7,7},{8,56},{9,57},{10,... | collective-permute-start | bytes 1695752 | tf_op jit(solution)/shard_map/ppermute | solution.py:30
  10.4 14.5 %collective-permute-start.2 = (bf16[1,80,768]{2,1,0:T(8,128)(2,1)}, bf16[1,80,768]{2,1,0:T(8,128)(2,1)S(1)}, u32[]{:S(2)}, u32[]{:S(2)}) collective-permute-start(bf16[1,80,768]{2,1,0:T(8,128)(2,1)} %get-tuple-element.33), channel_id=1, source_target_pairs={{0,0},{1,1},{2,2},{3,3},{4,4},{5,5},{6,6},{7,7},{8,56},{9,57},{10,... | collective-permute-start | bytes 368648 | tf_op jit(solution)/shard_map/ppermute | solution.py:30
  12.0 12.9 %collective-permute-start.1 = (bf16[1,64,768]{2,1,0:T(8,128)(2,1)}, bf16[1,64,768]{2,1,0:T(8,128)(2,1)S(1)}, u32[]{:S(2)}, u32[]{:S(2)}) collective-permute-start(bf16[1,64,768]{2,1,0:T(8,128)(2,1)} %get-tuple-element.32), channel_id=1, source_target_pairs={{0,0},{1,1},{2,2},{3,3},{4,4},{5,5},{6,6},{7,7},{8,56},{9,57},{10,... | collective-permute-start | bytes 294920 | tf_op jit(solution)/shard_map/ppermute | solution.py:30
  25.8 2.4 %collective-permute-start.3 = (bf16[1,64,768]{2,1,0:T(8,128)(2,1)S(1)}, bf16[1,64,768]{2,1,0:T(8,128)(2,1)S(1)}, u32[]{:S(2)}, u32[]{:S(2)}) collective-permute-start(bf16[1,64,768]{2,1,0:T(8,128)(2,1)S(1)} %collective-permute-done.1), channel_id=1, source_target_pairs={{0,1},{1,0},{2,3},{3,2},{4,5},{5,4},{6,7},{7,6},{8,9},{9,8},{10,11... | collective-permute-start | bytes 294920 | tf_op jit(solution)/shard_map/ppermute | solution.py:30
  27.3 3.6 %collective-permute-start.11 = (bf16[1,80,768]{2,1,0:T(8,128)(2,1)S(1)}, bf16[1,80,768]{2,1,0:T(8,128)(2,1)S(1)}, u32[]{:S(2)}, u32[]{:S(2)}) collective-permute-start(bf16[1,80,768]{2,1,0:T(8,128)(2,1)S(1)} %collective-permute-done.2), channel_id=1, source_target_pairs={{0,1},{1,0},{2,3},{3,2},{4,5},{5,4},{6,7},{7,6},{8,9},{9,8},{10,11... | collective-permute-start | bytes 368648 | tf_op jit(solution)/shard_map/ppermute | solution.py:30
  28.2 15.3 %collective-permute-start.4 = (bf16[2,64,768]{2,1,0:T(8,128)(2,1)S(1)}, bf16[2,64,768]{2,1,0:T(8,128)(2,1)S(1)}, u32[]{:S(2)}, u32[]{:S(2)}) collective-permute-start(bf16[2,64,768]{2,1,0:T(8,128)(2,1)S(1)} %pad_maximum_fusion.5), channel_id=1, source_target_pairs={{0,2},{1,7},{2,4},{3,1},{4,6},{5,3},{6,0},{7,5},{8,10},{9,15},{10,... | collective-permute-start | bytes 589832 | tf_op jit(solution)/shard_map/ppermute | solution.py:30
  30.9 15.8 %collective-permute-start.12 = (bf16[2,80,768]{2,1,0:T(8,128)(2,1)S(1)}, bf16[2,80,768]{2,1,0:T(8,128)(2,1)S(1)}, u32[]{:S(2)}, u32[]{:S(2)}) collective-permute-start(bf16[2,80,768]{2,1,0:T(8,128)(2,1)S(1)} %pad_maximum_fusion), channel_id=1, source_target_pairs={{0,8},{1,25},{2,10},{3,27},{4,12},{5,29},{6,14},{7,31},{8,16},{9,1... | collective-permute-start | bytes 737288 | tf_op jit(solution)/shard_map/ppermute | solution.py:30
  43.6 6.4 %collective-permute-start.6 = (bf16[1,64,768]{2,1,0:T(8,128)(2,1)S(1)}, bf16[1,64,768]{2,1,0:T(8,128)(2,1)S(1)}, u32[]{:S(2)}, u32[]{:S(2)}) collective-permute-start(bf16[1,64,768]{2,1,0:T(8,128)(2,1)S(1)} %slice.42), channel_id=1, source_target_pairs={{0,2},{1,7},{2,4},{3,1},{4,6},{5,3},{6,0},{7,5},{8,10},{9,15},{10,... | collective-permute-start | bytes 294920 | tf_op jit(solution)/shard_map/ppermute | solution.py:30
  44.2 5.8 %collective-permute-start.5 = (bf16[2,64,768]{2,1,0:T(8,128)(2,1)S(1)}, bf16[2,64,768]{2,1,0:T(8,128)(2,1)S(1)}, u32[]{:S(2)}, u32[]{:S(2)}) collective-permute-start(bf16[2,64,768]{2,1,0:T(8,128)(2,1)S(1)} %collective-permute-done.4), channel_id=1, source_target_pairs={{0,1},{1,0},{2,3},{3,2},{4,5},{5,4},{6,7},{7,6},{8,9},{9,8},{10,11... | collective-permute-start | bytes 589832 | tf_op jit(solution)/shard_map/ppermute | solution.py:30
  46.7 9.1 %collective-permute-start.13 = (bf16[2,80,768]{2,1,0:T(8,128)(2,1)S(1)}, bf16[2,80,768]{2,1,0:T(8,128)(2,1)S(1)}, u32[]{:S(2)}, u32[]{:S(2)}) collective-permute-start(bf16[2,80,768]{2,1,0:T(8,128)(2,1)S(1)} %collective-permute-done.12), channel_id=1, source_target_pairs={{0,1},{1,0},{2,3},{3,2},{4,5},{5,4},{6,7},{7,6},{8,9},{9,8},{10,11... | collective-permute-start | bytes 737288 | tf_op jit(solution)/shard_map/ppermute | solution.py:30
  47.4 6.8 %collective-permute-start.14 = (bf16[1,80,768]{2,1,0:T(8,128)(2,1)S(1)}, bf16[1,80,768]{2,1,0:T(8,128)(2,1)S(1)}, u32[]{:S(2)}, u32[]{:S(2)}) collective-permute-start(bf16[1,80,768]{2,1,0:T(8,128)(2,1)S(1)} %get-tuple-element.59), channel_id=1, source_target_pairs={{0,8},{1,25},{2,10},{3,27},{4,12},{5,29},{6,14},{7,31},{8,16},{9,1... | collective-permute-start | bytes 368648 | tf_op jit(solution)/shard_map/ppermute | solution.py:30
  50.0 8.2 %collective-permute-start.7 = (bf16[1,64,768]{2,1,0:T(8,128)(2,1)S(1)}, bf16[1,64,768]{2,1,0:T(8,128)(2,1)S(1)}, u32[]{:S(2)}, u32[]{:S(2)}) collective-permute-start(bf16[1,64,768]{2,1,0:T(8,128)(2,1)S(1)} %collective-permute-done.6), channel_id=1, source_target_pairs={{0,1},{1,0},{2,3},{3,2},{4,5},{5,4},{6,7},{7,6},{8,9},{9,8},{10,11... | collective-permute-start | bytes 294920 | tf_op jit(solution)/shard_map/ppermute | solution.py:30
  54.2 2.6 %collective-permute-start.15 = (bf16[1,80,768]{2,1,0:T(8,128)(2,1)S(1)}, bf16[1,80,768]{2,1,0:T(8,128)(2,1)S(1)}, u32[]{:S(2)}, u32[]{:S(2)}) collective-permute-start(bf16[1,80,768]{2,1,0:T(8,128)(2,1)S(1)} %collective-permute-done.14), channel_id=1, source_target_pairs={{0,1},{1,0},{2,3},{3,2},{4,5},{5,4},{6,7},{7,6},{8,9},{9,8},{10,11... | collective-permute-start | bytes 368648 | tf_op jit(solution)/shard_map/ppermute | solution.py:30
  56.8 15.4 %collective-permute-start.16 = (bf16[1,2,320,768]{3,2,1,0:T(8,128)(2,1)S(1)}, bf16[1,2,320,768]{3,2,1,0:T(8,128)(2,1)S(1)}, u32[]{:S(2)}, u32[]{:S(2)}) collective-permute-start(bf16[1,2,320,768]{3,2,1,0:T(8,128)(2,1)S(1)} %bitcast.14), channel_id=1, source_target_pairs={{0,2},{1,7},{2,4},{3,1},{4,6},{5,3},{6,0},{7,5},{8,10},{9,15},{10,... | collective-permute-start | bytes 2949128 | tf_op jit(solution)/shard_map/ppermute | solution.py:30
  58.3 15.3 %collective-permute-start.8 = (bf16[4,2,64,768]{3,2,0,1:T(8,128)(2,1)S(1)}, bf16[4,2,64,768]{3,2,0,1:T(8,128)(2,1)}, u32[]{:S(2)}, u32[]{:S(2)}) collective-permute-start(bf16[4,2,64,768]{3,2,0,1:T(8,128)(2,1)S(1)} %copy.20), channel_id=1, source_target_pairs={{0,8},{1,25},{2,10},{3,27},{4,12},{5,29},{6,14},{7,31},{8,16},{9,1... | collective-permute-start | bytes 2359304 | tf_op jit(solution)/shard_map/ppermute | solution.py:30
  72.2 16.4 %collective-permute-start.18 = (bf16[1,2,320,768]{3,2,1,0:T(8,128)(2,1)S(1)}, bf16[1,2,320,768]{3,2,1,0:T(8,128)(2,1)}, u32[]{:S(2)}, u32[]{:S(2)}) collective-permute-start(bf16[1,2,320,768]{3,2,1,0:T(8,128)(2,1)S(1)} %collective-permute-done.16.refs_1_), channel_id=1, source_target_pairs={{0,1},{1,0},{2,3},{3,2},{4,5},{5,4},{6,7},{7,6},{8,9},{9,8},{10,11... | collective-permute-start | bytes 2949128 | tf_op jit(solution)/shard_map/ppermute | solution.py:30
  73.5 6.4 %collective-permute-start.9 = (bf16[4,2,64,768]{3,2,0,1:T(8,128)(2,1)}, bf16[4,2,64,768]{3,2,0,1:T(8,128)(2,1)}, u32[]{:S(2)}, u32[]{:S(2)}) collective-permute-start(bf16[4,2,64,768]{3,2,0,1:T(8,128)(2,1)} %collective-permute-done.8), channel_id=1, source_target_pairs={{0,1},{1,0},{2,3},{3,2},{4,5},{5,4},{6,7},{7,6},{8,9},{9,8},{10,11... | collective-permute-start | bytes 2359304 | tf_op jit(solution)/shard_map/ppermute | solution.py:30
  74.3 21.4 %collective-permute-start.17 = (bf16[1,320,768]{2,1,0:T(8,128)(2,1)}, bf16[1,320,768]{2,1,0:T(8,128)(2,1)S(1)}, u32[]{:S(2)}, u32[]{:S(2)}) collective-permute-start(bf16[1,320,768]{2,1,0:T(8,128)(2,1)} %slice_bitcast_fusion), channel_id=1, source_target_pairs={{0,2},{1,7},{2,4},{3,1},{4,6},{5,3},{6,0},{7,5},{8,10},{9,15},{10,... | collective-permute-start | bytes 1474568 | tf_op jit(solution)/shard_map/ppermute | solution.py:30
  77.3 18.4 %collective-permute-start.10 = (bf16[4,64,768]{2,1,0:T(8,128)(2,1)}, bf16[4,64,768]{2,1,0:T(8,128)(2,1)}, u32[]{:S(2)}, u32[]{:S(2)}) collective-permute-start(bf16[4,64,768]{2,1,0:T(8,128)(2,1)} %slice_bitcast_fusion.1), channel_id=1, source_target_pairs={{0,8},{1,25},{2,10},{3,27},{4,12},{5,29},{6,14},{7,31},{8,16},{9,1... | collective-permute-start | bytes 1179656 | tf_op jit(solution)/shard_map/ppermute | solution.py:30
  88.6 10.1 %copy-start.14 = (s32[3,4]{1,0:T(4,128)S(1)}, s32[3,4]{1,0:T(4,128)}, u32[]{:S(2)}) copy-start(s32[3,4]{1,0:T(4,128)} %constant.71.clone.table_ref) | copy-start | bytes 148
  95.7 11.2 %collective-permute-start.19 = (bf16[1,320,768]{2,1,0:T(8,128)(2,1)S(1)}, bf16[1,320,768]{2,1,0:T(8,128)(2,1)S(1)}, u32[]{:S(2)}, u32[]{:S(2)}) collective-permute-start(bf16[1,320,768]{2,1,0:T(8,128)(2,1)S(1)} %collective-permute-done.17.refs_0_), channel_id=1, source_target_pairs={{0,1},{1,0},{2,3},{3,2},{4,5},{5,4},{6,7},{7,6},{8,9},{9,8},{10,11... | collective-permute-start | bytes 1474568 | tf_op jit(solution)/shard_map/ppermute | solution.py:30
  95.7 3.0 %collective-permute-start.20 = (bf16[4,64,768]{2,1,0:T(8,128)(2,1)}, bf16[4,64,768]{2,1,0:T(8,128)(2,1)S(1)}, u32[]{:S(2)}, u32[]{:S(2)}) collective-permute-start(bf16[4,64,768]{2,1,0:T(8,128)(2,1)} %collective-permute-done.10.refs_0_), channel_id=1, source_target_pairs={{0,1},{1,0},{2,3},{3,2},{4,5},{5,4},{6,7},{7,6},{8,9},{9,8},{10,11... | collective-permute-start | bytes 1179656 | tf_op jit(solution)/shard_map/ppermute | solution.py:30
  108.7 32.4 %collective-permute-start.27 = (f16[144,768]{1,0:T(8,128)(2,1)S(1)}, f16[144,768]{1,0:T(8,128)(2,1)S(1)}, u32[]{:S(2)}, u32[]{:S(2)}) collective-permute-start(f16[144,768]{1,0:T(8,128)(2,1)S(1)} %pad_maximum_fusion.4), channel_id=1, source_target_pairs={{0,64},{1,65},{2,66},{3,67},{4,68},{5,69},{6,70},{7,71},{8,104},{9... | collective-permute-start | bytes 663560 | tf_op jit(solution)/shard_map/ppermute | solution.py:30
  113.0 29.2 %collective-permute-start.26 = (f16[144,768]{1,0:T(8,128)(2,1)S(1)}, f16[144,768]{1,0:T(8,128)(2,1)S(1)}, u32[]{:S(2)}, u32[]{:S(2)}) collective-permute-start(f16[144,768]{1,0:T(8,128)(2,1)S(1)} %pad_maximum_fusion.3), channel_id=1, source_target_pairs={{0,32},{1,97},{2,34},{3,99},{4,36},{5,101},{6,38},{7,103},{8,72},{... | collective-permute-start | bytes 663560 | tf_op jit(solution)/shard_map/ppermute | solution.py:30
  116.0 26.2 %collective-permute-start.25 = (f16[144,768]{1,0:T(8,128)(2,1)S(1)}, f16[144,768]{1,0:T(8,128)(2,1)}, u32[]{:S(2)}, u32[]{:S(2)}) collective-permute-start(f16[144,768]{1,0:T(8,128)(2,1)S(1)} %pad_maximum_fusion.2), channel_id=1, source_target_pairs={{0,96},{1,33},{2,98},{3,35},{4,100},{5,37},{6,102},{7,39},{8,8},{9... | collective-permute-start | bytes 663560 | tf_op jit(solution)/shard_map/ppermute | solution.py:30
  118.5 23.7 %collective-permute-start.24 = (f16[144,768]{1,0:T(8,128)(2,1)S(1)}, f16[144,768]{1,0:T(8,128)(2,1)S(1)}, u32[]{:S(2)}, u32[]{:S(2)}) collective-permute-start(f16[144,768]{1,0:T(8,128)(2,1)S(1)} %pad_maximum_fusion.1), channel_id=1, source_target_pairs={{0,0},{1,1},{2,2},{3,3},{4,4},{5,5},{6,6},{7,7},{8,40},{9,41},{10,... | collective-permute-start | bytes 663560 | tf_op jit(solution)/shard_map/ppermute | solution.py:30
  128.4 11.9 %collective-permute-start.21 = (f16[368,768]{1,0:T(8,128)(2,1)S(1)}, f16[368,768]{1,0:T(8,128)(2,1)S(1)}, u32[]{:S(2)}, u32[]{:S(2)}) collective-permute-start(f16[368,768]{1,0:T(8,128)(2,1)S(1)} %convert_element_type.38), channel_id=1, source_target_pairs={{0,32},{1,97},{2,34},{3,99},{4,36},{5,101},{6,38},{7,103},{8,40},{... | collective-permute-start | bytes 1695752 | tf_op jit(solution)/shard_map/ppermute | solution.py:30
  140.6 13.1 %collective-permute-start.23 = (f16[368,768]{1,0:T(8,128)(2,1)S(1)}, f16[368,768]{1,0:T(8,128)(2,1)S(1)}, u32[]{:S(2)}, u32[]{:S(2)}) collective-permute-start(f16[368,768]{1,0:T(8,128)(2,1)S(1)} %get-tuple-element.56), channel_id=1, source_target_pairs={{0,96},{1,97},{2,98},{3,99},{4,100},{5,101},{6,102},{7,103},{8,104... | collective-permute-start | bytes 1695752 | tf_op jit(solution)/shard_map/ppermute | solution.py:30
  141.2 13.0 %collective-permute-start.22 = (f16[368,768]{1,0:T(8,128)(2,1)S(1)}, f16[368,768]{1,0:T(8,128)(2,1)S(1)}, u32[]{:S(2)}, u32[]{:S(2)}) collective-permute-start(f16[368,768]{1,0:T(8,128)(2,1)S(1)} %get-tuple-element.55), channel_id=1, source_target_pairs={{0,32},{1,33},{2,34},{3,35},{4,36},{5,37},{6,38},{7,39},{8,40},{9,... | collective-permute-start | bytes 1695752 | tf_op jit(solution)/shard_map/ppermute | solution.py:30
  148.7 5.8 %copy-start.17 = (bf16[512,768]{1,0:T(8,128)(2,1)S(1)}, bf16[512,768]{1,0:T(8,128)(2,1)}, u32[]{:S(2)}) copy-start(bf16[512,768]{1,0:T(8,128)(2,1)} %amps_ref.1) | copy-start | bytes 2359300
  148.7 5.8 %copy-start.19 = (f32[768]{0:T(1024)S(1)}, f32[768]{0:T(1024)}, u32[]{:S(2)}) copy-start(f32[768]{0:T(1024)} %param.14) | copy-start | bytes 9220
  (18 other events, 59.1 us)
Sparse Core Ops, SparseCore 0:
  25.9 93.1 all-gather.1

commit v4 on v3

--- a/solution.py
+++ b/solution.py
@@ -12,6 +12,7 @@
 AXES = ("pair", "virt")
 N = 4
 SENT = jnp.float16
+GAIN = 8.0
 FLIP = {0: 0, 1: -1, -1: 1, 2: 2}
 
 
@@ -255,7 +256,7 @@
 
 def to_owner(part, off):
     step = lambda c: off * side(c) if abs(off) == 1 else off
-    return permute(part.astype(SENT), lambda z, y, x, c: (z + y + step(c), y, x, c))
+    return permute(part, lambda z, y, x, c: (z + y + step(c), y, x, c))
 
 
 S_ROWS, A_ROWS, B_ROWS = 368, 64, 80
@@ -311,24 +312,24 @@
     a_other, b_other = swap(a_far), swap(b_far)
     b_done = product([[((b_far, b_other), OFFS, (2,), False)]], OFFS, kept, where, b_early)
     a_last = product([[((a_far, a_other), (2,), OFFS, False)]], (2,), kept, where)
-    p_parts = [jnp.concatenate([a, b], 0).astype(SENT) for a, b in zip([*a_early, *a_last], b_done)]
+    p_parts = [(jnp.concatenate([a, b], 0) * GAIN).astype(SENT) for a, b in zip([*a_early, *a_last], b_done)]
     p_got = [to_owner(part, o) for part, o in zip(p_parts, OFFS)]
     planes = lax.optimization_barrier((planes, p_parts))[0]
-    turn = lambda part, i: permute(part.astype(SENT), lambda z, y, x, c: (z + i, y, x, c))
+    turn = lambda part, i: permute(part, lambda z, y, x, c: (z + i, y, x, c))
     (across,) = product_plane(planes, (2,), kept)
-    across = permute(across.astype(SENT), lambda z, y, x, c: (z - side(c), y, x, c)).astype(jnp.float32)
+    across = permute((across * GAIN).astype(SENT), lambda z, y, x, c: (z - side(c), y, x, c)).astype(jnp.float32)
     up, down = product_plane(planes, (1, 3), kept)
-    up = (up + jnp.where(core == 0, across, 0.0)).astype(SENT)
-    down = (down + jnp.where(core == 1, across, 0.0)).astype(SENT)
+    up = (up * GAIN + jnp.where(core == 0, across, 0.0)).astype(SENT)
+    down = (down * GAIN + jnp.where(core == 1, across, 0.0)).astype(SENT)
     planes, up, down = lax.optimization_barrier((planes, up, down))
     up, down = turn(up, 1), turn(down, 3)
     (here,) = product_plane(planes, (0,), kept)
-    s_got = [here, up, down]
+    s_got = [here * GAIN, up, down]
 
     total = lambda got: sum(g.astype(jnp.float32) for g in got)
     contracted = jnp.concatenate([total(s_got), total(p_got)], 0)
     denom = vir_energy[None, :] - pair_energy[:, None]
-    return amps.astype(jnp.float32) + contracted / denom
+    return amps.astype(jnp.float32) + contracted / (GAIN * denom)
 
 
 def solution(mesh):

time: 166 us -> 166 us (level)
  other arithmetic: 5.4 us -> 2.57 us
  waiting for transfers between devices: 26.4 us -> 28.7 us
    ppermute x28, waiting for transfers between devices: 26.4 us -> 28.7 us  [permute(): return lax.ppermute(arr, AXES, pairs)]
    another operation x8 -> x0, other arithmetic: 1.99 us -> none
    unnamed x55 -> x63, local copies, waits for them, and re-layouts: 23 us -> 23.7 us
  transfers between devices with their start and end apart: 29 -> 29, of which waited for: 8 -> 8; matrix products, arithmetic and copies ran while one was open for 6% -> 4% of each run, Pallas kernels for 23% -> 23%
where the time goes in v4:
time: 166 us; the launch traced here: 163 us
  starting transfers between devices  48.8 us (29%)
  Pallas kernels  39.7 us (24%)
  local copies, waits for them, and re-layouts  29 us (17%)
  waiting for transfers between devices  28.7 us (17%)
  between operations  14 us (8%)
  other arithmetic  2.57 us (2%)
    ppermute x28, starting transfers between devices, permute(): return lax.ppermute(arr, AXES, pairs)  48.8 us
    ppermute x28, waiting for transfers between devices, permute(): return lax.ppermute(arr, AXES, pairs)  28.7 us
    unnamed x63, local copies, waits for them, and re-layouts  23.7 us
    pallas_call x3, Pallas kernels, product_plane(): pl.pallas_call(functools.partial(product_plane_kernel, ys), in_specs=[pl....  20.1 us
    pallas_call x4, Pallas kernels, product(): pl.pallas_call(functools.partial(product_kernel, phases, len(init), nf),...  14.2 us
  transfers between devices with their start and end apart: 29, of which 8 were waited for; matrix products, arithmetic and copies ran while one was open for 4% of the time, Pallas kernels for 23%

profile of v4, /device:TPU:1, one launch (start us, length us, event | category | flops | bytes accessed | tf_op | source)
XLA Modules:
  0.0 162.8 jit_solution(12093137517207924203)
XLA Ops:
  6.5 2.2 %shard_map.100 = (bf16[1,368,768]{2,1,0:T(8,128)(2,1)}, bf16[1,64,768]{2,1,0:T(8,128)(2,1)}, bf16[1,80,768]{2,1,0:T(8,128)(2,1)}) custom-call(s32[4,6]{1,0:T(4,128)} %mask_ref.2, bf16[512,768]{1,0:T(8,128)(2,1)} %amps_ref.1), custom_call_target="tpu_custom_call" | custom-call | tf_op jit(solution)/shard_map/pallas_call | solution.py:268
  8.7 1.7 %collective-permute-start = (bf16[1,368,768]{2,1,0:T(8,128)(2,1)}, bf16[1,368,768]{2,1,0:T(8,128)(2,1)S(1)}, u32[]{:S(2)}, u32[]{:S(2)}) collective-permute-start(bf16[1,368,768]{2,1,0:T(8,128)(2,1)} %get-tuple-element.31), channel_id=1, source_target_pairs={{0,0},{1,1},{2,2},{3,3},{4,4},{5,5},{6,6},{7,7},{8,56},{9,57},{10,... | collective-permute-start | bytes 1695752 | tf_op jit(solution)/shard_map/ppermute | solution.py:31
  10.4 1.5 collective-permute-start.2
  12.0 1.5 collective-permute-start.1
  14.3 3.7 %copy-done.4 = bf16[6144,768]{1,0:T(8,128)(2,1)S(1)} copy-done((bf16[6144,768]{1,0:T(8,128)(2,1)S(1)}, bf16[6144,768]{1,0:T(8,128)(2,1)}, u32[]{:S(2)}) %copy-start.4) | copy-done | bytes 9437208
  18.0 3.2 %shard_map.101.refs_3_.refs_2_.kept_ref = bf16[6144,768]{1,0:T(8,128)(2,1)S(1)} custom-call(s32[48,6]{1,0:T(8,128)S(1)} %copy.19.mask_ref, bf16[6144,768]{1,0:T(8,128)(2,1)S(1)} %copy-done.4), custom_call_target="tpu_custom_call" | custom-call | tf_op jit(solution)/shard_map/pallas_call | solution.py:276
  21.2 3.7 %copy-done = bf16[6144,768]{1,0:T(8,128)(2,1)} copy-done((bf16[6144,768]{1,0:T(8,128)(2,1)}, bf16[6144,768]{1,0:T(8,128)(2,1)S(1)}, u32[]{:S(2)}) %copy-start) | copy-done | bytes 9437208
  28.2 2.6 %collective-permute-start.4 = (bf16[2,64,768]{2,1,0:T(8,128)(2,1)S(1)}, bf16[2,64,768]{2,1,0:T(8,128)(2,1)S(1)}, u32[]{:S(2)}, u32[]{:S(2)}) collective-permute-start(bf16[2,64,768]{2,1,0:T(8,128)(2,1)S(1)} %pad_maximum_fusion.1), channel_id=1, source_target_pairs={{0,2},{1,7},{2,4},{3,1},{4,6},{5,3},{6,0},{7,5},{8,10},{9,15},{10,... | collective-permute-start | bytes 589832 | tf_op jit(solution)/shard_map/ppermute | solution.py:31
  30.9 12.7 %collective-permute-start.12 = (bf16[2,80,768]{2,1,0:T(8,128)(2,1)S(1)}, bf16[2,80,768]{2,1,0:T(8,128)(2,1)S(1)}, u32[]{:S(2)}, u32[]{:S(2)}) collective-permute-start(bf16[2,80,768]{2,1,0:T(8,128)(2,1)S(1)} %pad_maximum_fusion), channel_id=1, source_target_pairs={{0,8},{1,25},{2,10},{3,27},{4,12},{5,29},{6,14},{7,31},{8,16},{9,1... | collective-permute-start | bytes 737288 | tf_op jit(solution)/shard_map/ppermute | solution.py:31
  44.3 2.5 %collective-permute-done.12 = bf16[2,80,768]{2,1,0:T(8,128)(2,1)S(1)} collective-permute-done((bf16[2,80,768]{2,1,0:T(8,128)(2,1)S(1)}, bf16[2,80,768]{2,1,0:T(8,128)(2,1)S(1)}, u32[]{:S(2)}, u32[]{:S(2)}) %collective-permute-start.12) | collective-permute-done | bytes 245792 | tf_op jit(solution)/shard_map/ppermute | solution.py:31
  47.4 2.6 %collective-permute-start.14 = (bf16[1,80,768]{2,1,0:T(8,128)(2,1)S(1)}, bf16[1,80,768]{2,1,0:T(8,128)(2,1)S(1)}, u32[]{:S(2)}, u32[]{:S(2)}) collective-permute-start(bf16[1,80,768]{2,1,0:T(8,128)(2,1)S(1)} %get-tuple-element.59), channel_id=1, source_target_pairs={{0,8},{1,25},{2,10},{3,27},{4,12},{5,29},{6,14},{7,31},{8,16},{9,1... | collective-permute-start | bytes 368648 | tf_op jit(solution)/shard_map/ppermute | solution.py:31
  50.0 4.2 %collective-permute-done.14 = bf16[1,80,768]{2,1,0:T(8,128)(2,1)S(1)} collective-permute-done((bf16[1,80,768]{2,1,0:T(8,128)(2,1)S(1)}, bf16[1,80,768]{2,1,0:T(8,128)(2,1)S(1)}, u32[]{:S(2)}, u32[]{:S(2)}) %collective-permute-start.14) | collective-permute-done | bytes 122912 | tf_op jit(solution)/shard_map/ppermute | solution.py:31
  54.2 1.6 collective-permute-start.15
  58.3 2.1 %collective-permute-start.8 = (bf16[4,2,64,768]{3,2,0,1:T(8,128)(2,1)S(1)}, bf16[4,2,64,768]{3,2,0,1:T(8,128)(2,1)}, u32[]{:S(2)}, u32[]{:S(2)}) collective-permute-start(bf16[4,2,64,768]{3,2,0,1:T(8,128)(2,1)S(1)} %copy.20), channel_id=1, source_target_pairs={{0,8},{1,25},{2,10},{3,27},{4,12},{5,29},{6,14},{7,31},{8,16},{9,1... | collective-permute-start | bytes 2359304 | tf_op jit(solution)/shard_map/ppermute | solution.py:31
  60.4 11.8 %collective-permute-done.16.refs_1_ = bf16[1,2,320,768]{3,2,1,0:T(8,128)(2,1)S(1)} collective-permute-done((bf16[1,2,320,768]{3,2,1,0:T(8,128)(2,1)S(1)}, bf16[1,2,320,768]{3,2,1,0:T(8,128)(2,1)S(1)}, u32[]{:S(2)}, u32[]{:S(2)}) %collective-permute-start.16) | collective-permute-done | bytes 983072 | tf_op jit(solution)/shard_map/ppermute | solution.py:31
  75.5 1.8 %slice_bitcast_fusion.1 = bf16[4,64,768]{2,1,0:T(8,128)(2,1)} fusion(bf16[4,2,64,768]{3,2,0,1:T(8,128)(2,1)} %collective-permute-done.8), kind=kLoop, calls=%fused_computation.20 | loop fusion | bytes 786432 | tf_op jit(solution)/shard_map/squeeze | solution.py:305
  81.1 4.0 %copy-done.1 = bf16[6144,768]{1,0:T(8,128)(2,1)S(1)} copy-done((bf16[6144,768]{1,0:T(8,128)(2,1)S(1)}, bf16[6144,768]{1,0:T(8,128)(2,1)}, u32[]{:S(2)}) %copy-start.1) | copy-done | bytes 9437208
  85.2 3.4 %shard_map.102 = (f32[64,768]{1,0:T(8,128)S(1)}, f32[64,768]{1,0:T(8,128)S(1)}, f32[64,768]{1,0:T(8,128)S(1)}) custom-call(s32[4,4]{1,0:T(4,128)S(1)} %copy-done.19, s32[5]{0:T(128)S(1)} %stack.23.where_ref, bf16[4,2,64,768]{3,2,1,0:T(8,128)(2,1)S(1)} %bitcast.13, bf16[4,2,64,768]{3,2,1,0:T(8,128)(2,1)S(1)} %copy.21.refs_1_, ...), custom_call_target="tpu_custom_call" | custom-call | flops 113246208 | bytes 737280 | tf_op jit(solution)/shard_map/pallas_call | solution.py:183
  89.3 5.0 %shard_map.103 = (f32[80,768]{1,0:T(8,128)S(1)}, f32[80,768]{1,0:T(8,128)S(1)}, f32[80,768]{1,0:T(8,128)S(1)}, f32[80,768]{1,0:T(8,128)S(1)}) custom-call(s32[4,3]{1,0:T(4,128)S(1)} %copy-done.20, s32[5]{0:T(128)S(1)} %stack.23.where_ref, bf16[1,2,320,768]{3,2,1,0:T(8,128)(2,1)S(1)} %bitcast.15, ...), custom_call_target="tpu_custom_call" | custom-call | flops 141557760 | bytes 626688 | tf_op jit(solution)/shard_map/pallas_call | solution.py:183
  96.9 2.4 %collective-permute-done.20.refs_1_ = bf16[4,64,768]{2,1,0:T(8,128)(2,1)S(1)} collective-permute-done((bf16[4,64,768]{2,1,0:T(8,128)(2,1)}, bf16[4,64,768]{2,1,0:T(8,128)(2,1)S(1)}, u32[]{:S(2)}, u32[]{:S(2)}) %collective-permute-start.20) | collective-permute-done | bytes 393248 | tf_op jit(solution)/shard_map/ppermute | solution.py:31
  99.3 4.1 %copy-done.2 = bf16[6144,768]{1,0:T(8,128)(2,1)S(1)} copy-done((bf16[6144,768]{1,0:T(8,128)(2,1)S(1)}, bf16[6144,768]{1,0:T(8,128)(2,1)}, u32[]{:S(2)}) %copy-start.2) | copy-done | bytes 9437208
  103.4 4.1 %shard_map.105 = f32[64,768]{1,0:T(8,128)S(1)} custom-call(s32[3,4]{1,0:T(4,128)S(1)} %copy-done.18, s32[5]{0:T(128)S(1)} %stack.23.where_ref, bf16[4,64,768]{2,1,0:T(8,128)(2,1)} %collective-permute-done.10.refs_0_, bf16[4,64,768]{2,1,0:T(8,128)(2,1)S(1)} %collective-permute-done.20.refs_1_, bf16[6144,768]{1,0:T(8,128)(2,1)S(1)} %copy-done.2), custom_call_target="tpu_custom_call" | custom-call | flops 37748736 | bytes 638976 | tf_op jit(solution)/shard_map/pallas_call | solution.py:183
  107.5 1.7 %shard_map.104 = (f32[80,768]{1,0:T(8,128)S(1)}, f32[80,768]{1,0:T(8,128)S(1)}, f32[80,768]{1,0:T(8,128)S(1)}, f32[80,768]{1,0:T(8,128)S(1)}) custom-call(s32[3,1]{1,0:T(4,128)S(1)} %copy-done.17, s32[5]{0:T(128)S(1)} %stack.23.where_ref, bf16[1,320,768]{2,1,0:T(8,128)(2,1)S(1)} %collective-permute-done.17.refs_0_, ...), custom_call_target="tpu_custom_call" | custom-call | flops 47185920 | bytes 208896 | tf_op jit(solution)/shard_map/pallas_call | solution.py:183
  109.3 3.9 %collective-permute-start.27 = (f16[144,768]{1,0:T(8,128)(2,1)S(1)}, f16[144,768]{1,0:T(8,128)(2,1)S(1)}, u32[]{:S(2)}, u32[]{:S(2)}) collective-permute-start(f16[144,768]{1,0:T(8,128)(2,1)S(1)} %fusion.8), channel_id=1, source_target_pairs={{0,64},{1,65},{2,66},{3,67},{4,68},{5,69},{6,70},{7,71},{8,104},{9... | collective-permute-start | bytes 663560 | tf_op jit(solution)/shard_map/ppermute | solution.py:31
  113.2 3.3 %collective-permute-start.26 = (f16[144,768]{1,0:T(8,128)(2,1)S(1)}, f16[144,768]{1,0:T(8,128)(2,1)S(1)}, u32[]{:S(2)}, u32[]{:S(2)}) collective-permute-start(f16[144,768]{1,0:T(8,128)(2,1)S(1)} %fusion.7), channel_id=1, source_target_pairs={{0,32},{1,97},{2,34},{3,99},{4,36},{5,101},{6,38},{7,103},{8,72},{... | collective-permute-start | bytes 663560 | tf_op jit(solution)/shard_map/ppermute | solution.py:31
  116.6 2.0 %collective-permute-start.25 = (f16[144,768]{1,0:T(8,128)(2,1)S(1)}, f16[144,768]{1,0:T(8,128)(2,1)S(1)}, u32[]{:S(2)}, u32[]{:S(2)}) collective-permute-start(f16[144,768]{1,0:T(8,128)(2,1)S(1)} %fusion.6), channel_id=1, source_target_pairs={{0,96},{1,33},{2,98},{3,35},{4,100},{5,37},{6,102},{7,39},{8,8},{9... | collective-permute-start | bytes 663560 | tf_op jit(solution)/shard_map/ppermute | solution.py:31
  119.4 3.7 %copy-done.3 = bf16[6144,768]{1,0:T(8,128)(2,1)S(1)} copy-done((bf16[6144,768]{1,0:T(8,128)(2,1)S(1)}, bf16[6144,768]{1,0:T(8,128)(2,1)}, u32[]{:S(2)}) %copy-start.3) | copy-done | bytes 9437208
  123.1 5.4 %shard_map.107 = f32[368,768]{1,0:T(8,128)S(1)} custom-call(bf16[4,8,368,768]{3,2,1,0:T(8,128)(2,1)} %bitcast.16, bf16[6144,768]{1,0:T(8,128)(2,1)S(1)} %copy-done.3), custom_call_target="tpu_custom_call" | custom-call | flops 3472883712 | bytes 15089664 | tf_op jit(solution)/shard_map/pallas_call | solution.py:237
  128.6 2.7 %collective-permute-start.21 = (f16[368,768]{1,0:T(8,128)(2,1)S(1)}, f16[368,768]{1,0:T(8,128)(2,1)S(1)}, u32[]{:S(2)}, u32[]{:S(2)}) collective-permute-start(f16[368,768]{1,0:T(8,128)(2,1)S(1)} %multiply_convert_fusion), channel_id=1, source_target_pairs={{0,32},{1,97},{2,34},{3,99},{4,36},{5,101},{6,38},{7,103},{8,40},{... | collective-permute-start | bytes 1695752 | tf_op jit(solution)/shard_map/ppermute | solution.py:31
  131.3 9.3 %shard_map.106 = (f32[368,768]{1,0:T(8,128)S(1)}, f32[368,768]{1,0:T(8,128)S(1)}) custom-call(bf16[4,8,368,768]{3,2,1,0:T(8,128)(2,1)} %bitcast.17, bf16[6144,768]{1,0:T(8,128)(2,1)S(1)} %copy-done.3), custom_call_target="tpu_custom_call" | custom-call | flops 6945767424 | bytes 20742144 | tf_op jit(solution)/shard_map/pallas_call | solution.py:237
  142.7 5.4 %shard_map.108 = f32[368,768]{1,0:T(8,128)S(1)} custom-call(bf16[4,8,368,768]{3,2,1,0:T(8,128)(2,1)} %bitcast.18, bf16[6144,768]{1,0:T(8,128)(2,1)S(1)} %copy-done.3), custom_call_target="tpu_custom_call" | custom-call | flops 3472883712 | bytes 15089664 | tf_op jit(solution)/shard_map/pallas_call | solution.py:237
  148.1 5.9 %collective-permute-done.23 = f16[368,768]{1,0:T(8,128)(2,1)S(1)} collective-permute-done((f16[368,768]{1,0:T(8,128)(2,1)S(1)}, f16[368,768]{1,0:T(8,128)(2,1)S(1)}, u32[]{:S(2)}, u32[]{:S(2)}) %collective-permute-start.23) | collective-permute-done | bytes 565280 | tf_op jit(solution)/shard_map/ppermute | solution.py:31
  (120 shorter events, 23.1 us)
Async XLA Ops:
  6.5 112.8 %all-gather.2.cloned.1.call-start = ((), (), s32[]{:S(2)}) async-start(), calls=%async_computation | async-start | bytes 18653184 | tf_op jit(solution)/shard_map/all_gather | solution.py:295
  8.7 16.2 %collective-permute-start = (bf16[1,368,768]{2,1,0:T(8,128)(2,1)}, bf16[1,368,768]{2,1,0:T(8,128)(2,1)S(1)}, u32[]{:S(2)}, u32[]{:S(2)}) collective-permute-start(bf16[1,368,768]{2,1,0:T(8,128)(2,1)} %get-tuple-element.31), channel_id=1, source_target_pairs={{0,0},{1,1},{2,2},{3,3},{4,4},{5,5},{6,6},{7,7},{8,56},{9,57},{10,... | collective-permute-start | bytes 1695752 | tf_op jit(solution)/shard_map/ppermute | solution.py:31
  10.4 14.5 %collective-permute-start.2 = (bf16[1,80,768]{2,1,0:T(8,128)(2,1)}, bf16[1,80,768]{2,1,0:T(8,128)(2,1)S(1)}, u32[]{:S(2)}, u32[]{:S(2)}) collective-permute-start(bf16[1,80,768]{2,1,0:T(8,128)(2,1)} %get-tuple-element.33), channel_id=1, source_target_pairs={{0,0},{1,1},{2,2},{3,3},{4,4},{5,5},{6,6},{7,7},{8,56},{9,57},{10,... | collective-permute-start | bytes 368648 | tf_op jit(solution)/shard_map/ppermute | solution.py:31
  12.0 12.9 %collective-permute-start.1 = (bf16[1,64,768]{2,1,0:T(8,128)(2,1)}, bf16[1,64,768]{2,1,0:T(8,128)(2,1)S(1)}, u32[]{:S(2)}, u32[]{:S(2)}) collective-permute-start(bf16[1,64,768]{2,1,0:T(8,128)(2,1)} %get-tuple-element.32), channel_id=1, source_target_pairs={{0,0},{1,1},{2,2},{3,3},{4,4},{5,5},{6,6},{7,7},{8,56},{9,57},{10,... | collective-permute-start | bytes 294920 | tf_op jit(solution)/shard_map/ppermute | solution.py:31
  25.8 2.4 %collective-permute-start.3 = (bf16[1,64,768]{2,1,0:T(8,128)(2,1)S(1)}, bf16[1,64,768]{2,1,0:T(8,128)(2,1)S(1)}, u32[]{:S(2)}, u32[]{:S(2)}) collective-permute-start(bf16[1,64,768]{2,1,0:T(8,128)(2,1)S(1)} %collective-permute-done.1), channel_id=1, source_target_pairs={{0,1},{1,0},{2,3},{3,2},{4,5},{5,4},{6,7},{7,6},{8,9},{9,8},{10,11... | collective-permute-start | bytes 294920 | tf_op jit(solution)/shard_map/ppermute | solution.py:31
  27.3 3.6 %collective-permute-start.11 = (bf16[1,80,768]{2,1,0:T(8,128)(2,1)S(1)}, bf16[1,80,768]{2,1,0:T(8,128)(2,1)S(1)}, u32[]{:S(2)}, u32[]{:S(2)}) collective-permute-start(bf16[1,80,768]{2,1,0:T(8,128)(2,1)S(1)} %collective-permute-done.2), channel_id=1, source_target_pairs={{0,1},{1,0},{2,3},{3,2},{4,5},{5,4},{6,7},{7,6},{8,9},{9,8},{10,11... | collective-permute-start | bytes 368648 | tf_op jit(solution)/shard_map/ppermute | solution.py:31
  28.2 15.3 %collective-permute-start.4 = (bf16[2,64,768]{2,1,0:T(8,128)(2,1)S(1)}, bf16[2,64,768]{2,1,0:T(8,128)(2,1)S(1)}, u32[]{:S(2)}, u32[]{:S(2)}) collective-permute-start(bf16[2,64,768]{2,1,0:T(8,128)(2,1)S(1)} %pad_maximum_fusion.1), channel_id=1, source_target_pairs={{0,2},{1,7},{2,4},{3,1},{4,6},{5,3},{6,0},{7,5},{8,10},{9,15},{10,... | collective-permute-start | bytes 589832 | tf_op jit(solution)/shard_map/ppermute | solution.py:31
  30.9 15.8 %collective-permute-start.12 = (bf16[2,80,768]{2,1,0:T(8,128)(2,1)S(1)}, bf16[2,80,768]{2,1,0:T(8,128)(2,1)S(1)}, u32[]{:S(2)}, u32[]{:S(2)}) collective-permute-start(bf16[2,80,768]{2,1,0:T(8,128)(2,1)S(1)} %pad_maximum_fusion), channel_id=1, source_target_pairs={{0,8},{1,25},{2,10},{3,27},{4,12},{5,29},{6,14},{7,31},{8,16},{9,1... | collective-permute-start | bytes 737288 | tf_op jit(solution)/shard_map/ppermute | solution.py:31
  43.6 6.4 %collective-permute-start.6 = (bf16[1,64,768]{2,1,0:T(8,128)(2,1)S(1)}, bf16[1,64,768]{2,1,0:T(8,128)(2,1)S(1)}, u32[]{:S(2)}, u32[]{:S(2)}) collective-permute-start(bf16[1,64,768]{2,1,0:T(8,128)(2,1)S(1)} %slice.42), channel_id=1, source_target_pairs={{0,2},{1,7},{2,4},{3,1},{4,6},{5,3},{6,0},{7,5},{8,10},{9,15},{10,... | collective-permute-start | bytes 294920 | tf_op jit(solution)/shard_map/ppermute | solution.py:31
  44.2 5.8 %collective-permute-start.5 = (bf16[2,64,768]{2,1,0:T(8,128)(2,1)S(1)}, bf16[2,64,768]{2,1,0:T(8,128)(2,1)S(1)}, u32[]{:S(2)}, u32[]{:S(2)}) collective-permute-start(bf16[2,64,768]{2,1,0:T(8,128)(2,1)S(1)} %collective-permute-done.4), channel_id=1, source_target_pairs={{0,1},{1,0},{2,3},{3,2},{4,5},{5,4},{6,7},{7,6},{8,9},{9,8},{10,11... | collective-permute-start | bytes 589832 | tf_op jit(solution)/shard_map/ppermute | solution.py:31
  46.7 9.1 %collective-permute-start.13 = (bf16[2,80,768]{2,1,0:T(8,128)(2,1)S(1)}, bf16[2,80,768]{2,1,0:T(8,128)(2,1)S(1)}, u32[]{:S(2)}, u32[]{:S(2)}) collective-permute-start(bf16[2,80,768]{2,1,0:T(8,128)(2,1)S(1)} %collective-permute-done.12), channel_id=1, source_target_pairs={{0,1},{1,0},{2,3},{3,2},{4,5},{5,4},{6,7},{7,6},{8,9},{9,8},{10,11... | collective-permute-start | bytes 737288 | tf_op jit(solution)/shard_map/ppermute | solution.py:31
  47.4 6.8 %collective-permute-start.14 = (bf16[1,80,768]{2,1,0:T(8,128)(2,1)S(1)}, bf16[1,80,768]{2,1,0:T(8,128)(2,1)S(1)}, u32[]{:S(2)}, u32[]{:S(2)}) collective-permute-start(bf16[1,80,768]{2,1,0:T(8,128)(2,1)S(1)} %get-tuple-element.59), channel_id=1, source_target_pairs={{0,8},{1,25},{2,10},{3,27},{4,12},{5,29},{6,14},{7,31},{8,16},{9,1... | collective-permute-start | bytes 368648 | tf_op jit(solution)/shard_map/ppermute | solution.py:31
  50.0 8.2 %collective-permute-start.7 = (bf16[1,64,768]{2,1,0:T(8,128)(2,1)S(1)}, bf16[1,64,768]{2,1,0:T(8,128)(2,1)S(1)}, u32[]{:S(2)}, u32[]{:S(2)}) collective-permute-start(bf16[1,64,768]{2,1,0:T(8,128)(2,1)S(1)} %collective-permute-done.6), channel_id=1, source_target_pairs={{0,1},{1,0},{2,3},{3,2},{4,5},{5,4},{6,7},{7,6},{8,9},{9,8},{10,11... | collective-permute-start | bytes 294920 | tf_op jit(solution)/shard_map/ppermute | solution.py:31
  54.2 2.6 %collective-permute-start.15 = (bf16[1,80,768]{2,1,0:T(8,128)(2,1)S(1)}, bf16[1,80,768]{2,1,0:T(8,128)(2,1)S(1)}, u32[]{:S(2)}, u32[]{:S(2)}) collective-permute-start(bf16[1,80,768]{2,1,0:T(8,128)(2,1)S(1)} %collective-permute-done.14), channel_id=1, source_target_pairs={{0,1},{1,0},{2,3},{3,2},{4,5},{5,4},{6,7},{7,6},{8,9},{9,8},{10,11... | collective-permute-start | bytes 368648 | tf_op jit(solution)/shard_map/ppermute | solution.py:31
  56.8 15.4 %collective-permute-start.16 = (bf16[1,2,320,768]{3,2,1,0:T(8,128)(2,1)S(1)}, bf16[1,2,320,768]{3,2,1,0:T(8,128)(2,1)S(1)}, u32[]{:S(2)}, u32[]{:S(2)}) collective-permute-start(bf16[1,2,320,768]{3,2,1,0:T(8,128)(2,1)S(1)} %bitcast.14), channel_id=1, source_target_pairs={{0,2},{1,7},{2,4},{3,1},{4,6},{5,3},{6,0},{7,5},{8,10},{9,15},{10,... | collective-permute-start | bytes 2949128 | tf_op jit(solution)/shard_map/ppermute | solution.py:31
  58.3 15.2 %collective-permute-start.8 = (bf16[4,2,64,768]{3,2,0,1:T(8,128)(2,1)S(1)}, bf16[4,2,64,768]{3,2,0,1:T(8,128)(2,1)}, u32[]{:S(2)}, u32[]{:S(2)}) collective-permute-start(bf16[4,2,64,768]{3,2,0,1:T(8,128)(2,1)S(1)} %copy.20), channel_id=1, source_target_pairs={{0,8},{1,25},{2,10},{3,27},{4,12},{5,29},{6,14},{7,31},{8,16},{9,1... | collective-permute-start | bytes 2359304 | tf_op jit(solution)/shard_map/ppermute | solution.py:31
  72.2 17.1 %collective-permute-start.18 = (bf16[1,2,320,768]{3,2,1,0:T(8,128)(2,1)S(1)}, bf16[1,2,320,768]{3,2,1,0:T(8,128)(2,1)}, u32[]{:S(2)}, u32[]{:S(2)}) collective-permute-start(bf16[1,2,320,768]{3,2,1,0:T(8,128)(2,1)S(1)} %collective-permute-done.16.refs_1_), channel_id=1, source_target_pairs={{0,1},{1,0},{2,3},{3,2},{4,5},{5,4},{6,7},{7,6},{8,9},{9,8},{10,11... | collective-permute-start | bytes 2949128 | tf_op jit(solution)/shard_map/ppermute | solution.py:31
  73.5 6.3 %collective-permute-start.9 = (bf16[4,2,64,768]{3,2,0,1:T(8,128)(2,1)}, bf16[4,2,64,768]{3,2,0,1:T(8,128)(2,1)}, u32[]{:S(2)}, u32[]{:S(2)}) collective-permute-start(bf16[4,2,64,768]{3,2,0,1:T(8,128)(2,1)} %collective-permute-done.8), channel_id=1, source_target_pairs={{0,1},{1,0},{2,3},{3,2},{4,5},{5,4},{6,7},{7,6},{8,9},{9,8},{10,11... | collective-permute-start | bytes 2359304 | tf_op jit(solution)/shard_map/ppermute | solution.py:31
  74.3 22.1 %collective-permute-start.17 = (bf16[1,320,768]{2,1,0:T(8,128)(2,1)}, bf16[1,320,768]{2,1,0:T(8,128)(2,1)S(1)}, u32[]{:S(2)}, u32[]{:S(2)}) collective-permute-start(bf16[1,320,768]{2,1,0:T(8,128)(2,1)} %slice_bitcast_fusion), channel_id=1, source_target_pairs={{0,2},{1,7},{2,4},{3,1},{4,6},{5,3},{6,0},{7,5},{8,10},{9,15},{10,... | collective-permute-start | bytes 1474568 | tf_op jit(solution)/shard_map/ppermute | solution.py:31
  77.3 19.1 %collective-permute-start.10 = (bf16[4,64,768]{2,1,0:T(8,128)(2,1)}, bf16[4,64,768]{2,1,0:T(8,128)(2,1)}, u32[]{:S(2)}, u32[]{:S(2)}) collective-permute-start(bf16[4,64,768]{2,1,0:T(8,128)(2,1)} %slice_bitcast_fusion.1), channel_id=1, source_target_pairs={{0,8},{1,25},{2,10},{3,27},{4,12},{5,29},{6,14},{7,31},{8,16},{9,1... | collective-permute-start | bytes 1179656 | tf_op jit(solution)/shard_map/ppermute | solution.py:31
  89.3 10.0 %copy-start.18 = (s32[3,4]{1,0:T(4,128)S(1)}, s32[3,4]{1,0:T(4,128)}, u32[]{:S(2)}) copy-start(s32[3,4]{1,0:T(4,128)} %constant.75.clone.table_ref) | copy-start | bytes 148
  96.4 11.0 %collective-permute-start.19 = (bf16[1,320,768]{2,1,0:T(8,128)(2,1)S(1)}, bf16[1,320,768]{2,1,0:T(8,128)(2,1)S(1)}, u32[]{:S(2)}, u32[]{:S(2)}) collective-permute-start(bf16[1,320,768]{2,1,0:T(8,128)(2,1)S(1)} %collective-permute-done.17.refs_0_), channel_id=1, source_target_pairs={{0,1},{1,0},{2,3},{3,2},{4,5},{5,4},{6,7},{7,6},{8,9},{9,8},{10,11... | collective-permute-start | bytes 1474568 | tf_op jit(solution)/shard_map/ppermute | solution.py:31
  96.4 2.9 %collective-permute-start.20 = (bf16[4,64,768]{2,1,0:T(8,128)(2,1)}, bf16[4,64,768]{2,1,0:T(8,128)(2,1)S(1)}, u32[]{:S(2)}, u32[]{:S(2)}) collective-permute-start(bf16[4,64,768]{2,1,0:T(8,128)(2,1)} %collective-permute-done.10.refs_0_), channel_id=1, source_target_pairs={{0,1},{1,0},{2,3},{3,2},{4,5},{5,4},{6,7},{7,6},{8,9},{9,8},{10,11... | collective-permute-start | bytes 1179656 | tf_op jit(solution)/shard_map/ppermute | solution.py:31
  109.2 7.4 %copy-start.14 = (f32[64,768]{1,0:T(8,128)S(1)}, f32[64,768]{1,0:T(8,128)}, u32[]{:S(2)}) copy-start(f32[64,768]{1,0:T(8,128)} %copy-done.13) | copy-start | bytes 589828
  109.2 9.4 %copy-start.12 = (f32[64,768]{1,0:T(8,128)S(1)}, f32[64,768]{1,0:T(8,128)}, u32[]{:S(2)}) copy-start(f32[64,768]{1,0:T(8,128)} %copy-done.11) | copy-start | bytes 589828
  109.3 32.1 %collective-permute-start.27 = (f16[144,768]{1,0:T(8,128)(2,1)S(1)}, f16[144,768]{1,0:T(8,128)(2,1)S(1)}, u32[]{:S(2)}, u32[]{:S(2)}) collective-permute-start(f16[144,768]{1,0:T(8,128)(2,1)S(1)} %fusion.8), channel_id=1, source_target_pairs={{0,64},{1,65},{2,66},{3,67},{4,68},{5,69},{6,70},{7,71},{8,104},{9... | collective-permute-start | bytes 663560 | tf_op jit(solution)/shard_map/ppermute | solution.py:31
  113.2 29.3 %collective-permute-start.26 = (f16[144,768]{1,0:T(8,128)(2,1)S(1)}, f16[144,768]{1,0:T(8,128)(2,1)S(1)}, u32[]{:S(2)}, u32[]{:S(2)}) collective-permute-start(f16[144,768]{1,0:T(8,128)(2,1)S(1)} %fusion.7), channel_id=1, source_target_pairs={{0,32},{1,97},{2,34},{3,99},{4,36},{5,101},{6,38},{7,103},{8,72},{... | collective-permute-start | bytes 663560 | tf_op jit(solution)/shard_map/ppermute | solution.py:31
  116.6 25.9 %collective-permute-start.25 = (f16[144,768]{1,0:T(8,128)(2,1)S(1)}, f16[144,768]{1,0:T(8,128)(2,1)S(1)}, u32[]{:S(2)}, u32[]{:S(2)}) collective-permute-start(f16[144,768]{1,0:T(8,128)(2,1)S(1)} %fusion.6), channel_id=1, source_target_pairs={{0,96},{1,33},{2,98},{3,35},{4,100},{5,37},{6,102},{7,39},{8,8},{9... | collective-permute-start | bytes 663560 | tf_op jit(solution)/shard_map/ppermute | solution.py:31
  118.7 23.9 %collective-permute-start.24 = (f16[144,768]{1,0:T(8,128)(2,1)S(1)}, f16[144,768]{1,0:T(8,128)(2,1)S(1)}, u32[]{:S(2)}, u32[]{:S(2)}) collective-permute-start(f16[144,768]{1,0:T(8,128)(2,1)S(1)} %fusion.5), channel_id=1, source_target_pairs={{0,0},{1,1},{2,2},{3,3},{4,4},{5,5},{6,6},{7,7},{8,40},{9,41},{10,... | collective-permute-start | bytes 663560 | tf_op jit(solution)/shard_map/ppermute | solution.py:31
  128.6 12.0 %collective-permute-start.21 = (f16[368,768]{1,0:T(8,128)(2,1)S(1)}, f16[368,768]{1,0:T(8,128)(2,1)S(1)}, u32[]{:S(2)}, u32[]{:S(2)}) collective-permute-start(f16[368,768]{1,0:T(8,128)(2,1)S(1)} %multiply_convert_fusion), channel_id=1, source_target_pairs={{0,32},{1,97},{2,34},{3,99},{4,36},{5,101},{6,38},{7,103},{8,40},{... | collective-permute-start | bytes 1695752 | tf_op jit(solution)/shard_map/ppermute | solution.py:31
  141.0 13.0 %collective-permute-start.23 = (f16[368,768]{1,0:T(8,128)(2,1)S(1)}, f16[368,768]{1,0:T(8,128)(2,1)S(1)}, u32[]{:S(2)}, u32[]{:S(2)}) collective-permute-start(f16[368,768]{1,0:T(8,128)(2,1)S(1)} %get-tuple-element.56), channel_id=1, source_target_pairs={{0,96},{1,97},{2,98},{3,99},{4,100},{5,101},{6,102},{7,103},{8,104... | collective-permute-start | bytes 1695752 | tf_op jit(solution)/shard_map/ppermute | solution.py:31
  141.4 12.7 %collective-permute-start.22 = (f16[368,768]{1,0:T(8,128)(2,1)S(1)}, f16[368,768]{1,0:T(8,128)(2,1)S(1)}, u32[]{:S(2)}, u32[]{:S(2)}) collective-permute-start(f16[368,768]{1,0:T(8,128)(2,1)S(1)} %get-tuple-element.55), channel_id=1, source_target_pairs={{0,32},{1,33},{2,34},{3,35},{4,36},{5,37},{6,38},{7,39},{8,40},{9,... | collective-permute-start | bytes 1695752 | tf_op jit(solution)/shard_map/ppermute | solution.py:31
  (22 other events, 79.4 us)
Sparse Core Ops, SparseCore 0:
  25.9 93.1 all-gather.1

commit v5 on v4

--- a/solution.py
+++ b/solution.py
@@ -314,7 +314,6 @@
     a_last = product([[((a_far, a_other), (2,), OFFS, False)]], (2,), kept, where)
     p_parts = [(jnp.concatenate([a, b], 0) * GAIN).astype(SENT) for a, b in zip([*a_early, *a_last], b_done)]
     p_got = [to_owner(part, o) for part, o in zip(p_parts, OFFS)]
-    planes = lax.optimization_barrier((planes, p_parts))[0]
     turn = lambda part, i: permute(part, lambda z, y, x, c: (z + i, y, x, c))
     (across,) = product_plane(planes, (2,), kept)
     across = permute((across * GAIN).astype(SENT), lambda z, y, x, c: (z - side(c), y, x, c)).astype(jnp.float32)

time: 166 us -> 165 us (level)
  transfers between devices with their start and end apart: 29 -> 29, of which waited for: 8 -> 7; matrix products, arithmetic and copies ran while one was open for 4% -> 4% of each run, Pallas kernels for 23% -> 23%
where the time goes in v5:
time: 165 us; the launch traced here: 163 us
  starting transfers between devices  49.8 us (30%)
  Pallas kernels  39.7 us (24%)
  local copies, waits for them, and re-layouts  29 us (18%)
  waiting for transfers between devices  28.4 us (17%)
  between operations  14 us (8%)
  other arithmetic  2.56 us (2%)
    ppermute x28, starting transfers between devices, permute(): return lax.ppermute(arr, AXES, pairs)  49.8 us
    ppermute x28, waiting for transfers between devices, permute(): return lax.ppermute(arr, AXES, pairs)  28.3 us
    unnamed x63, local copies, waits for them, and re-layouts  23.7 us
    pallas_call x3, Pallas kernels, product_plane(): pl.pallas_call(functools.partial(product_plane_kernel, ys), in_specs=[pl....  20.1 us
    pallas_call x4, Pallas kernels, product(): pl.pallas_call(functools.partial(product_kernel, phases, len(init), nf),...  14.2 us
  transfers between devices with their start and end apart: 29, of which 7 were waited for; matrix products, arithmetic and copies ran while one was open for 4% of the time, Pallas kernels for 23%

profile of v5, /device:TPU:1, one launch (start us, length us, event | category | flops | bytes accessed | tf_op | source)
XLA Modules:
  0.0 163.4 jit_solution(14268875304124836239)
XLA Ops:
  6.5 2.2 %shard_map.100 = (bf16[1,368,768]{2,1,0:T(8,128)(2,1)}, bf16[1,64,768]{2,1,0:T(8,128)(2,1)}, bf16[1,80,768]{2,1,0:T(8,128)(2,1)}) custom-call(s32[4,6]{1,0:T(4,128)} %mask_ref.2, bf16[512,768]{1,0:T(8,128)(2,1)} %amps_ref.1), custom_call_target="tpu_custom_call" | custom-call | tf_op jit(solution)/shard_map/pallas_call | solution.py:268
  8.7 1.7 %collective-permute-start = (bf16[1,368,768]{2,1,0:T(8,128)(2,1)}, bf16[1,368,768]{2,1,0:T(8,128)(2,1)S(1)}, u32[]{:S(2)}, u32[]{:S(2)}) collective-permute-start(bf16[1,368,768]{2,1,0:T(8,128)(2,1)} %get-tuple-element.30), channel_id=1, source_target_pairs={{0,0},{1,1},{2,2},{3,3},{4,4},{5,5},{6,6},{7,7},{8,56},{9,57},{10,... | collective-permute-start | bytes 1695752 | tf_op jit(solution)/shard_map/ppermute | solution.py:31
  10.4 1.5 collective-permute-start.2
  14.3 3.7 %copy-done.4 = bf16[6144,768]{1,0:T(8,128)(2,1)S(1)} copy-done((bf16[6144,768]{1,0:T(8,128)(2,1)S(1)}, bf16[6144,768]{1,0:T(8,128)(2,1)}, u32[]{:S(2)}) %copy-start.4) | copy-done | bytes 9437208
  18.0 3.2 %shard_map.101.kept_ref.refs_3_.refs_2_ = bf16[6144,768]{1,0:T(8,128)(2,1)S(1)} custom-call(s32[48,6]{1,0:T(8,128)S(1)} %copy.19.mask_ref, bf16[6144,768]{1,0:T(8,128)(2,1)S(1)} %copy-done.4), custom_call_target="tpu_custom_call" | custom-call | tf_op jit(solution)/shard_map/pallas_call | solution.py:276
  21.2 3.7 %copy-done = bf16[6144,768]{1,0:T(8,128)(2,1)} copy-done((bf16[6144,768]{1,0:T(8,128)(2,1)}, bf16[6144,768]{1,0:T(8,128)(2,1)S(1)}, u32[]{:S(2)}) %copy-start) | copy-done | bytes 9437208
  28.2 2.6 %collective-permute-start.7 = (bf16[2,64,768]{2,1,0:T(8,128)(2,1)S(1)}, bf16[2,64,768]{2,1,0:T(8,128)(2,1)S(1)}, u32[]{:S(2)}, u32[]{:S(2)}) collective-permute-start(bf16[2,64,768]{2,1,0:T(8,128)(2,1)S(1)} %pad_maximum_fusion.1), channel_id=1, source_target_pairs={{0,2},{1,7},{2,4},{3,1},{4,6},{5,3},{6,0},{7,5},{8,10},{9,15},{10,... | collective-permute-start | bytes 589832 | tf_op jit(solution)/shard_map/ppermute | solution.py:31
  30.9 12.7 %collective-permute-start.15 = (bf16[2,80,768]{2,1,0:T(8,128)(2,1)S(1)}, bf16[2,80,768]{2,1,0:T(8,128)(2,1)S(1)}, u32[]{:S(2)}, u32[]{:S(2)}) collective-permute-start(bf16[2,80,768]{2,1,0:T(8,128)(2,1)S(1)} %pad_maximum_fusion), channel_id=1, source_target_pairs={{0,8},{1,25},{2,10},{3,27},{4,12},{5,29},{6,14},{7,31},{8,16},{9,1... | collective-permute-start | bytes 737288 | tf_op jit(solution)/shard_map/ppermute | solution.py:31
  44.3 2.5 %collective-permute-done.15 = bf16[2,80,768]{2,1,0:T(8,128)(2,1)S(1)} collective-permute-done((bf16[2,80,768]{2,1,0:T(8,128)(2,1)S(1)}, bf16[2,80,768]{2,1,0:T(8,128)(2,1)S(1)}, u32[]{:S(2)}, u32[]{:S(2)}) %collective-permute-start.15) | collective-permute-done | bytes 245792 | tf_op jit(solution)/shard_map/ppermute | solution.py:31
  47.4 2.6 %collective-permute-start.17 = (bf16[1,80,768]{2,1,0:T(8,128)(2,1)S(1)}, bf16[1,80,768]{2,1,0:T(8,128)(2,1)S(1)}, u32[]{:S(2)}, u32[]{:S(2)}) collective-permute-start(bf16[1,80,768]{2,1,0:T(8,128)(2,1)S(1)} %get-tuple-element.57), channel_id=1, source_target_pairs={{0,8},{1,25},{2,10},{3,27},{4,12},{5,29},{6,14},{7,31},{8,16},{9,1... | collective-permute-start | bytes 368648 | tf_op jit(solution)/shard_map/ppermute | solution.py:31
  50.0 4.2 %collective-permute-done.17 = bf16[1,80,768]{2,1,0:T(8,128)(2,1)S(1)} collective-permute-done((bf16[1,80,768]{2,1,0:T(8,128)(2,1)S(1)}, bf16[1,80,768]{2,1,0:T(8,128)(2,1)S(1)}, u32[]{:S(2)}, u32[]{:S(2)}) %collective-permute-start.17) | collective-permute-done | bytes 122912 | tf_op jit(solution)/shard_map/ppermute | solution.py:31
  54.2 1.6 collective-permute-start.18
  58.3 2.1 %collective-permute-start.11 = (bf16[4,2,64,768]{3,2,0,1:T(8,128)(2,1)S(1)}, bf16[4,2,64,768]{3,2,0,1:T(8,128)(2,1)}, u32[]{:S(2)}, u32[]{:S(2)}) collective-permute-start(bf16[4,2,64,768]{3,2,0,1:T(8,128)(2,1)S(1)} %copy.20), channel_id=1, source_target_pairs={{0,8},{1,25},{2,10},{3,27},{4,12},{5,29},{6,14},{7,31},{8,16},{9,1... | collective-permute-start | bytes 2359304 | tf_op jit(solution)/shard_map/ppermute | solution.py:31
  60.4 11.8 %collective-permute-done.19.refs_1_ = bf16[1,2,320,768]{3,2,1,0:T(8,128)(2,1)S(1)} collective-permute-done((bf16[1,2,320,768]{3,2,1,0:T(8,128)(2,1)S(1)}, bf16[1,2,320,768]{3,2,1,0:T(8,128)(2,1)S(1)}, u32[]{:S(2)}, u32[]{:S(2)}) %collective-permute-start.19) | collective-permute-done | bytes 983072 | tf_op jit(solution)/shard_map/ppermute | solution.py:31
  75.5 1.8 %slice_bitcast_fusion.1 = bf16[4,64,768]{2,1,0:T(8,128)(2,1)} fusion(bf16[4,2,64,768]{3,2,0,1:T(8,128)(2,1)} %collective-permute-done.11), kind=kLoop, calls=%fused_computation.20 | loop fusion | bytes 786432 | tf_op jit(solution)/shard_map/squeeze | solution.py:305
  81.1 4.0 %copy-done.1 = bf16[6144,768]{1,0:T(8,128)(2,1)S(1)} copy-done((bf16[6144,768]{1,0:T(8,128)(2,1)S(1)}, bf16[6144,768]{1,0:T(8,128)(2,1)}, u32[]{:S(2)}) %copy-start.1) | copy-done | bytes 9437208
  85.2 3.4 %shard_map.105 = (f32[64,768]{1,0:T(8,128)S(1)}, f32[64,768]{1,0:T(8,128)S(1)}, f32[64,768]{1,0:T(8,128)S(1)}) custom-call(s32[4,4]{1,0:T(4,128)S(1)} %copy-done.19, s32[5]{0:T(128)S(1)} %stack.23.where_ref, bf16[4,2,64,768]{3,2,1,0:T(8,128)(2,1)S(1)} %bitcast.13, bf16[4,2,64,768]{3,2,1,0:T(8,128)(2,1)S(1)} %copy.21.refs_1_, ...), custom_call_target="tpu_custom_call" | custom-call | flops 113246208 | bytes 737280 | tf_op jit(solution)/shard_map/pallas_call | solution.py:183
  89.3 5.0 %shard_map.106 = (f32[80,768]{1,0:T(8,128)S(1)}, f32[80,768]{1,0:T(8,128)S(1)}, f32[80,768]{1,0:T(8,128)S(1)}, f32[80,768]{1,0:T(8,128)S(1)}) custom-call(s32[4,3]{1,0:T(4,128)S(1)} %copy-done.20, s32[5]{0:T(128)S(1)} %stack.23.where_ref, bf16[1,2,320,768]{3,2,1,0:T(8,128)(2,1)S(1)} %bitcast.15, ...), custom_call_target="tpu_custom_call" | custom-call | flops 141557760 | bytes 626688 | tf_op jit(solution)/shard_map/pallas_call | solution.py:183
  96.9 2.4 %collective-permute-done.26.refs_1_ = bf16[4,64,768]{2,1,0:T(8,128)(2,1)S(1)} collective-permute-done((bf16[4,64,768]{2,1,0:T(8,128)(2,1)}, bf16[4,64,768]{2,1,0:T(8,128)(2,1)S(1)}, u32[]{:S(2)}, u32[]{:S(2)}) %collective-permute-start.26) | collective-permute-done | bytes 393248 | tf_op jit(solution)/shard_map/ppermute | solution.py:31
  99.3 4.1 %copy-done.2 = bf16[6144,768]{1,0:T(8,128)(2,1)S(1)} copy-done((bf16[6144,768]{1,0:T(8,128)(2,1)S(1)}, bf16[6144,768]{1,0:T(8,128)(2,1)}, u32[]{:S(2)}) %copy-start.2) | copy-done | bytes 9437208
  103.4 4.1 %shard_map.108 = f32[64,768]{1,0:T(8,128)S(1)} custom-call(s32[3,4]{1,0:T(4,128)S(1)} %copy-done.18, s32[5]{0:T(128)S(1)} %stack.23.where_ref, bf16[4,64,768]{2,1,0:T(8,128)(2,1)} %collective-permute-done.13.refs_0_, bf16[4,64,768]{2,1,0:T(8,128)(2,1)S(1)} %collective-permute-done.26.refs_1_, bf16[6144,768]{1,0:T(8,128)(2,1)S(1)} %copy-done.2), custom_call_target="tpu_custom_call" | custom-call | flops 37748736 | bytes 638976 | tf_op jit(solution)/shard_map/pallas_call | solution.py:183
  107.5 1.7 %shard_map.107 = (f32[80,768]{1,0:T(8,128)S(1)}, f32[80,768]{1,0:T(8,128)S(1)}, f32[80,768]{1,0:T(8,128)S(1)}, f32[80,768]{1,0:T(8,128)S(1)}) custom-call(s32[3,1]{1,0:T(4,128)S(1)} %copy-done.17, s32[5]{0:T(128)S(1)} %stack.23.where_ref, bf16[1,320,768]{2,1,0:T(8,128)(2,1)S(1)} %collective-permute-done.20.refs_0_, ...), custom_call_target="tpu_custom_call" | custom-call | flops 47185920 | bytes 208896 | tf_op jit(solution)/shard_map/pallas_call | solution.py:183
  110.1 2.8 %collective-permute-start.24 = (f16[144,768]{1,0:T(8,128)(2,1)S(1)}, f16[144,768]{1,0:T(8,128)(2,1)S(1)}, u32[]{:S(2)}, u32[]{:S(2)}) collective-permute-start(f16[144,768]{1,0:T(8,128)(2,1)S(1)} %fusion.6), channel_id=1, source_target_pairs={{0,96},{1,33},{2,98},{3,35},{4,100},{5,37},{6,102},{7,39},{8,8},{9... | collective-permute-start | bytes 663560 | tf_op jit(solution)/shard_map/ppermute | solution.py:31
  113.0 3.7 %collective-permute-start.25 = (f16[144,768]{1,0:T(8,128)(2,1)S(1)}, f16[144,768]{1,0:T(8,128)(2,1)S(1)}, u32[]{:S(2)}, u32[]{:S(2)}) collective-permute-start(f16[144,768]{1,0:T(8,128)(2,1)S(1)} %fusion.7), channel_id=1, source_target_pairs={{0,32},{1,97},{2,34},{3,99},{4,36},{5,101},{6,38},{7,103},{8,72},{... | collective-permute-start | bytes 663560 | tf_op jit(solution)/shard_map/ppermute | solution.py:31
  116.8 3.1 %collective-permute-start.27 = (f16[144,768]{1,0:T(8,128)(2,1)S(1)}, f16[144,768]{1,0:T(8,128)(2,1)S(1)}, u32[]{:S(2)}, u32[]{:S(2)}) collective-permute-start(f16[144,768]{1,0:T(8,128)(2,1)S(1)} %fusion.8), channel_id=1, source_target_pairs={{0,64},{1,65},{2,66},{3,67},{4,68},{5,69},{6,70},{7,71},{8,104},{9... | collective-permute-start | bytes 663560 | tf_op jit(solution)/shard_map/ppermute | solution.py:31
  119.9 3.7 %copy-done.3 = bf16[6144,768]{1,0:T(8,128)(2,1)S(1)} copy-done((bf16[6144,768]{1,0:T(8,128)(2,1)S(1)}, bf16[6144,768]{1,0:T(8,128)(2,1)}, u32[]{:S(2)}) %copy-start.3) | copy-done | bytes 9437208
  123.6 5.4 %shard_map.103 = f32[368,768]{1,0:T(8,128)S(1)} custom-call(bf16[4,8,368,768]{3,2,1,0:T(8,128)(2,1)} %bitcast.16, bf16[6144,768]{1,0:T(8,128)(2,1)S(1)} %copy-done.3), custom_call_target="tpu_custom_call" | custom-call | flops 3472883712 | bytes 15089664 | tf_op jit(solution)/shard_map/pallas_call | solution.py:237
  129.1 1.9 %collective-permute-start.3 = (f16[368,768]{1,0:T(8,128)(2,1)S(1)}, f16[368,768]{1,0:T(8,128)(2,1)S(1)}, u32[]{:S(2)}, u32[]{:S(2)}) collective-permute-start(f16[368,768]{1,0:T(8,128)(2,1)S(1)} %multiply_convert_fusion), channel_id=1, source_target_pairs={{0,32},{1,97},{2,34},{3,99},{4,36},{5,101},{6,38},{7,103},{8,40},{... | collective-permute-start | bytes 1695752 | tf_op jit(solution)/shard_map/ppermute | solution.py:31
  131.0 9.3 %shard_map.102 = (f32[368,768]{1,0:T(8,128)S(1)}, f32[368,768]{1,0:T(8,128)S(1)}) custom-call(bf16[4,8,368,768]{3,2,1,0:T(8,128)(2,1)} %bitcast.17, bf16[6144,768]{1,0:T(8,128)(2,1)S(1)} %copy-done.3), custom_call_target="tpu_custom_call" | custom-call | flops 6945767424 | bytes 20742144 | tf_op jit(solution)/shard_map/pallas_call | solution.py:237
  140.8 2.7 %collective-permute-start.5 = (f16[368,768]{1,0:T(8,128)(2,1)S(1)}, f16[368,768]{1,0:T(8,128)(2,1)S(1)}, u32[]{:S(2)}, u32[]{:S(2)}) collective-permute-start(f16[368,768]{1,0:T(8,128)(2,1)S(1)} %get-tuple-element.39), channel_id=1, source_target_pairs={{0,96},{1,97},{2,98},{3,99},{4,100},{5,101},{6,102},{7,103},{8,104... | collective-permute-start | bytes 1695752 | tf_op jit(solution)/shard_map/ppermute | solution.py:31
  143.6 5.4 %shard_map.104 = f32[368,768]{1,0:T(8,128)S(1)} custom-call(bf16[4,8,368,768]{3,2,1,0:T(8,128)(2,1)} %bitcast.18, bf16[6144,768]{1,0:T(8,128)(2,1)S(1)} %copy-done.3), custom_call_target="tpu_custom_call" | custom-call | flops 3472883712 | bytes 15089664 | tf_op jit(solution)/shard_map/pallas_call | solution.py:237
  149.1 5.7 %collective-permute-done.4 = f16[368,768]{1,0:T(8,128)(2,1)S(1)} collective-permute-done((f16[368,768]{1,0:T(8,128)(2,1)S(1)}, f16[368,768]{1,0:T(8,128)(2,1)S(1)}, u32[]{:S(2)}, u32[]{:S(2)}) %collective-permute-start.4) | collective-permute-done | bytes 565280 | tf_op jit(solution)/shard_map/ppermute | solution.py:31
  (120 shorter events, 23.2 us)
Async XLA Ops:
  6.5 113.3 %all-gather.2.cloned.1.call-start = ((), (), s32[]{:S(2)}) async-start(), calls=%async_computation | async-start | bytes 18653184 | tf_op jit(solution)/shard_map/all_gather | solution.py:295
  8.7 16.2 %collective-permute-start = (bf16[1,368,768]{2,1,0:T(8,128)(2,1)}, bf16[1,368,768]{2,1,0:T(8,128)(2,1)S(1)}, u32[]{:S(2)}, u32[]{:S(2)}) collective-permute-start(bf16[1,368,768]{2,1,0:T(8,128)(2,1)} %get-tuple-element.30), channel_id=1, source_target_pairs={{0,0},{1,1},{2,2},{3,3},{4,4},{5,5},{6,6},{7,7},{8,56},{9,57},{10,... | collective-permute-start | bytes 1695752 | tf_op jit(solution)/shard_map/ppermute | solution.py:31
  10.4 14.5 %collective-permute-start.2 = (bf16[1,80,768]{2,1,0:T(8,128)(2,1)}, bf16[1,80,768]{2,1,0:T(8,128)(2,1)S(1)}, u32[]{:S(2)}, u32[]{:S(2)}) collective-permute-start(bf16[1,80,768]{2,1,0:T(8,128)(2,1)} %get-tuple-element.32), channel_id=1, source_target_pairs={{0,0},{1,1},{2,2},{3,3},{4,4},{5,5},{6,6},{7,7},{8,56},{9,57},{10,... | collective-permute-start | bytes 368648 | tf_op jit(solution)/shard_map/ppermute | solution.py:31
  12.0 12.9 %collective-permute-start.1 = (bf16[1,64,768]{2,1,0:T(8,128)(2,1)}, bf16[1,64,768]{2,1,0:T(8,128)(2,1)S(1)}, u32[]{:S(2)}, u32[]{:S(2)}) collective-permute-start(bf16[1,64,768]{2,1,0:T(8,128)(2,1)} %get-tuple-element.31), channel_id=1, source_target_pairs={{0,0},{1,1},{2,2},{3,3},{4,4},{5,5},{6,6},{7,7},{8,56},{9,57},{10,... | collective-permute-start | bytes 294920 | tf_op jit(solution)/shard_map/ppermute | solution.py:31
  25.8 2.4 %collective-permute-start.6 = (bf16[1,64,768]{2,1,0:T(8,128)(2,1)S(1)}, bf16[1,64,768]{2,1,0:T(8,128)(2,1)S(1)}, u32[]{:S(2)}, u32[]{:S(2)}) collective-permute-start(bf16[1,64,768]{2,1,0:T(8,128)(2,1)S(1)} %collective-permute-done.1), channel_id=1, source_target_pairs={{0,1},{1,0},{2,3},{3,2},{4,5},{5,4},{6,7},{7,6},{8,9},{9,8},{10,11... | collective-permute-start | bytes 294920 | tf_op jit(solution)/shard_map/ppermute | solution.py:31
  27.3 3.6 %collective-permute-start.14 = (bf16[1,80,768]{2,1,0:T(8,128)(2,1)S(1)}, bf16[1,80,768]{2,1,0:T(8,128)(2,1)S(1)}, u32[]{:S(2)}, u32[]{:S(2)}) collective-permute-start(bf16[1,80,768]{2,1,0:T(8,128)(2,1)S(1)} %collective-permute-done.2), channel_id=1, source_target_pairs={{0,1},{1,0},{2,3},{3,2},{4,5},{5,4},{6,7},{7,6},{8,9},{9,8},{10,11... | collective-permute-start | bytes 368648 | tf_op jit(solution)/shard_map/ppermute | solution.py:31
  28.2 15.3 %collective-permute-start.7 = (bf16[2,64,768]{2,1,0:T(8,128)(2,1)S(1)}, bf16[2,64,768]{2,1,0:T(8,128)(2,1)S(1)}, u32[]{:S(2)}, u32[]{:S(2)}) collective-permute-start(bf16[2,64,768]{2,1,0:T(8,128)(2,1)S(1)} %pad_maximum_fusion.1), channel_id=1, source_target_pairs={{0,2},{1,7},{2,4},{3,1},{4,6},{5,3},{6,0},{7,5},{8,10},{9,15},{10,... | collective-permute-start | bytes 589832 | tf_op jit(solution)/shard_map/ppermute | solution.py:31
  30.9 15.8 %collective-permute-start.15 = (bf16[2,80,768]{2,1,0:T(8,128)(2,1)S(1)}, bf16[2,80,768]{2,1,0:T(8,128)(2,1)S(1)}, u32[]{:S(2)}, u32[]{:S(2)}) collective-permute-start(bf16[2,80,768]{2,1,0:T(8,128)(2,1)S(1)} %pad_maximum_fusion), channel_id=1, source_target_pairs={{0,8},{1,25},{2,10},{3,27},{4,12},{5,29},{6,14},{7,31},{8,16},{9,1... | collective-permute-start | bytes 737288 | tf_op jit(solution)/shard_map/ppermute | solution.py:31
  43.6 6.4 %collective-permute-start.9 = (bf16[1,64,768]{2,1,0:T(8,128)(2,1)S(1)}, bf16[1,64,768]{2,1,0:T(8,128)(2,1)S(1)}, u32[]{:S(2)}, u32[]{:S(2)}) collective-permute-start(bf16[1,64,768]{2,1,0:T(8,128)(2,1)S(1)} %slice.42), channel_id=1, source_target_pairs={{0,2},{1,7},{2,4},{3,1},{4,6},{5,3},{6,0},{7,5},{8,10},{9,15},{10,... | collective-permute-start | bytes 294920 | tf_op jit(solution)/shard_map/ppermute | solution.py:31
  44.2 5.8 %collective-permute-start.8 = (bf16[2,64,768]{2,1,0:T(8,128)(2,1)S(1)}, bf16[2,64,768]{2,1,0:T(8,128)(2,1)S(1)}, u32[]{:S(2)}, u32[]{:S(2)}) collective-permute-start(bf16[2,64,768]{2,1,0:T(8,128)(2,1)S(1)} %collective-permute-done.7), channel_id=1, source_target_pairs={{0,1},{1,0},{2,3},{3,2},{4,5},{5,4},{6,7},{7,6},{8,9},{9,8},{10,11... | collective-permute-start | bytes 589832 | tf_op jit(solution)/shard_map/ppermute | solution.py:31
  46.7 9.1 %collective-permute-start.16 = (bf16[2,80,768]{2,1,0:T(8,128)(2,1)S(1)}, bf16[2,80,768]{2,1,0:T(8,128)(2,1)S(1)}, u32[]{:S(2)}, u32[]{:S(2)}) collective-permute-start(bf16[2,80,768]{2,1,0:T(8,128)(2,1)S(1)} %collective-permute-done.15), channel_id=1, source_target_pairs={{0,1},{1,0},{2,3},{3,2},{4,5},{5,4},{6,7},{7,6},{8,9},{9,8},{10,11... | collective-permute-start | bytes 737288 | tf_op jit(solution)/shard_map/ppermute | solution.py:31
  47.4 6.8 %collective-permute-start.17 = (bf16[1,80,768]{2,1,0:T(8,128)(2,1)S(1)}, bf16[1,80,768]{2,1,0:T(8,128)(2,1)S(1)}, u32[]{:S(2)}, u32[]{:S(2)}) collective-permute-start(bf16[1,80,768]{2,1,0:T(8,128)(2,1)S(1)} %get-tuple-element.57), channel_id=1, source_target_pairs={{0,8},{1,25},{2,10},{3,27},{4,12},{5,29},{6,14},{7,31},{8,16},{9,1... | collective-permute-start | bytes 368648 | tf_op jit(solution)/shard_map/ppermute | solution.py:31
  50.0 8.2 %collective-permute-start.10 = (bf16[1,64,768]{2,1,0:T(8,128)(2,1)S(1)}, bf16[1,64,768]{2,1,0:T(8,128)(2,1)S(1)}, u32[]{:S(2)}, u32[]{:S(2)}) collective-permute-start(bf16[1,64,768]{2,1,0:T(8,128)(2,1)S(1)} %collective-permute-done.9), channel_id=1, source_target_pairs={{0,1},{1,0},{2,3},{3,2},{4,5},{5,4},{6,7},{7,6},{8,9},{9,8},{10,11... | collective-permute-start | bytes 294920 | tf_op jit(solution)/shard_map/ppermute | solution.py:31
  54.2 2.6 %collective-permute-start.18 = (bf16[1,80,768]{2,1,0:T(8,128)(2,1)S(1)}, bf16[1,80,768]{2,1,0:T(8,128)(2,1)S(1)}, u32[]{:S(2)}, u32[]{:S(2)}) collective-permute-start(bf16[1,80,768]{2,1,0:T(8,128)(2,1)S(1)} %collective-permute-done.17), channel_id=1, source_target_pairs={{0,1},{1,0},{2,3},{3,2},{4,5},{5,4},{6,7},{7,6},{8,9},{9,8},{10,11... | collective-permute-start | bytes 368648 | tf_op jit(solution)/shard_map/ppermute | solution.py:31
  56.8 15.4 %collective-permute-start.19 = (bf16[1,2,320,768]{3,2,1,0:T(8,128)(2,1)S(1)}, bf16[1,2,320,768]{3,2,1,0:T(8,128)(2,1)S(1)}, u32[]{:S(2)}, u32[]{:S(2)}) collective-permute-start(bf16[1,2,320,768]{3,2,1,0:T(8,128)(2,1)S(1)} %bitcast.14), channel_id=1, source_target_pairs={{0,2},{1,7},{2,4},{3,1},{4,6},{5,3},{6,0},{7,5},{8,10},{9,15},{10,... | collective-permute-start | bytes 2949128 | tf_op jit(solution)/shard_map/ppermute | solution.py:31
  58.3 15.2 %collective-permute-start.11 = (bf16[4,2,64,768]{3,2,0,1:T(8,128)(2,1)S(1)}, bf16[4,2,64,768]{3,2,0,1:T(8,128)(2,1)}, u32[]{:S(2)}, u32[]{:S(2)}) collective-permute-start(bf16[4,2,64,768]{3,2,0,1:T(8,128)(2,1)S(1)} %copy.20), channel_id=1, source_target_pairs={{0,8},{1,25},{2,10},{3,27},{4,12},{5,29},{6,14},{7,31},{8,16},{9,1... | collective-permute-start | bytes 2359304 | tf_op jit(solution)/shard_map/ppermute | solution.py:31
  72.2 17.1 %collective-permute-start.21 = (bf16[1,2,320,768]{3,2,1,0:T(8,128)(2,1)S(1)}, bf16[1,2,320,768]{3,2,1,0:T(8,128)(2,1)}, u32[]{:S(2)}, u32[]{:S(2)}) collective-permute-start(bf16[1,2,320,768]{3,2,1,0:T(8,128)(2,1)S(1)} %collective-permute-done.19.refs_1_), channel_id=1, source_target_pairs={{0,1},{1,0},{2,3},{3,2},{4,5},{5,4},{6,7},{7,6},{8,9},{9,8},{10,11... | collective-permute-start | bytes 2949128 | tf_op jit(solution)/shard_map/ppermute | solution.py:31
  73.5 6.3 %collective-permute-start.12 = (bf16[4,2,64,768]{3,2,0,1:T(8,128)(2,1)}, bf16[4,2,64,768]{3,2,0,1:T(8,128)(2,1)}, u32[]{:S(2)}, u32[]{:S(2)}) collective-permute-start(bf16[4,2,64,768]{3,2,0,1:T(8,128)(2,1)} %collective-permute-done.11), channel_id=1, source_target_pairs={{0,1},{1,0},{2,3},{3,2},{4,5},{5,4},{6,7},{7,6},{8,9},{9,8},{10,11... | collective-permute-start | bytes 2359304 | tf_op jit(solution)/shard_map/ppermute | solution.py:31
  74.3 22.1 %collective-permute-start.20 = (bf16[1,320,768]{2,1,0:T(8,128)(2,1)}, bf16[1,320,768]{2,1,0:T(8,128)(2,1)S(1)}, u32[]{:S(2)}, u32[]{:S(2)}) collective-permute-start(bf16[1,320,768]{2,1,0:T(8,128)(2,1)} %slice_bitcast_fusion), channel_id=1, source_target_pairs={{0,2},{1,7},{2,4},{3,1},{4,6},{5,3},{6,0},{7,5},{8,10},{9,15},{10,... | collective-permute-start | bytes 1474568 | tf_op jit(solution)/shard_map/ppermute | solution.py:31
  77.3 19.1 %collective-permute-start.13 = (bf16[4,64,768]{2,1,0:T(8,128)(2,1)}, bf16[4,64,768]{2,1,0:T(8,128)(2,1)}, u32[]{:S(2)}, u32[]{:S(2)}) collective-permute-start(bf16[4,64,768]{2,1,0:T(8,128)(2,1)} %slice_bitcast_fusion.1), channel_id=1, source_target_pairs={{0,8},{1,25},{2,10},{3,27},{4,12},{5,29},{6,14},{7,31},{8,16},{9,1... | collective-permute-start | bytes 1179656 | tf_op jit(solution)/shard_map/ppermute | solution.py:31
  89.3 10.0 %copy-start.18 = (s32[3,4]{1,0:T(4,128)S(1)}, s32[3,4]{1,0:T(4,128)}, u32[]{:S(2)}) copy-start(s32[3,4]{1,0:T(4,128)} %constant.75.clone.table_ref) | copy-start | bytes 148
  96.4 11.0 %collective-permute-start.22 = (bf16[1,320,768]{2,1,0:T(8,128)(2,1)S(1)}, bf16[1,320,768]{2,1,0:T(8,128)(2,1)S(1)}, u32[]{:S(2)}, u32[]{:S(2)}) collective-permute-start(bf16[1,320,768]{2,1,0:T(8,128)(2,1)S(1)} %collective-permute-done.20.refs_0_), channel_id=1, source_target_pairs={{0,1},{1,0},{2,3},{3,2},{4,5},{5,4},{6,7},{7,6},{8,9},{9,8},{10,11... | collective-permute-start | bytes 1474568 | tf_op jit(solution)/shard_map/ppermute | solution.py:31
  96.4 2.9 %collective-permute-start.26 = (bf16[4,64,768]{2,1,0:T(8,128)(2,1)}, bf16[4,64,768]{2,1,0:T(8,128)(2,1)S(1)}, u32[]{:S(2)}, u32[]{:S(2)}) collective-permute-start(bf16[4,64,768]{2,1,0:T(8,128)(2,1)} %collective-permute-done.13.refs_0_), channel_id=1, source_target_pairs={{0,1},{1,0},{2,3},{3,2},{4,5},{5,4},{6,7},{7,6},{8,9},{9,8},{10,11... | collective-permute-start | bytes 1179656 | tf_op jit(solution)/shard_map/ppermute | solution.py:31
  109.3 31.6 %collective-permute-start.23 = (f16[144,768]{1,0:T(8,128)(2,1)S(1)}, f16[144,768]{1,0:T(8,128)(2,1)S(1)}, u32[]{:S(2)}, u32[]{:S(2)}) collective-permute-start(f16[144,768]{1,0:T(8,128)(2,1)S(1)} %fusion.5), channel_id=1, source_target_pairs={{0,0},{1,1},{2,2},{3,3},{4,4},{5,5},{6,6},{7,7},{8,40},{9,41},{10,... | collective-permute-start | bytes 663560 | tf_op jit(solution)/shard_map/ppermute | solution.py:31
  110.1 33.3 %collective-permute-start.24 = (f16[144,768]{1,0:T(8,128)(2,1)S(1)}, f16[144,768]{1,0:T(8,128)(2,1)S(1)}, u32[]{:S(2)}, u32[]{:S(2)}) collective-permute-start(f16[144,768]{1,0:T(8,128)(2,1)S(1)} %fusion.6), channel_id=1, source_target_pairs={{0,96},{1,33},{2,98},{3,35},{4,100},{5,37},{6,102},{7,39},{8,8},{9... | collective-permute-start | bytes 663560 | tf_op jit(solution)/shard_map/ppermute | solution.py:31
  113.0 30.5 %collective-permute-start.25 = (f16[144,768]{1,0:T(8,128)(2,1)S(1)}, f16[144,768]{1,0:T(8,128)(2,1)S(1)}, u32[]{:S(2)}, u32[]{:S(2)}) collective-permute-start(f16[144,768]{1,0:T(8,128)(2,1)S(1)} %fusion.7), channel_id=1, source_target_pairs={{0,32},{1,97},{2,34},{3,99},{4,36},{5,101},{6,38},{7,103},{8,72},{... | collective-permute-start | bytes 663560 | tf_op jit(solution)/shard_map/ppermute | solution.py:31
  116.8 26.7 %collective-permute-start.27 = (f16[144,768]{1,0:T(8,128)(2,1)S(1)}, f16[144,768]{1,0:T(8,128)(2,1)S(1)}, u32[]{:S(2)}, u32[]{:S(2)}) collective-permute-start(f16[144,768]{1,0:T(8,128)(2,1)S(1)} %fusion.8), channel_id=1, source_target_pairs={{0,64},{1,65},{2,66},{3,67},{4,68},{5,69},{6,70},{7,71},{8,104},{9... | collective-permute-start | bytes 663560 | tf_op jit(solution)/shard_map/ppermute | solution.py:31
  129.1 11.3 %collective-permute-start.3 = (f16[368,768]{1,0:T(8,128)(2,1)S(1)}, f16[368,768]{1,0:T(8,128)(2,1)S(1)}, u32[]{:S(2)}, u32[]{:S(2)}) collective-permute-start(f16[368,768]{1,0:T(8,128)(2,1)S(1)} %multiply_convert_fusion), channel_id=1, source_target_pairs={{0,32},{1,97},{2,34},{3,99},{4,36},{5,101},{6,38},{7,103},{8,40},{... | collective-permute-start | bytes 1695752 | tf_op jit(solution)/shard_map/ppermute | solution.py:31
  140.7 14.0 %collective-permute-start.4 = (f16[368,768]{1,0:T(8,128)(2,1)S(1)}, f16[368,768]{1,0:T(8,128)(2,1)S(1)}, u32[]{:S(2)}, u32[]{:S(2)}) collective-permute-start(f16[368,768]{1,0:T(8,128)(2,1)S(1)} %get-tuple-element.38), channel_id=1, source_target_pairs={{0,32},{1,33},{2,34},{3,35},{4,36},{5,37},{6,38},{7,39},{8,40},{9,... | collective-permute-start | bytes 1695752 | tf_op jit(solution)/shard_map/ppermute | solution.py:31
  140.8 13.9 %collective-permute-start.5 = (f16[368,768]{1,0:T(8,128)(2,1)S(1)}, f16[368,768]{1,0:T(8,128)(2,1)S(1)}, u32[]{:S(2)}, u32[]{:S(2)}) collective-permute-start(f16[368,768]{1,0:T(8,128)(2,1)S(1)} %get-tuple-element.39), channel_id=1, source_target_pairs={{0,96},{1,97},{2,98},{3,99},{4,100},{5,101},{6,102},{7,103},{8,104... | collective-permute-start | bytes 1695752 | tf_op jit(solution)/shard_map/ppermute | solution.py:31
  149.0 6.0 %copy-start.21 = (bf16[512,768]{1,0:T(8,128)(2,1)S(1)}, bf16[512,768]{1,0:T(8,128)(2,1)}, u32[]{:S(2)}) copy-start(bf16[512,768]{1,0:T(8,128)(2,1)} %amps_ref.1) | copy-start | bytes 2359300
  149.1 6.0 %copy-start.23 = (f32[768]{0:T(1024)S(1)}, f32[768]{0:T(1024)}, u32[]{:S(2)}) copy-start(f32[768]{0:T(1024)} %param.14) | copy-start | bytes 9220
  (22 other events, 68.9 us)
Sparse Core Ops, SparseCore 0:
  25.9 93.1 all-gather.1
